TPU v7x, 32 devices: a whole 2x2x4 slice. The times are simulated.
32 devices in a mesh: flow: 8 (over z, y), trans: 4 (over x, core).
Axes of the slice: x: 2, y: 2, z: 4, core: 2. Of those that a mesh axis runs over, the one named last changes fastest.
Arguments:
- concentration: float32 [4, 128, 64, 256], P(None, 'flow', 'trans'), may hold values from 0 to 2
- stratum: int32 [128, 64, 256], P('flow', 'trans'), may hold values from 0 to 15
- porosity: float32 [16], replicated, may hold values from 0.1 to 0.4
- dispersion_table: float32 [16, 2], replicated, may hold values from 512 to 15360
- transverse_table: float32 [16], replicated, may hold values from 0.2 to 2
- exchange_table: float32 [16], replicated, may hold values from 0.01 to 0.2
- decay_table: float32 [16], replicated, may hold values from 0.01 to 0.2
Outputs:
- new_concentration: float32 [4, 128, 64, 256], P(None, 'flow', 'trans')
All inputs are finite; a program needn't handle non-finite values.
Results may differ from a plain program's by a relative error of at most 0.001.
Values sent between devices are 32-bit elements; how exact they have to be, the bound alone decides.
No kernel may reach another device: no remote copies, remote signals or barrier semaphores. Data moves between devices by JAX's collectives and lax.ppermute only.
A program may use at most 128 MiB of HBM per device.

v0:
```python
import jax
import jax.numpy as jnp
from jax import lax
from jax.sharding import PartitionSpec as P


def with_halo(x, sides, width):
    for axis, dim in sides:
        peers, length = (lax.axis_size(axis), x.shape[dim])
        up = [(i, (i + 1) % peers) for i in range(peers - 1)]
        down = [(j, i) for i, j in up]
        last = lax.slice_in_dim(x, length - width, length, axis=dim)
        initial = lax.slice_in_dim(x, 0, width, axis=dim)
        before = lax.ppermute(last, axis, up)
        after = lax.ppermute(initial, axis, down)
        x = jnp.concatenate([before, x, after], axis=dim)
    return x


def harmonic(first, second):
    return 2.0 * first * second / (first + second)


def assemble(diagonal, exchange, decay):
    nothing = jnp.zeros_like(exchange)
    block_rows = [
        [diagonal[0] + exchange + decay, nothing, -exchange, nothing],
        [-decay, diagonal[1] + exchange, nothing, -exchange],
        [-exchange, nothing, diagonal[2] + exchange + decay, nothing],
        [nothing, -exchange, -decay, diagonal[3] + exchange],
    ]
    return jnp.stack([jnp.stack(entries) for entries in block_rows])


def invert(matrix):
    matrix_order = matrix.shape[0]
    work_rows = [
        [matrix[target, column] for column in range(matrix_order)] for target in range(matrix_order)
    ]
    unit_rows = [
        [
            jnp.ones_like(matrix[0, 0]) if target == column else jnp.zeros_like(matrix[0, 0])
            for column in range(matrix_order)
        ]
        for target in range(matrix_order)
    ]
    for column in range(matrix_order):
        pivot_scale = 1.0 / work_rows[column][column]
        work_rows[column] = [element * pivot_scale for element in work_rows[column]]
        unit_rows[column] = [element * pivot_scale for element in unit_rows[column]]
        for target in range(matrix_order):
            if target != column:
                multiplier = work_rows[target][column]
                work_rows[target] = [
                    element - multiplier * partner
                    for element, partner in zip(work_rows[target], work_rows[column])
                ]
                unit_rows[target] = [
                    element - multiplier * partner
                    for element, partner in zip(unit_rows[target], unit_rows[column])
                ]
    return jnp.stack([jnp.stack(entries) for entries in unit_rows])


def matmul(first, second):
    return jnp.sum(first[:, :, None, :] * second[None, :, :, :], axis=1)


def matvec(matrix, vector):
    return jnp.sum(matrix * vector[None, :, :], axis=1)


def merge_parts(left_group, right_group):
    top_free_l, bot_free_l, top_right_l, bot_right_l, top_left_l, bot_left_l = left_group
    top_free_r, bot_free_r, top_right_r, bot_right_r, top_left_r, bot_left_r = right_group
    unit_block = jnp.broadcast_to(
        jnp.eye(top_right_l.shape[0], dtype=jnp.float32)[:, :, None], top_right_l.shape
    )
    coupling = invert(unit_block - matmul(bot_right_l, top_left_r))
    inner_free = matvec(coupling, bot_free_l - matvec(bot_right_l, top_free_r))
    inner_right = -matmul(coupling, matmul(bot_right_l, top_right_r))
    inner_left = matmul(coupling, bot_left_l)
    outer_free = top_free_r - matvec(top_left_r, inner_free)
    outer_right = top_right_r - matmul(top_left_r, inner_right)
    outer_left = -matmul(top_left_r, inner_left)
    merged = (
        top_free_l - matvec(top_right_l, outer_free),
        bot_free_r - matvec(bot_left_r, inner_free),
        -matmul(top_right_l, outer_right),
        bot_right_r - matmul(bot_left_r, inner_right),
        top_left_l - matmul(top_right_l, outer_left),
        -matmul(bot_left_r, inner_left),
    )
    return (merged, inner_free, inner_right)


def cell_major(field):
    return jnp.transpose(field, (1, 0, 2, 3)).reshape(
        field.shape[1], field.shape[0], field.shape[2] * field.shape[3]
    )


def factor_scan(diagonal, exchange, decay, left_mobile, right_mobile):
    line_count = diagonal.shape[2]
    zero_pair = jnp.zeros((2, 2, line_count), jnp.float32)
    unit_pair = jnp.broadcast_to(jnp.eye(2, dtype=jnp.float32)[:, :, None], (2, 2, line_count))

    def factor_step(carry_pair, inputs_cell):
        upper_mobile, west_mobile = carry_pair
        diagonal_cell, exchange_cell, decay_cell, left_num, right_num = inputs_cell
        cell_block = assemble(diagonal_cell, exchange_cell, decay_cell)
        correction = left_num[:, None, :] * upper_mobile
        pivot_block = cell_block + jnp.pad(correction, ((0, 2), (0, 2), (0, 0)))
        inverse = invert(pivot_block)
        mobile_columns = inverse[:, :2]
        upper_part = -mobile_columns * right_num[None, :, :]
        west_part = matmul(mobile_columns, left_num[:, None, :] * west_mobile)
        return ((upper_part[:2], west_part[:2]), (inverse, upper_part, west_part))

    ignored_pair, stored = lax.scan(
        factor_step,
        (zero_pair, -unit_pair),
        (diagonal, exchange, decay, left_mobile, right_mobile),
        unroll=min(8, diagonal.shape[0]),
    )
    return stored


def source_scan(inverses, left_mobile, source):
    line_count = source.shape[2]

    def source_step(vector_mobile, inputs_cell):
        inverse, left_num, forcing = inputs_cell
        lifted = forcing + jnp.pad(left_num * vector_mobile, ((0, 2), (0, 0)))
        vector_part = matvec(inverse, lifted)
        return (vector_part[:2], vector_part)

    ignored_vector, vectors = lax.scan(
        source_step,
        jnp.zeros((2, line_count), jnp.float32),
        (inverses, left_mobile, source),
        unroll=min(8, source.shape[0]),
    )
    return vectors


def segment_solve(diagonal, exchange, decay, left_mobile, right_mobile, source):
    line_count = diagonal.shape[2]
    unroll_depth = min(8, diagonal.shape[0])
    zero_vector = jnp.zeros((2, line_count), jnp.float32)
    zero_pair = jnp.zeros((2, 2, line_count), jnp.float32)
    unit_pair = jnp.broadcast_to(jnp.eye(2, dtype=jnp.float32)[:, :, None], (2, 2, line_count))
    inverses, uppers, wests = factor_scan(diagonal, exchange, decay, left_mobile, right_mobile)
    vectors = source_scan(inverses, left_mobile, source)

    def tip_step(state_triple, inputs_cell):
        free_after, west_after, east_after = state_triple
        upper_part, vector_part, west_part = inputs_cell
        upper_mobile = upper_part[:2]
        return (
            (
                vector_part[:2] - matvec(upper_mobile, free_after),
                west_part[:2] - matmul(upper_mobile, west_after),
                -matmul(upper_mobile, east_after),
            ),
            None,
        )

    (top_free, top_left, top_right), ignored_out = lax.scan(
        tip_step,
        (zero_vector, zero_pair, -unit_pair),
        (uppers, vectors, wests),
        reverse=True,
        unroll=unroll_depth,
    )
    bottom_free = vectors[-1][:2]
    bottom_right = uppers[-1][:2]
    bottom_left = wests[-1][:2]
    own_group = (top_free, bottom_free, top_right, bottom_right, top_left, bottom_left)
    identity = (zero_vector, zero_vector, -unit_pair, zero_pair, zero_pair, -unit_pair)
    collected = (
        lax.all_gather(top_free[None], "flow", axis=0, tiled=True),
        lax.all_gather(bottom_free[None], "flow", axis=0, tiled=True),
        lax.all_gather(top_right[None], "flow", axis=0, tiled=True),
        lax.all_gather(bottom_right[None], "flow", axis=0, tiled=True),
        lax.all_gather(top_left[None], "flow", axis=0, tiled=True),
        lax.all_gather(bottom_left[None], "flow", axis=0, tiled=True),
    )
    group_count = lax.axis_size("flow")
    position = lax.axis_index("flow")
    indices = jnp.arange(group_count, dtype=jnp.int32)

    def pick_group(which):
        return tuple(
            (lax.dynamic_index_in_dim(member, which, 0, keepdims=False) for member in collected)
        )

    def lower_step(accumulated, which):
        candidate = merge_parts(accumulated, pick_group(which))[0]
        keeping = which < position
        return (
            tuple(
                (jnp.where(keeping, fresh, stale) for fresh, stale in zip(candidate, accumulated))
            ),
            None,
        )

    def upper_step(accumulated, which):
        candidate = merge_parts(pick_group(which), accumulated)[0]
        keeping = which > position
        return (
            tuple(
                (jnp.where(keeping, fresh, stale) for fresh, stale in zip(candidate, accumulated))
            ),
            None,
        )

    prefix, ignored_low = lax.scan(lower_step, identity, indices, unroll=4)
    suffix, ignored_high = lax.scan(upper_step, identity, group_count - 1 - indices, unroll=4)
    joined, inner_free, inner_right = merge_parts(prefix, own_group)
    bottom_value = matvec(
        invert(unit_pair - matmul(joined[3], suffix[4])), joined[1] - matvec(joined[3], suffix[0])
    )
    after_value = suffix[0] - matvec(suffix[4], bottom_value)
    before_value = inner_free - matvec(inner_right, after_value)

    def final_step(after_mobile, inputs_cell):
        upper_part, vector_part, west_part = inputs_cell
        current = vector_part - matvec(west_part, before_value) - matvec(upper_part, after_mobile)
        return (current[:2], current)

    ignored_final, solved = lax.scan(
        final_step, after_value, (uppers, vectors, wests), reverse=True, unroll=unroll_depth
    )
    return solved


def per_device(
    concentration,
    stratum,
    porosity,
    dispersion_table,
    transverse_table,
    exchange_table,
    decay_table,
):
    cell_count = concentration.shape[1]
    planes_y = concentration.shape[2]
    planes_z = concentration.shape[3]
    line_count = planes_y * planes_z
    porosity_cell = jnp.zeros(stratum.shape, jnp.float32)
    transverse = jnp.zeros(stratum.shape, jnp.float32)
    exchange = jnp.zeros(stratum.shape, jnp.float32)
    decay = jnp.zeros(stratum.shape, jnp.float32)
    dispersion = jnp.zeros((2,) + stratum.shape, jnp.float32)
    for stratum_id in range(porosity.shape[0]):
        chosen = stratum == stratum_id
        porosity_cell = jnp.where(chosen, porosity[stratum_id], porosity_cell)
        transverse = jnp.where(chosen, transverse_table[stratum_id], transverse)
        exchange = jnp.where(chosen, exchange_table[stratum_id], exchange)
        decay = jnp.where(chosen, decay_table[stratum_id], decay)
        dispersion = jnp.where(
            chosen[None], dispersion_table[stratum_id][:, None, None, None], dispersion
        )
    capacity = jnp.stack([porosity_cell, porosity_cell, 1.0 - porosity_cell, 1.0 - porosity_cell])
    stacked = jnp.concatenate([concentration[:2], transverse[None]], axis=0)
    widened = with_halo(stacked, (("trans", 2),), 1)
    widened = jnp.pad(widened, ((0, 0), (0, 0), (0, 0), (1, 1)))
    mobile = concentration[:2]
    flux = jnp.zeros_like(mobile)
    for offset_y, offset_z in ((2, 1), (0, 1), (1, 2), (1, 0)):
        neighbour_num = widened[
            2, :, offset_y : offset_y + planes_y, offset_z : offset_z + planes_z
        ]
        neighbour_conc = widened[
            :2, :, offset_y : offset_y + planes_y, offset_z : offset_z + planes_z
        ]
        flux = flux + harmonic(transverse, neighbour_num) * (neighbour_conc - mobile)
    source = capacity * concentration + jnp.concatenate([flux, jnp.zeros_like(flux)])
    padded_flow = with_halo(dispersion, (("flow", 1),), 1)
    right_mobile = harmonic(dispersion, padded_flow[:, 2:])
    left_mobile = harmonic(dispersion, padded_flow[:, :-2])
    diagonal = capacity + jnp.concatenate([left_mobile + right_mobile, jnp.zeros_like(left_mobile)])
    solved_cells = segment_solve(
        cell_major(diagonal),
        exchange.reshape(cell_count, line_count),
        decay.reshape(cell_count, line_count),
        cell_major(left_mobile),
        cell_major(right_mobile),
        cell_major(source),
    )
    solved = solved_cells.reshape(cell_count, 4, planes_y, planes_z)
    return jnp.transpose(solved, (1, 0, 2, 3))


def solution(mesh):
    in_specs = (P(None, "flow", "trans", None), P("flow", "trans", None), P(), P(), P(), P(), P())
    out_specs = P(None, "flow", "trans", None)
    return jax.shard_map(
        per_device, mesh=mesh, in_specs=in_specs, out_specs=out_specs, check_vma=False
    )
```

profile of v0, /device:TPU:0, one launch (start us, length us, event | category | flops | bytes accessed | tf_op | source)
XLA Modules:
  0.0 610.3 jit_solution(12641816417576401793)
XLA Ops:
  0.0 2.0 fusion.691
  2.0 1.7 slice_reduce_fusion.15
  3.7 11.7 %select_select_fusion.1 = (f32[16,16,256]{2,1,0:T(8,128)S(1)}, pred[16,16,256]{2,1,0:T(8,128)(4,1)S(1)}, pred[16,16,256]{2,1,0:T(8,128)(4,1)S(1)}, pred[16,16,25...) fusion(f32[]{:T(128)} %bitcast.433, ...), kind=kLoop, calls=%fused_computation.1522 | loop fusion | flops 2097152 | bytes 1572928 | tf_op jit(solution)/shard_map/jit(_where)/select_n | solution.py:259
  16.7 4.9 collective-permute-start
  24.3 3.0 collective-permute-start.3
  30.1 10.9 %select_select_fusion.2 = f32[16,16,256]{2,1,0:T(8,128)} fusion(pred[16,16,256]{2,1,0:T(8,128)(4,1)S(1)} %get-tuple-element.1279, pred[16,16,256]{2,1,0:T(8,128)(4,1)S(1)} %get-tuple-element.1280, pred[16,16,256]{2,1,0:T(8,128)(4,1)S(1)} %get-tuple-element.1281, pred[16,16,256]{2,1,0:T(8,128)(4,1)S(1)} %get-tuple-element.1282, ...), kind=kLoop, calls=%fused_computation.1523 | loop fusion | flops 1048576 | bytes 1310784 | tf_op jit(solution)/shard_map/jit(_where)/select_n | solution.py:261
  41.0 11.1 %select_select_fusion.3 = f32[16,16,256]{2,1,0:T(8,128)} fusion(pred[16,16,256]{2,1,0:T(8,128)(4,1)S(1)} %get-tuple-element.1279, pred[16,16,256]{2,1,0:T(8,128)(4,1)S(1)} %get-tuple-element.1280, pred[16,16,256]{2,1,0:T(8,128)(4,1)S(1)} %get-tuple-element.1281, pred[16,16,256]{2,1,0:T(8,128)(4,1)S(1)} %get-tuple-element.1282, ...), kind=kLoop, calls=%fused_computation.1524 | loop fusion | flops 1048576 | bytes 1310784 | tf_op jit(solution)/shard_map/jit(_where)/select_n | solution.py:260
  52.1 11.2 %subtract_bitcast_fusion = (f32[1,16,16,256]{3,2,1,0:T(8,128)}, f32[16,16,256]{2,1,0:T(8,128)}) fusion(pred[16,16,256]{2,1,0:T(8,128)(4,1)S(1)} %get-tuple-element.1279, pred[16,16,256]{2,1,0:T(8,128)(4,1)S(1)} %get-tuple-element.1280, pred[16,16,256]{2,1,0:T(8,128)(4,1)S(1)} %get-tuple-element.1281, pred[16,16,256]{2,1,0:T(8,128)(4,1)S(1)} %get-tuple-element.1282, ...), kind=kLoop, calls=%fused_computation.1525 | loop fusion | flops 1114112 | bytes 1572928 | tf_op jit(solution)/shard_map/stack | solution.py:265
  63.3 1.7 reshape_reshape.24
  65.0 1.7 reshape_reshape.23
  68.3 1.9 reshape.27958
  71.7 2.0 reshape.27959
  73.7 1.9 select_maximum_fusion
  78.6 1.6 add_bitcast_fusion
  80.2 2.4 reshape.27957
  82.7 80.0 %while.95 = (s32[]{:T(128)}, f32[2,2,4096]{2,0,1:T(2,128)S(1)}, f32[2,2,4096]{2,0,1:T(2,128)S(1)}, f32[2,8,4,4,4096]{4,3,2,1,0:T(4,128)}, f32[2,8,4,2,4096]{4,3,...) while((s32[]{:T(128)}, f32[2,2,4096]{2,0,1:T(2,128)S(1)}, ...), condition=%wide.region_9.10_spmd, body=%wide.region_0.9_spmd.sunk | while | flops 13926409 | bytes 116277768 | solution.py:120
  99.7 4.5 fusion.790
  122.7 1.8 copy_dynamic-update-slice_fusion.42
  127.4 1.5 copy_dynamic-update-slice_fusion.41
  128.9 1.9 copy-done.7
  130.9 4.6 fusion.790
  154.1 1.8 copy_dynamic-update-slice_fusion.42
  158.8 1.5 copy_dynamic-update-slice_fusion.41
  160.3 1.9 copy-done.7
  162.7 3.3 reshape.27960
  166.9 41.2 %while.96 = (s32[]{:T(128)}, f32[2,4096]{1,0:T(2,128)}, f32[2,8,4,4096]{3,2,1,0:T(4,128)S(1)}, f32[2,8,4,4,4096]{4,3,2,1,0:T(4,128)}, f32[2,8,4,4096]{3,1,0,2:T(...) while((s32[]{:T(128)}, f32[2,4096]{1,0:T(2,128)}, ...), condition=%wide.region_19.20_spmd, body=%wide.region_10.19_spmd.sunk | while | flops 1114121 | bytes 8454525 | solution.py:138
  166.9 3.9 constant_dynamic-slice_fusion.71
  187.7 3.5 constant_dynamic-slice_fusion.71
  209.0 45.1 %while.98 = (s32[]{:T(128)}, f32[2,4096]{1,0:T(2,128)S(1)}, f32[2,2,4096]{2,1,0:T(2,128)S(1)}, f32[2,2,4096]{2,1,0:T(2,128)S(1)}, f32[2,8,4,4096]{3,2,1,0:T(4,12...) while((s32[]{:T(128)}, f32[2,4096]{1,0:T(2,128)S(1)}, ...), condition=%wide.region_45.46_spmd.clone, body=%wide.region_20.45_spmd.clone.sunk | while | flops 1335307 | bytes 7799216 | solution.py:169
  254.2 35.9 %all-gather.1 = f32[16,2,4096]{2,1,0:T(2,128)} all-gather(f32[2,2,4096]{2,1,0:T(2,128)S(1)} %get-tuple-element.626), channel_id=3, replica_groups=mesh['flow'=8,'trans'=4] {'flow'}, dimensions={0}, use_global_device_ids=true | all-gather | bytes 589824 | tf_op jit(solution)/shard_map/all_gather | solution.py:184
  290.1 33.5 %all-gather.2 = f32[16,2,4096]{2,1,0:T(2,128)} all-gather(f32[2,2,4096]{2,1,0:T(2,128)S(1)} %get-tuple-element.627), channel_id=4, replica_groups=mesh['flow'=8,'trans'=4] {'flow'}, dimensions={0}, use_global_device_ids=true | all-gather | bytes 589824 | tf_op jit(solution)/shard_map/all_gather | solution.py:186
  323.5 33.0 %all-gather.3 = f32[8,2,4096]{2,1,0:T(2,128)} all-gather(f32[1,2,4096]{2,1,0:T(2,128)S(1)} %bitcast.3380), channel_id=2, replica_groups=mesh['flow'=8,'trans'=4] {'flow'}, dimensions={0}, use_global_device_ids=true | all-gather | bytes 294912 | tf_op jit(solution)/shard_map/all_gather | solution.py:182
  357.4 32.9 %all_gather.21 = f32[8,2,4096]{2,1,0:T(2,128)} all-gather(f32[1,2,4096]{2,1,0:T(2,128)S(1)} %slice.3182), channel_id=1, replica_groups=mesh['flow'=8,'trans'=4] {'flow'}, dimensions={0}, use_global_device_ids=true | all-gather | bytes 294912 | tf_op jit(solution)/shard_map/all_gather | solution.py:183
  390.3 1.5 slice_bitcast_fusion.152
  391.7 31.4 %all_gather.23 = f32[8,2,2,4096]{3,2,1,0:T(2,128)S(1)} all-gather(f32[1,2,2,4096]{3,2,1,0:T(2,128)S(1)} %get-tuple-element.1621), channel_id=1, replica_groups=mesh['flow'=8,'trans'=4] {'flow'}, dimensions={0}, use_global_device_ids=true | all-gather | bytes 589824 | tf_op jit(solution)/shard_map/all_gather | solution.py:187
  423.2 31.2 %all_gather.20 = f32[8,2,2,4096]{3,2,1,0:T(2,128)S(1)} all-gather(f32[1,2,2,4096]{3,2,1,0:T(2,128)S(1)} %slice.3181), channel_id=1, replica_groups=mesh['flow'=8,'trans'=4] {'flow'}, dimensions={0}, use_global_device_ids=true | all-gather | bytes 589824 | tf_op jit(solution)/shard_map/all_gather | solution.py:185
  454.4 62.8 %while.100 = (s32[]{:T(128)}, f32[2,4096]{1,0:T(2,128)S(1)}, f32[2,2,4096]{2,1,0:T(2,128)}, s32[2,4]{1,0:T(2,128)S(1)}, s32[]{:T(128)}, /*index=5*/f32[8,2,4096]...) while((s32[]{:T(128)}, f32[2,4096]{1,0:T(2,128)S(1)}, ...), condition=%wide.region_109.110_spmd.clone, body=%wide.region_80.109_spmd.clone.sunk | while | flops 1884187 | bytes 10519081 | solution.py:218
  462.7 1.5 dynamic-slice_bitcast_fusion.128
  464.3 1.8 dynamic-slice_bitcast_fusion.129
  496.0 1.8 dynamic-slice_bitcast_fusion.129
  519.9 1.5 multiply_reduce_fusion.100
  522.2 67.0 %while.99 = (s32[]{:T(128)}, f32[2,4096]{1,0:T(2,128)S(1)}, f32[2,2,4096]{2,1,0:T(2,128)S(1)}, s32[2,4]{1,0:T(2,128)S(1)}, s32[]{:T(128)}, /*index=5*/f32[8,2,40...) while((s32[]{:T(128)}, f32[2,4096]{1,0:T(2,128)S(1)}, ...), condition=%wide.region_79.80_spmd.clone, body=%wide.region_46.79_spmd.clone.sunk | while | flops 2056219 | bytes 11862616 | solution.py:219
  532.4 1.6 dynamic-slice_bitcast_fusion.127
  565.8 1.6 dynamic-slice_bitcast_fusion.127
  594.7 12.3 %while.97 = (s32[]{:T(128)}, f32[2,4096]{1,0:T(2,128)S(1)}, f32[2,8,4,4096]{3,2,1,0:T(4,128)}, f32[2,8,4,4096]{3,2,1,0:T(4,128)S(1)}, f32[2,8,4,2,4096]{4,3,2,1,...) while((s32[]{:T(128)}, f32[2,4096]{1,0:T(2,128)S(1)}, ...), condition=%wide.region_139.140_spmd, body=%wide.region_122.139_spmd.sunk | while | flops 1179657 | bytes 17072608 | solution.py:232
  594.7 3.0 fusion.836
  600.9 3.0 fusion.836
  607.0 1.9 reshape.27961
  (989 shorter events, 230.5 us)
Async XLA Ops:
  0.0 22.9 %copy-start.20 = (f32[4,16,16,256]{3,2,1,0:T(8,128)S(1)}, f32[4,16,16,256]{3,2,1,0:T(8,128)}, u32[]{:S(2)}) copy-start(f32[4,16,16,256]{3,2,1,0:T(8,128)} %param.19) | copy-start | bytes 3145732
  15.4 25.6 %copy-start.11 = (f32[16,16,256]{2,1,0:T(8,128)}, f32[16,16,256]{2,1,0:T(8,128)S(1)}, u32[]{:S(2)}) copy-start(f32[16,16,256]{2,1,0:T(8,128)S(1)} %get-tuple-element.1278) | copy-start | bytes 786436
  15.4 12.5 %copy-start.29 = (f32[16]{0:T(128)S(1)}, f32[16]{0:T(128)}, u32[]{:S(2)}) copy-start(f32[16]{0:T(128)} %param.25) | copy-start | bytes 196
  15.4 13.3 %copy-start.30 = (f32[16]{0:T(128)S(1)}, f32[16]{0:T(128)}, u32[]{:S(2)}) copy-start(f32[16]{0:T(128)} %param.24) | copy-start | bytes 196
  15.4 14.0 %copy-start.31 = (f32[16]{0:T(128)S(1)}, f32[16]{0:T(128)}, u32[]{:S(2)}) copy-start(f32[16]{0:T(128)} %param.21) | copy-start | bytes 196
  16.7 50.1 %collective-permute-start = (f32[2,1,16,256]{3,2,1,0:T(8,128)}, f32[2,1,16,256]{3,2,1,0:T(8,128)S(1)}, u32[]{:S(2)}, u32[]{:S(2)}) collective-permute-start(f32[2,1,16,256]{3,2,1,0:T(8,128)} %get-tuple-element.1634), channel_id=1, source_target_pairs={{0,4},{4,8},{8,12},{12,16},{16,20},{20,24},{24,28},{1,5},{5,9},{9,... | collective-permute-start | bytes 98312 | tf_op jit(solution)/shard_map/ppermute | solution.py:14
  21.6 45.2 %collective-permute-start.1 = (f32[2,1,16,256]{3,2,1,0:T(8,128)}, f32[2,1,16,256]{3,2,1,0:T(8,128)S(1)}, u32[]{:S(2)}, u32[]{:S(2)}) collective-permute-start(f32[2,1,16,256]{3,2,1,0:T(8,128)} %get-tuple-element.1633), channel_id=1, source_target_pairs={{4,0},{8,4},{12,8},{16,12},{20,16},{24,20},{28,24},{5,1},{9,5},{13... | collective-permute-start | bytes 98312 | tf_op jit(solution)/shard_map/ppermute | solution.py:15
  23.0 50.6 %collective-permute-start.2 = (f32[3,16,1,256]{3,2,1,0:T(1,128)S(1)}, f32[3,16,1,256]{3,2,1,0:T(1,128)S(1)}, u32[]{:S(2)}, u32[]{:S(2)}) collective-permute-start(f32[3,16,1,256]{3,2,1,0:T(1,128)S(1)} %get-tuple-element.1627), channel_id=1, source_target_pairs={{1,0},{2,1},{3,2},{5,4},{6,5},{7,6},{9,8},{10,9},{11,10},{13,12},{... | collective-permute-start | bytes 147464 | tf_op jit(solution)/shard_map/ppermute | solution.py:15
  24.3 49.3 %collective-permute-start.3 = (f32[3,16,1,256]{3,2,1,0:T(1,128)S(1)}, f32[3,16,1,256]{3,2,1,0:T(1,128)S(1)}, u32[]{:S(2)}, u32[]{:S(2)}) collective-permute-start(f32[3,16,1,256]{3,2,1,0:T(1,128)S(1)} %get-tuple-element.1626), channel_id=1, source_target_pairs={{0,1},{1,2},{2,3},{4,5},{5,6},{6,7},{8,9},{9,10},{10,11},{12,13},{... | collective-permute-start | bytes 147464 | tf_op jit(solution)/shard_map/ppermute | solution.py:14
  73.6 3.5 copy-start.12
  77.0 1.2 copy-start.21
  77.1 1.3 copy-start.22
  77.1 1.4 copy-start.25
  77.1 1.5 copy-start.26
  104.4 1.6 copy-start.14
  121.0 1.7 copy-start.4
  124.5 1.7 copy-start.5
  124.5 2.9 copy-start.6
  128.9 1.9 copy-start.7
  135.8 1.6 copy-start.14
  152.4 1.7 copy-start.4
  155.9 1.7 copy-start.5
  155.9 2.9 copy-start.6
  160.3 1.9 copy-start.7
  162.7 3.3 copy-start.8
  162.7 4.1 copy-start.2
  166.8 42.2 %copy-start.18 = (f32[2,2,4096]{2,1,0:T(2,128)S(1)}, f32[2,2,4096]{2,1,0:T(2,128)}, u32[]{:S(2)}) copy-start(f32[2,2,4096]{2,1,0:T(2,128)} %custom-call.1) | copy-start | bytes 196612
  166.8 42.2 %copy-start.23 = (f32[2,4096]{1,0:T(2,128)S(1)}, f32[2,4096]{1,0:T(2,128)}, u32[]{:S(2)}) copy-start(f32[2,4096]{1,0:T(2,128)} %custom-call) | copy-start | bytes 98308
  208.0 1.0 copy-start
  254.1 200.2 %copy-start.15 = (f32[2,2,4096]{2,1,0:T(2,128)}, f32[2,2,4096]{2,1,0:T(2,128)S(1)}, u32[]{:S(2)}) copy-start(f32[2,2,4096]{2,1,0:T(2,128)S(1)} %get-tuple-element.626) | copy-start | bytes 196612
  254.2 200.2 %copy-start.19 = (f32[2,2,4096]{2,1,0:T(2,128)}, f32[2,2,4096]{2,1,0:T(2,128)S(1)}, u32[]{:S(2)}) copy-start(f32[2,2,4096]{2,1,0:T(2,128)S(1)} %get-tuple-element.627) | copy-start | bytes 196612
  254.2 200.2 %copy-start.24 = (f32[2,4096]{1,0:T(2,128)}, f32[2,4096]{1,0:T(2,128)S(1)}, u32[]{:S(2)}) copy-start(f32[2,4096]{1,0:T(2,128)S(1)} %get-tuple-element.625) | copy-start | bytes 98308
  254.2 169.0 %copy-start.3 = (f32[2,8,4,2,4096]{4,3,2,1,0:T(2,128)S(1)}, f32[2,8,4,2,4096]{4,3,2,1,0:T(2,128)}, u32[]{:S(2)}) copy-start(f32[2,8,4,2,4096]{4,3,2,1,0:T(2,128)} %get-tuple-element.3596) | copy-start | bytes 6291460
  254.2 200.2 %copy-start.32 = (s32[2,4]{1,0:T(2,128)S(1)}, s32[2,4]{1,0:T(2,128)}, u32[]{:S(2)}) copy-start(s32[2,4]{1,0:T(2,128)} %multiply_add_fusion) | copy-start | bytes 100
  517.2 5.1 copy-start.9
  517.2 5.1 copy-start.10
  519.9 1.6 copy-start.28
  521.6 0.7 copy-start.27
  522.2 68.4 %copy-start.1 = (f32[2,8,4,4096]{3,2,1,0:T(4,128)S(1)}, f32[2,8,4,4096]{3,2,1,0:T(4,128)}, u32[]{:S(2)}) copy-start(f32[2,8,4,4096]{3,2,1,0:T(4,128)} %get-tuple-element.3595) | copy-start | bytes 3145732
  536.9 9.9 %copy-start.13 = (f32[2,2,4096]{2,1,0:T(2,128)S(1)}, f32[2,2,4096]{2,1,0:T(2,128)}, u32[]{:S(2)}) copy-start(f32[2,2,4096]{2,1,0:T(2,128)} %get-tuple-element.3201) | copy-start | bytes 196612 | tf_op jit(solution)/shard_map/while
  570.3 9.9 %copy-start.13 = (f32[2,2,4096]{2,1,0:T(2,128)S(1)}, f32[2,2,4096]{2,1,0:T(2,128)}, u32[]{:S(2)}) copy-start(f32[2,2,4096]{2,1,0:T(2,128)} %get-tuple-element.3201) | copy-start | bytes 196612 | tf_op jit(solution)/shard_map/while
  598.1 1.7 copy-start.16
  599.9 1.0 copy-start.17
  604.2 1.7 copy-start.16
  606.0 1.0 copy-start.17
where the time goes:
time: 617 us; the launch traced here: 610 us
  other arithmetic  265 us (43%)
  blocking collectives  198 us (32%)
  local copies, waits for them, and re-layouts  74.3 us (12%)
  loops' own time  61.9 us (10%)
  starting transfers between devices  10.5 us (2%)
    reduce_sum x101, other arithmetic, matvec(): return jnp.sum(matrix * vector[None, :, :], axis=1)  75.4 us
    all_gather x1, blocking collectives, segment_solve(): lax.all_gather(top_right[None], 'flow', axis=0, tiled=True)  35.9 us
    all_gather x1, blocking collectives, segment_solve(): lax.all_gather(top_left[None], 'flow', axis=0, tiled=True)  33.5 us
    all_gather x1, blocking collectives, segment_solve(): lax.all_gather(top_free[None], 'flow', axis=0, tiled=True)  33 us
    all_gather x1, blocking collectives, segment_solve(): lax.all_gather(bottom_free[None], 'flow', axis=0, tiled=True)  32.9 us
    all_gather x1, blocking collectives, segment_solve(): lax.all_gather(bottom_left[None], 'flow', axis=0, tiled=True)  31.4 us
    all_gather x1, blocking collectives, segment_solve(): lax.all_gather(bottom_right[None], 'flow', axis=0, tiled=True)  31.2 us
    another operation x1, loops' own time, segment_solve(): prefix, ignored_low = lax.scan(lower_step, identity, indices, unroll=4)  20.7 us
  transfers between devices with their start and end apart: 4, of which 0 were waited for; matrix products, arithmetic and copies ran while one was open for 8% of the time, Pallas kernels for 0%

commit v1 on v0

v1 whole, which is shorter than its diff:
```python
import functools

import jax
import jax.numpy as jnp
from jax import lax
from jax.experimental import pallas as pl
from jax.experimental.pallas import tpu as pltpu
from jax.sharding import PartitionSpec as P

SUB, LANE = 8, 128
POR, DISP_A, DISP_B, TRANS, EXCH, DECAY = range(6)
ZA_LL, ZA_LR, ZA_RR, ZB_LL, ZB_LR, ZB_RR, C_LL, C_LR, C_RL, C_RR, FA_L, FA_R, FB_L, FB_R = range(14)
QUANTITIES = 14
CURRENTS = 4
VMEM_LIMIT = 40 * 1024 * 1024


def recip(x):
    return 1.0 / x


def lookup(row, index):
    tiles = []
    for y in range(0, index.shape[0], SUB):
        across = [
            jnp.take_along_axis(
                row, index[y : y + SUB, z : z + LANE], axis=1, mode="promise_in_bounds"
            )
            for z in range(0, index.shape[1], LANE)
        ]
        tiles.append(jnp.concatenate(across, axis=1))
    return jnp.concatenate(tiles, axis=0)


def derived(tab_ref):
    por, disp_a, disp_b, trans, exch, decay = [
        jnp.broadcast_to(tab_ref[k : k + 1, :], (SUB, LANE)) for k in range(6)
    ]
    immobile = 1.0 - por
    over_a = 1.0 / (immobile + exch + decay)
    over_b = 1.0 / (immobile + exch)
    beta = immobile * over_a
    gamma = exch * over_a
    share_b = exch * over_b
    return dict(
        por=por,
        shunt_a=por + decay + exch * (immobile + decay) * over_a,
        shunt_b=por + exch * immobile * over_b,
        half_a=0.5 / disp_a,
        half_b=0.5 / disp_b,
        half_t=0.5 / trans,
        beta=beta,
        gamma=gamma,
        alpha_a=exch * beta,
        alpha_b=share_b * immobile,
        kappa=decay + share_b * decay * gamma,
        delta=share_b * decay * beta,
        free_b=immobile * over_b,
        share_b=share_b,
        decay_b=decay * over_b,
    )


def chunk_of(peers, planes_y, planes_z):
    if peers <= planes_y:
        return planes_y // peers, planes_z
    return 1, planes_y * planes_z // peers


def chunk_place(which, block, planes_z):
    rows, width = block
    across = planes_z // width
    return (which // across) * rows, (which % across) * width


def shifted_difference(value, axis):
    return pltpu.roll(value, value.shape[axis] - 1, axis) - value


def local_kernel(
    block,
    tab_ref,
    stratum_ref,
    conc_ref,
    pay_ref,
    edge_ref,
    pass_a_ref,
    drop_a_ref,
    pass_b_ref,
    drop_b_ref,
    over_ref,
    source_a_ref,
    source_b_ref,
    head_a,
    head_b,
    kappa_ref,
    left_a,
    right_a,
    left_b,
    right_b,
    adj_l,
    adj_r,
):
    n, planes_y, planes_z = stratum_ref.shape
    numbers = derived(tab_ref)

    cond_a = cond_b = half_a = half_b = through_a = through_b = None
    for i in range(n):
        index = stratum_ref[i]
        shunt_a, shunt_b = lookup(numbers["shunt_a"], index), lookup(numbers["shunt_b"], index)
        new_a, new_b = lookup(numbers["half_a"], index), lookup(numbers["half_b"], index)
        kappa_ref[i] = lookup(numbers["kappa"], index)
        if i == 0:
            first_half_a, first_half_b = new_a, new_b
            cond_a, cond_b = shunt_a, shunt_b
            through_a = through_b = jnp.ones_like(shunt_a)
        else:
            face_a, face_b = half_a + new_a, half_b + new_b
            pass_a, pass_b = recip(1.0 + face_a * cond_a), recip(1.0 + face_b * cond_b)
            cond_a, cond_b = shunt_a + cond_a * pass_a, shunt_b + cond_b * pass_b
            pass_a_ref[i], pass_b_ref[i] = pass_a, pass_b
            drop_a_ref[i], drop_b_ref[i] = face_a * pass_a, face_b * pass_b
            through_a, through_b = through_a * pass_a, through_b * pass_b
        head_a[i], head_b[i] = through_a, through_b
        half_a, half_b = new_a, new_b
    over_a, over_b = recip(cond_a), recip(cond_b)
    over_ref[0], over_ref[1] = over_a, over_b

    r_a, r_b = over_a, over_b
    l_a, l_b = through_a * over_a, through_b * over_b
    couple = [None] * 4
    for i in reversed(range(n)):
        if i < n - 1:
            pass_a, pass_b = pass_a_ref[i + 1], pass_b_ref[i + 1]
            l_a = pass_a * l_a + drop_a_ref[i + 1] * head_a[i]
            l_b = pass_b * l_b + drop_b_ref[i + 1] * head_b[i]
            r_a, r_b = pass_a * r_a, pass_b * r_b
        left_a[i], right_a[i], left_b[i], right_b[i] = l_a, r_a, l_b, r_b
        kappa = kappa_ref[i]
        k_l, k_r = kappa * l_a, kappa * r_a
        terms = [l_b * k_l, l_b * k_r, r_b * k_l, r_b * k_r]
        couple = [t if c is None else c + t for c, t in zip(couple, terms)]

    g_l = g_r = None
    for i in range(n):
        kappa = kappa_ref[i]
        s_l, s_r = kappa * left_b[i], kappa * right_b[i]
        if i > 0:
            pass_a = pass_a_ref[i]
            s_l, s_r = s_l + pass_a * g_l, s_r + pass_a * g_r
        g_l, g_r = s_l, s_r
        adj_l[i], adj_r[i] = g_l, g_r

    lane = lax.broadcasted_iota(jnp.int32, (planes_y, planes_z), 1)
    line = lax.broadcasted_iota(jnp.int32, (planes_y, planes_z), 0)
    inside = (line < planes_y - 1, lane < planes_z - 1)
    w_l, w_r = adj_l[n - 1] * over_a, adj_r[n - 1] * over_a
    free = [None] * 4
    for i in reversed(range(n)):
        if i < n - 1:
            pass_a, drop_a = pass_a_ref[i + 1], drop_a_ref[i + 1]
            w_l, w_r = pass_a * w_l + drop_a * adj_l[i], pass_a * w_r + drop_a * adj_r[i]
        adj_l[i], adj_r[i] = w_l, w_r
        index = stratum_ref[i]
        half_t = lookup(numbers["half_t"], index)
        por = lookup(numbers["por"], index)
        c0, c1, c2, c3 = [conc_ref[k, i] for k in range(4)]
        source_a = por * c0 + lookup(numbers["alpha_a"], index) * c2
        source_b = (
            por * c1
            + lookup(numbers["alpha_b"], index) * c3
            + lookup(numbers["delta"], index) * c2
        )
        for axis in (0, 1):
            last = half_t.shape[axis] - 1
            face = jnp.where(
                inside[axis], recip(half_t + pltpu.roll(half_t, last, axis)), 0.0
            )
            flow_a = face * shifted_difference(c0, axis)
            flow_b = face * shifted_difference(c1, axis)
            source_a = source_a + (flow_a - pltpu.roll(flow_a, 1, axis))
            source_b = source_b + (flow_b - pltpu.roll(flow_b, 1, axis))
        source_a_ref[i], source_b_ref[i] = source_a, source_b
        terms = [
            left_a[i] * source_a,
            right_a[i] * source_a,
            left_b[i] * source_b + w_l * source_a,
            right_b[i] * source_b + w_r * source_a,
        ]
        free = [t if f is None else f + t for f, t in zip(free, terms)]

    quantities = [
        left_a[0] + first_half_a,
        right_a[0],
        over_a + half_a,
        left_b[0] + first_half_b,
        right_b[0],
        over_b + half_b,
        *couple,
        *free,
    ]
    rows, width = block
    for p in range(pay_ref.shape[0]):
        y, z = chunk_place(p, block, planes_z)
        for q, value in enumerate(quantities):
            pay_ref[p, q * rows : (q + 1) * rows, :] = value[y : y + rows, z : z + width]
    for k, ref in enumerate((left_a, right_a, left_b, right_b, adj_l, adj_r)):
        edge_ref[0, k] = ref[:, 0, :]
        edge_ref[1, k] = ref[:, planes_y - 1, :]


def border_kernel(
    block,
    tab_ref,
    own_lo_ref,
    own_hi_ref,
    next_lo_ref,
    next_hi_ref,
    edge_ref,
    pay_ref,
    out_ref,
    flow_ref,
):
    peers = pay_ref.shape[0]
    rows, width = block
    planes_z = own_lo_ref.shape[2]
    half_row = 0.5 / jnp.broadcast_to(tab_ref[TRANS : TRANS + 1, :], (SUB, LANE))
    out_ref[...] = pay_ref[...]
    for side, (own_ref, next_ref) in enumerate(
        ((own_lo_ref, next_lo_ref), (own_hi_ref, next_hi_ref))
    ):
        own_id = own_ref[2].astype(jnp.int32) - 1
        next_id = next_ref[2].astype(jnp.int32) - 1
        present = next_id >= 0
        half = lookup(half_row, own_id) + lookup(half_row, jnp.maximum(next_id, 0))
        face = jnp.where(present, recip(half), 0.0)
        flow_a = face * (next_ref[0] - own_ref[0])
        flow_b = face * (next_ref[1] - own_ref[1])
        flow_ref[side, 0], flow_ref[side, 1] = flow_a, flow_b
        l_a, r_a, l_b, r_b, w_l, w_r = [edge_ref[side, k] for k in range(6)]
        changes = {
            FA_L: l_a * flow_a,
            FA_R: r_a * flow_a,
            FB_L: l_b * flow_b + w_l * flow_a,
            FB_R: r_b * flow_b + w_r * flow_a,
        }
        across = planes_z // width
        for q, change in changes.items():
            total = jnp.sum(change, axis=0, keepdims=True)
            for part in range(across):
                p = part if side == 0 else peers - across + part
                row = q * rows + (0 if side == 0 else rows - 1)
                out_ref[p, row : row + 1, :] = (
                    pay_ref[p, row : row + 1, :] + total[:, part * width : (part + 1) * width]
                )


def chain_kernel(block, pay_ref, out_ref):
    peers = pay_ref.shape[0]
    rows, width = block

    def take(segment, q):
        return pay_ref[segment, q * rows : (q + 1) * rows, :]

    count = peers - 1
    pass_a, over_a, rhs_a = [None] * count, [None] * count, [None] * count
    pass_b, over_b = [None] * count, [None] * count
    for k in range(count):
        diag_a = take(k, ZA_RR) + take(k + 1, ZA_LL)
        diag_b = take(k, ZB_RR) + take(k + 1, ZB_LL)
        rhs = take(k, FA_R) - take(k + 1, FA_L)
        if k > 0:
            off_a, off_b = take(k, ZA_LR), take(k, ZB_LR)
            ratio_a = off_a * over_a[k - 1]
            pass_a[k - 1] = ratio_a
            diag_a = diag_a - off_a * ratio_a
            rhs = rhs + ratio_a * rhs_a[k - 1]
            ratio_b = off_b * over_b[k - 1]
            pass_b[k - 1] = ratio_b
            diag_b = diag_b - off_b * ratio_b
        over_a[k], over_b[k], rhs_a[k] = recip(diag_a), recip(diag_b), rhs
    current_a = [None] * count
    for k in reversed(range(count)):
        value = rhs_a[k] * over_a[k]
        if k < count - 1:
            value = value + pass_a[k] * current_a[k + 1]
        current_a[k] = value
    nothing = jnp.zeros((rows, width), jnp.float32)
    into = [nothing] + current_a + [nothing]
    rhs_b = [None] * count
    for k in range(count):
        rhs = (
            take(k, FB_R)
            - take(k + 1, FB_L)
            + take(k, C_RL) * into[k]
            - (take(k, C_RR) + take(k + 1, C_LL)) * into[k + 1]
            + take(k + 1, C_LR) * into[k + 2]
        )
        if k > 0:
            rhs = rhs + pass_b[k - 1] * rhs_b[k - 1]
        rhs_b[k] = rhs
    current_b = [None] * count
    for k in reversed(range(count)):
        value = rhs_b[k] * over_b[k]
        if k < count - 1:
            value = value + pass_b[k] * current_b[k + 1]
        current_b[k] = value
    into_b = [nothing] + current_b + [nothing]
    for k in range(peers):
        values = (into[k], -into[k + 1], into_b[k], -into_b[k + 1])
        for q, value in enumerate(values):
            out_ref[k, q * rows : (q + 1) * rows, :] = value


def final_kernel(
    block,
    tab_ref,
    stratum_ref,
    conc_ref,
    pass_a_ref,
    drop_a_ref,
    pass_b_ref,
    drop_b_ref,
    over_ref,
    source_a_ref,
    source_b_ref,
    flow_ref,
    current_ref,
    out_ref,
    gather_a,
    gather_b,
):
    n, planes_y, planes_z = stratum_ref.shape
    peers = current_ref.shape[0]
    rows, width = block
    numbers = derived(tab_ref)
    across = planes_z // width

    def plane(q):
        lines = []
        for p in range(0, peers, across):
            pieces = [current_ref[p + j, q * rows : (q + 1) * rows, :] for j in range(across)]
            lines.append(jnp.concatenate(pieces, axis=1) if across > 1 else pieces[0])
        return jnp.concatenate(lines, axis=0)

    line = lax.broadcasted_iota(jnp.int32, (planes_y, planes_z), 0)
    first_line, last_line = line == 0, line == planes_y - 1

    def with_border(source, component, i):
        low = jnp.broadcast_to(flow_ref[0, component, i : i + 1, :], source.shape)
        high = jnp.broadcast_to(flow_ref[1, component, i : i + 1, :], source.shape)
        return source + jnp.where(first_line, low, jnp.where(last_line, high, 0.0))

    value = plane(0)
    for i in range(n):
        value = with_border(source_a_ref[i], 0, i) + value
        if i < n - 1:
            gather_a[i] = value
            value = pass_a_ref[i + 1] * value
    x = (value + plane(1)) * over_ref[0]
    for i in reversed(range(n)):
        if i < n - 1:
            x = pass_a_ref[i + 1] * x + drop_a_ref[i + 1] * gather_a[i]
        out_ref[0, i] = x
    value = plane(2)
    for i in range(n):
        kappa = lookup(numbers["kappa"], stratum_ref[i])
        value = with_border(source_b_ref[i], 1, i) + kappa * out_ref[0, i] + value
        if i < n - 1:
            gather_b[i] = value
            value = pass_b_ref[i + 1] * value
    x = (value + plane(3)) * over_ref[1]
    for i in reversed(range(n)):
        if i < n - 1:
            x = pass_b_ref[i + 1] * x + drop_b_ref[i + 1] * gather_b[i]
        out_ref[1, i] = x
        index = stratum_ref[i]
        x2 = (
            lookup(numbers["beta"], index) * conc_ref[2, i]
            + lookup(numbers["gamma"], index) * out_ref[0, i]
        )
        out_ref[2, i] = x2
        out_ref[3, i] = (
            lookup(numbers["free_b"], index) * conc_ref[3, i]
            + lookup(numbers["share_b"], index) * x
            + lookup(numbers["decay_b"], index) * x2
        )


def call(kernel, outs, scratch=()):
    return pl.pallas_call(
        kernel,
        out_shape=[jax.ShapeDtypeStruct(shape, jnp.float32) for shape in outs],
        scratch_shapes=[pltpu.VMEM(shape, jnp.float32) for shape in scratch],
        compiler_params=pltpu.CompilerParams(vmem_limit_bytes=VMEM_LIMIT),
    )


def per_device(
    concentration,
    stratum,
    porosity,
    dispersion_table,
    transverse_table,
    exchange_table,
    decay_table,
):
    n, planes_y, planes_z = stratum.shape
    peers = lax.axis_size("flow")
    block = chunk_of(peers, planes_y, planes_z)
    rows, width = block
    cells = (n, planes_y, planes_z)

    numbered = (stratum + 1).astype(jnp.float32)
    own_lo = jnp.concatenate([concentration[:2, :, 0], numbered[None, :, 0]])
    own_hi = jnp.concatenate([concentration[:2, :, -1], numbered[None, :, -1]])
    groups = lax.axis_size("trans")
    up = [(i, i + 1) for i in range(groups - 1)]
    down = [(i + 1, i) for i in range(groups - 1)]
    next_lo = lax.ppermute(own_hi, "trans", up)
    next_hi = lax.ppermute(own_lo, "trans", down)

    table = jnp.stack(
        [
            porosity,
            dispersion_table[:, 0],
            dispersion_table[:, 1],
            transverse_table,
            exchange_table,
            decay_table,
        ]
    )
    strata = porosity.shape[0]
    table = jnp.pad(table, ((0, SUB - 6), (0, LANE - strata)), constant_values=0.5)

    pay_shape = (peers, QUANTITIES * rows, width)
    pay, edge, pass_a, drop_a, pass_b, drop_b, over, source_a, source_b = call(
        functools.partial(local_kernel, block),
        [pay_shape, (2, 6, n, planes_z), cells, cells, cells, cells, (2, planes_y, planes_z), cells, cells],
        [cells] * 9,
    )(table, stratum, concentration)
    pay, flow = call(
        functools.partial(border_kernel, block), [pay_shape, (2, 2, n, planes_z)]
    )(table, own_lo, own_hi, next_lo, next_hi, edge, pay)
    gathered = lax.all_to_all(pay, "flow", 0, 0, tiled=True)
    (currents,) = call(
        functools.partial(chain_kernel, block), [(peers, CURRENTS * rows, width)]
    )(gathered)
    currents = lax.all_to_all(currents, "flow", 0, 0, tiled=True)
    (out,) = call(
        functools.partial(final_kernel, block), [(4,) + cells], [cells] * 2
    )(
        table,
        stratum,
        concentration,
        pass_a,
        drop_a,
        pass_b,
        drop_b,
        over,
        source_a,
        source_b,
        flow,
        currents,
    )
    return out


def solution(mesh):
    in_specs = (P(None, "flow", "trans", None), P("flow", "trans", None), P(), P(), P(), P(), P())
    out_specs = P(None, "flow", "trans", None)
    return jax.shard_map(
        per_device, mesh=mesh, in_specs=in_specs, out_specs=out_specs, check_vma=False
    )
```

time: 617 us -> 42.5 us (0.07); the launches traced: 610 us -> 42.2 us
  other arithmetic: 265 us -> 1.13 us
  blocking collectives: 198 us -> 27.6 us
  local copies, waits for them, and re-layouts: 74.3 us -> 2.84 us
  loops' own time: 61.9 us -> 0 us
  Pallas kernels: 0 us -> 6.19 us
  starting transfers between devices: 10.5 us -> 4.32 us
    all_gather x6 -> x0, blocking collectives: 198 us -> none  [the longest x1 35.9 us: segment_solve(): lax.all_gather(top_right[None], 'flow', axis=0, tiled=True)]
    reduce_sum x193 -> x0, other arithmetic: 95.5 us -> none  [the longest x101 75.4 us: matvec(): return jnp.sum(matrix * vector[None, :, :], axis=1)]
    another operation x6 -> x0, loops' own time: 61.9 us -> none  [the longest x1 20.7 us: segment_solve(): prefix, ignored_low = lax.scan(lower_step, identity, indices, unroll=4)]
    sub x200 -> x0, other arithmetic: 51.2 us -> none  [the longest x116 15.8 us: invert(): element - multiplier * partner]
    select_n x22 -> x0, other arithmetic: 49 us -> none  [the longest x14 11.8 us: upper_step(): jnp.where(keeping, fresh, stale)]
    all_to_all x0 -> x2, blocking collectives: none -> 27.6 us  [the longest x1 17.2 us: per_device(): gathered = lax.all_to_all(pay, 'flow', 0, 0, tiled=True)]
    another operation x136 -> x0, other arithmetic: 22.3 us -> none  [the longest x1 11.2 us: per_device(): jnp.stack([porosity_cell, porosity_cell, 1.0 - porosity_cell, 1.0 - poros...]
    mul x57 -> x0, other arithmetic: 21.5 us -> none  [the longest x16 12.6 us: source_step(): lifted = forcing + jnp.pad(left_num * vector_mobile, ((0, 2), (0, 0)))]
  transfers between devices with their start and end apart: 4 -> 2, of which waited for: 0 -> 0; matrix products, arithmetic and copies ran while one was open for 8% -> 0% of each run, Pallas kernels for 0% -> 9%
where the time goes in v1:
time: 42.5 us; the launch traced here: 42.2 us
  blocking collectives  27.6 us (65%)
  Pallas kernels  6.19 us (15%)
  starting transfers between devices  4.32 us (10%)
  local copies, waits for them, and re-layouts  2.84 us (7%)
  other arithmetic  1.13 us (3%)
    all_to_all x1, blocking collectives, per_device(): gathered = lax.all_to_all(pay, 'flow', 0, 0, tiled=True)  17.2 us
    all_to_all x1, blocking collectives, per_device(): currents = lax.all_to_all(currents, 'flow', 0, 0, tiled=True)  10.3 us
    pallas_call x1, Pallas kernels, per_device(): call(functools.partial(local_kernel, block), [pay_shape, (2, 6, n, planes...  3.73 us
    ppermute x1, starting transfers between devices, per_device(): next_lo = lax.ppermute(own_hi, 'trans', up)  3.03 us
    pallas_call x1, Pallas kernels, per_device(): call(functools.partial(final_kernel, block), [(4,) + cells], [cells] * 2)  2.16 us
    unnamed x18, local copies, waits for them, and re-layouts  1.64 us
    ppermute x1, starting transfers between devices, per_device(): next_hi = lax.ppermute(own_lo, 'trans', down)  1.29 us
    slice x1, local copies, waits for them, and re-layouts, per_device(): own_hi = jnp.concatenate([concentration[:2, :, -1], numbered[None, :, -1]])  1.16 us
  transfers between devices with their start and end apart: 2, of which 0 were waited for; matrix products, arithmetic and copies ran while one was open for 0% of the time, Pallas kernels for 9%

profile of v1, /device:TPU:0, one launch (start us, length us, event | category | flops | bytes accessed | tf_op | source)
XLA Modules:
  0.0 42.2 jit_solution(3429221130812640542)
XLA Ops:
  0.0 0.0 copy-start
  0.0 1.2 %fusion.1 = (f32[2,16,1,256]{3,2,1,0:T(1,128)S(1)}, f32[2,16,1,256]{3,2,1,0:T(1,128)S(1)}) fusion(f32[4,16,16,256]{3,2,1,0:T(8,128)} %conc_ref.3), kind=kLoop, calls=%fused_computation.10 | loop fusion | bytes 131072 | tf_op jit(solution)/shard_map/slice | solution.py:416
  1.2 1.1 %fusion = f32[16,16,256]{2,0,1:T(8,128)S(1)} fusion(s32[16,16,256]{2,1,0:T(8,128)} %stratum_ref.3), kind=kLoop, calls=%fused_computation.1 | loop fusion | flops 131072 | bytes 524288 | tf_op jit(solution)/shard_map/convert_element_type | solution.py:414
  2.3 1.3 %collective-permute-start.1 = (f32[3,16,256]{2,1,0:T(8,128)S(1)}, f32[3,16,256]{2,1,0:T(8,128)S(1)}, u32[]{:S(2)}, u32[]{:S(2)}) collective-permute-start(f32[3,16,256]{2,1,0:T(8,128)S(1)} %pad_maximum_fusion.own_lo_ref), channel_id=1, source_target_pairs={{1,0},{2,1},{3,2},{5,4},{6,5},{7,6},{9,8},{10,9},{11,10},{13,12},{... | collective-permute-start | bytes 147464 | tf_op jit(solution)/shard_map/ppermute | solution.py:421
  3.6 0.0 copy-start.3
  3.7 3.0 %collective-permute-start = (f32[3,16,256]{2,1,0:T(8,128)S(1)}, f32[3,16,256]{2,1,0:T(8,128)S(1)}, u32[]{:S(2)}, u32[]{:S(2)}) collective-permute-start(f32[3,16,256]{2,1,0:T(8,128)S(1)} %pad_maximum_fusion.1.own_hi_ref), channel_id=1, source_target_pairs={{0,1},{1,2},{2,3},{4,5},{5,6},{6,7},{8,9},{9,10},{10,11},{12,13},{... | collective-permute-start | bytes 147464 | tf_op jit(solution)/shard_map/ppermute | solution.py:420
  6.7 0.0 copy-done.3
  6.7 0.0 copy-start.7
  6.7 0.0 copy-start.4
  6.8 0.0 copy-start.5
  6.8 0.0 copy-start.6
  6.8 0.6 %copy-done.7 = f32[16]{0:T(128)S(1)} copy-done((f32[16]{0:T(128)S(1)}, f32[16]{0:T(128)}, u32[]{:S(2)}) %copy-start.7) | copy-done | bytes 88
  7.4 0.0 copy-done.4
  7.4 0.0 copy-done.5
  7.4 0.0 copy-done.6
  7.5 0.0 copy-done
  7.5 0.0 copy-start.1
  7.5 0.9 %copy-done.1 = s32[16,16,256]{2,1,0:T(8,128)S(1)} copy-done((s32[16,16,256]{2,1,0:T(8,128)S(1)}, s32[16,16,256]{2,1,0:T(8,128)}, u32[]{:S(2)}) %copy-start.1) | copy-done | bytes 262168
  8.4 3.7 %shard_map.73 = (f32[8,28,256]{2,1,0:T(8,128)S(1)}, f32[2,6,16,256]{3,2,1,0:T(8,128)S(1)}, f32[16,16,256]{2,1,0:T(8,128)S(1)}, f32[16,16,256]{2,1,0:T(8,128)S(1)...) custom-call(f32[8,128]{1,0:T(8,128)S(1)} %pad.4.tab_ref, ...), custom_call_target="tpu_custom_call" | custom-call | tf_op jit(solution)/shard_map/pallas_call | solution.py:437
  12.2 0.0 collective-permute-done.1.next_hi_ref
  12.2 0.0 collective-permute-done.next_lo_ref
  12.2 0.1 shard_map.74
  12.3 17.2 %all_to_all.10.pay_ref = f32[8,28,256]{2,1,0:T(8,128)S(1)} all-to-all(f32[8,28,256]{2,1,0:T(8,128)S(1)} %get-tuple-element.26), channel_id=1, replica_groups=mesh['flow'=8,'trans'=4] {'flow'}, dimensions={0} | all-to-all | bytes 458752 | tf_op jit(solution)/shard_map/all_to_all | solution.py:445
  29.6 0.0 copy-start.2
  29.6 0.2 shard_map.75
  29.7 10.3 %all_to_all.11.current_ref = f32[8,8,256]{2,1,0:T(8,128)S(1)} all-to-all(f32[8,8,256]{2,1,0:T(8,128)S(1)} %shard_map.75), channel_id=1, replica_groups=mesh['flow'=8,'trans'=4] {'flow'}, dimensions={0} | all-to-all | bytes 131072 | tf_op jit(solution)/shard_map/all_to_all | solution.py:449
  40.1 0.0 copy-done.2
  40.1 2.2 %shard_map.76 = f32[4,16,16,256]{3,2,1,0:T(8,128)} custom-call(f32[8,128]{1,0:T(8,128)S(1)} %pad.4.tab_ref, s32[16,16,256]{2,1,0:T(8,128)S(1)} %copy-done.2, f32[4,16,16,256]{3,2,1,0:T(8,128)S(1)} %copy-done, f32[16,16,256]{2,1,0:T(8,128)S(1)} %get-tuple-element.16.pass_a_ref, f32[16,16,256]{2,1,0:T(8,128)S(1)} %get-tuple-element.17.drop_a_ref, ...), custom_call_target="tpu_custom_call" | custom-call | tf_op jit(solution)/shard_map/pallas_call | solution.py:450
  (8 shorter events, 0.1 us)
Async XLA Ops:
  0.0 7.5 %copy-start = (f32[4,16,16,256]{3,2,1,0:T(8,128)S(1)}, f32[4,16,16,256]{3,2,1,0:T(8,128)}, u32[]{:S(2)}) copy-start(f32[4,16,16,256]{3,2,1,0:T(8,128)} %conc_ref.3) | copy-start | bytes 3145732
  2.3 9.8 %collective-permute-start.1 = (f32[3,16,256]{2,1,0:T(8,128)S(1)}, f32[3,16,256]{2,1,0:T(8,128)S(1)}, u32[]{:S(2)}, u32[]{:S(2)}) collective-permute-start(f32[3,16,256]{2,1,0:T(8,128)S(1)} %pad_maximum_fusion.own_lo_ref), channel_id=1, source_target_pairs={{1,0},{2,1},{3,2},{5,4},{6,5},{7,6},{9,8},{10,9},{11,10},{13,12},{... | collective-permute-start | bytes 147464 | tf_op jit(solution)/shard_map/ppermute | solution.py:421
  3.6 3.1 %copy-start.3 = (f32[16,2]{0,1:T(2,128)S(1)}, f32[16,2]{0,1:T(2,128)}, u32[]{:S(2)}) copy-start(f32[16,2]{0,1:T(2,128)} %param.10) | copy-start | bytes 388
  3.7 8.5 %collective-permute-start = (f32[3,16,256]{2,1,0:T(8,128)S(1)}, f32[3,16,256]{2,1,0:T(8,128)S(1)}, u32[]{:S(2)}, u32[]{:S(2)}) collective-permute-start(f32[3,16,256]{2,1,0:T(8,128)S(1)} %pad_maximum_fusion.1.own_hi_ref), channel_id=1, source_target_pairs={{0,1},{1,2},{2,3},{4,5},{5,6},{6,7},{8,9},{9,10},{10,11},{12,13},{... | collective-permute-start | bytes 147464 | tf_op jit(solution)/shard_map/ppermute | solution.py:420
  6.7 0.7 %copy-start.7 = (f32[16]{0:T(128)S(1)}, f32[16]{0:T(128)}, u32[]{:S(2)}) copy-start(f32[16]{0:T(128)} %param.13) | copy-start | bytes 196
  6.7 0.7 %copy-start.4 = (f32[16]{0:T(128)S(1)}, f32[16]{0:T(128)}, u32[]{:S(2)}) copy-start(f32[16]{0:T(128)} %param.9) | copy-start | bytes 196
  6.8 0.7 %copy-start.5 = (f32[16]{0:T(128)S(1)}, f32[16]{0:T(128)}, u32[]{:S(2)}) copy-start(f32[16]{0:T(128)} %param.11) | copy-start | bytes 196
  6.8 0.7 %copy-start.6 = (f32[16]{0:T(128)S(1)}, f32[16]{0:T(128)}, u32[]{:S(2)}) copy-start(f32[16]{0:T(128)} %param.12) | copy-start | bytes 196
  7.5 1.0 %copy-start.1 = (s32[16,16,256]{2,1,0:T(8,128)S(1)}, s32[16,16,256]{2,1,0:T(8,128)}, u32[]{:S(2)}) copy-start(s32[16,16,256]{2,1,0:T(8,128)} %stratum_ref.3) | copy-start | bytes 786436
  29.6 10.5 %copy-start.2 = (s32[16,16,256]{2,1,0:T(8,128)S(1)}, s32[16,16,256]{2,1,0:T(8,128)}, u32[]{:S(2)}) copy-start(s32[16,16,256]{2,1,0:T(8,128)} %stratum_ref.3) | copy-start | bytes 786436

commit v2 on v1

--- a/solution.py
+++ b/solution.py
@@ -8,7 +8,6 @@
 from jax.sharding import PartitionSpec as P
 
 SUB, LANE = 8, 128
-POR, DISP_A, DISP_B, TRANS, EXCH, DECAY = range(6)
 ZA_LL, ZA_LR, ZA_RR, ZB_LL, ZB_LR, ZB_RR, C_LL, C_LR, C_RL, C_RR, FA_L, FA_R, FB_L, FB_R = range(14)
 QUANTITIES = 14
 CURRENTS = 4
@@ -32,10 +31,26 @@
     return jnp.concatenate(tiles, axis=0)
 
 
-def derived(tab_ref):
-    por, disp_a, disp_b, trans, exch, decay = [
-        jnp.broadcast_to(tab_ref[k : k + 1, :], (SUB, LANE)) for k in range(6)
-    ]
+NUMBERS = (
+    "por",
+    "shunt_a",
+    "shunt_b",
+    "half_a",
+    "half_b",
+    "half_t",
+    "beta",
+    "gamma",
+    "alpha_a",
+    "alpha_b",
+    "kappa",
+    "delta",
+    "free_b",
+    "share_b",
+    "decay_b",
+)
+
+
+def derive(por, disp_a, disp_b, trans, exch, decay):
     immobile = 1.0 - por
     over_a = 1.0 / (immobile + exch + decay)
     over_b = 1.0 / (immobile + exch)
@@ -61,6 +76,16 @@
     )
 
 
+class Numbers:
+    def __init__(self, tab_ref):
+        self.tab_ref = tab_ref
+
+    def __call__(self, name, index):
+        k = NUMBERS.index(name)
+        row = jnp.broadcast_to(self.tab_ref[k : k + 1, :], (SUB, LANE))
+        return lookup(row, index)
+
+
 def chunk_of(peers, planes_y, planes_z):
     if peers <= planes_y:
         return planes_y // peers, planes_z
@@ -75,6 +100,64 @@
 
 def shifted_difference(value, axis):
     return pltpu.roll(value, value.shape[axis] - 1, axis) - value
+
+
+def pack_kernel(
+    conc_hbm,
+    stratum_hbm,
+    por_hbm,
+    disp_hbm,
+    trans_hbm,
+    exch_hbm,
+    decay_hbm,
+    lo_ref,
+    hi_ref,
+    tab_ref,
+    conc_ref,
+    stratum_ref,
+    por_ref,
+    disp_ref,
+    trans_ref,
+    exch_ref,
+    decay_ref,
+    raw,
+    sems,
+):
+    moves = [
+        (stratum_hbm, stratum_ref),
+        (conc_hbm.at[0:2], conc_ref.at[0:2]),
+        (por_hbm, por_ref),
+        (disp_hbm, disp_ref),
+        (trans_hbm, trans_ref),
+        (exch_hbm, exch_ref),
+        (decay_hbm, decay_ref),
+        (conc_hbm.at[2:4], conc_ref.at[2:4]),
+    ]
+    copies = [pltpu.make_async_copy(src, dst, sems.at[k]) for k, (src, dst) in enumerate(moves)]
+    for copy in copies:
+        copy.start()
+    raw[...] = jnp.full(raw.shape, 0.5, jnp.float32)
+    for copy in copies[2:7]:
+        copy.wait()
+    strata = por_ref.shape[1]
+    raw[0:1, 0:strata] = por_ref[...]
+    raw[1:3, 0:strata] = disp_ref[...]
+    raw[3:4, 0:strata] = trans_ref[...]
+    raw[4:5, 0:strata] = exch_ref[...]
+    raw[5:6, 0:strata] = decay_ref[...]
+    made = derive(*[raw[k : k + 1, :] for k in range(6)])
+    for k, name in enumerate(NUMBERS):
+        tab_ref[k : k + 1, :] = made[name]
+    tab_ref[len(NUMBERS) : 2 * SUB, :] = raw[0 : 2 * SUB - len(NUMBERS), :]
+    copies[0].wait()
+    last = stratum_ref.shape[1] - 1
+    for ref, y in ((lo_ref, 0), (hi_ref, last)):
+        ref[2] = (stratum_ref[:, y, :] + 1).astype(jnp.float32)
+    copies[1].wait()
+    for ref, y in ((lo_ref, 0), (hi_ref, last)):
+        ref[0] = conc_ref[0, :, y, :]
+        ref[1] = conc_ref[1, :, y, :]
+    copies[7].wait()
 
 
 def local_kernel(
@@ -102,14 +185,14 @@
     adj_r,
 ):
     n, planes_y, planes_z = stratum_ref.shape
-    numbers = derived(tab_ref)
+    number = Numbers(tab_ref)
 
     cond_a = cond_b = half_a = half_b = through_a = through_b = None
     for i in range(n):
         index = stratum_ref[i]
-        shunt_a, shunt_b = lookup(numbers["shunt_a"], index), lookup(numbers["shunt_b"], index)
-        new_a, new_b = lookup(numbers["half_a"], index), lookup(numbers["half_b"], index)
-        kappa_ref[i] = lookup(numbers["kappa"], index)
+        shunt_a, shunt_b = number("shunt_a", index), number("shunt_b", index)
+        new_a, new_b = number("half_a", index), number("half_b", index)
+        kappa_ref[i] = number("kappa", index)
         if i == 0:
             first_half_a, first_half_b = new_a, new_b
             cond_a, cond_b = shunt_a, shunt_b
@@ -162,14 +245,14 @@
             w_l, w_r = pass_a * w_l + drop_a * adj_l[i], pass_a * w_r + drop_a * adj_r[i]
         adj_l[i], adj_r[i] = w_l, w_r
         index = stratum_ref[i]
-        half_t = lookup(numbers["half_t"], index)
-        por = lookup(numbers["por"], index)
+        half_t = number("half_t", index)
+        por = number("por", index)
         c0, c1, c2, c3 = [conc_ref[k, i] for k in range(4)]
-        source_a = por * c0 + lookup(numbers["alpha_a"], index) * c2
+        source_a = por * c0 + number("alpha_a", index) * c2
         source_b = (
             por * c1
-            + lookup(numbers["alpha_b"], index) * c3
-            + lookup(numbers["delta"], index) * c2
+            + number("alpha_b", index) * c3
+            + number("delta", index) * c2
         )
         for axis in (0, 1):
             last = half_t.shape[axis] - 1
@@ -224,7 +307,7 @@
     peers = pay_ref.shape[0]
     rows, width = block
     planes_z = own_lo_ref.shape[2]
-    half_row = 0.5 / jnp.broadcast_to(tab_ref[TRANS : TRANS + 1, :], (SUB, LANE))
+    number = Numbers(tab_ref)
     out_ref[...] = pay_ref[...]
     for side, (own_ref, next_ref) in enumerate(
         ((own_lo_ref, next_lo_ref), (own_hi_ref, next_hi_ref))
@@ -232,7 +315,7 @@
         own_id = own_ref[2].astype(jnp.int32) - 1
         next_id = next_ref[2].astype(jnp.int32) - 1
         present = next_id >= 0
-        half = lookup(half_row, own_id) + lookup(half_row, jnp.maximum(next_id, 0))
+        half = number("half_t", own_id) + number("half_t", jnp.maximum(next_id, 0))
         face = jnp.where(present, recip(half), 0.0)
         flow_a = face * (next_ref[0] - own_ref[0])
         flow_b = face * (next_ref[1] - own_ref[1])
@@ -333,7 +416,7 @@
     n, planes_y, planes_z = stratum_ref.shape
     peers = current_ref.shape[0]
     rows, width = block
-    numbers = derived(tab_ref)
+    number = Numbers(tab_ref)
     across = planes_z // width
 
     def plane(q):
@@ -364,7 +447,7 @@
         out_ref[0, i] = x
     value = plane(2)
     for i in range(n):
-        kappa = lookup(numbers["kappa"], stratum_ref[i])
+        kappa = number("kappa", stratum_ref[i])
         value = with_border(source_b_ref[i], 1, i) + kappa * out_ref[0, i] + value
         if i < n - 1:
             gather_b[i] = value
@@ -376,14 +459,14 @@
         out_ref[1, i] = x
         index = stratum_ref[i]
         x2 = (
-            lookup(numbers["beta"], index) * conc_ref[2, i]
-            + lookup(numbers["gamma"], index) * out_ref[0, i]
+            number("beta", index) * conc_ref[2, i]
+            + number("gamma", index) * out_ref[0, i]
         )
         out_ref[2, i] = x2
         out_ref[3, i] = (
-            lookup(numbers["free_b"], index) * conc_ref[3, i]
-            + lookup(numbers["share_b"], index) * x
-            + lookup(numbers["decay_b"], index) * x2
+            number("free_b", index) * conc_ref[3, i]
+            + number("share_b", index) * x
+            + number("decay_b", index) * x2
         )
 
 
@@ -411,27 +494,48 @@
     rows, width = block
     cells = (n, planes_y, planes_z)
 
-    numbered = (stratum + 1).astype(jnp.float32)
-    own_lo = jnp.concatenate([concentration[:2, :, 0], numbered[None, :, 0]])
-    own_hi = jnp.concatenate([concentration[:2, :, -1], numbered[None, :, -1]])
+    halo = (3, n, planes_z)
+    strata = porosity.shape[0]
+    hbm = pl.BlockSpec(memory_space=pltpu.HBM)
+    own_lo, own_hi, table, concentration, stratum = pl.pallas_call(
+        pack_kernel,
+        out_shape=[
+            jax.ShapeDtypeStruct(halo, jnp.float32),
+            jax.ShapeDtypeStruct(halo, jnp.float32),
+            jax.ShapeDtypeStruct((2 * SUB, LANE), jnp.float32),
+            jax.ShapeDtypeStruct(concentration.shape, jnp.float32),
+            jax.ShapeDtypeStruct(cells, jnp.int32),
+        ],
+        in_specs=[hbm] * 7,
+        scratch_shapes=[
+            pltpu.VMEM((1, strata), jnp.float32),
+            pltpu.VMEM((2, strata), jnp.float32),
+            pltpu.VMEM((1, strata), jnp.float32),
+            pltpu.VMEM((1, strata), jnp.float32),
+            pltpu.VMEM((1, strata), jnp.float32),
+            pltpu.VMEM((SUB, LANE), jnp.float32),
+            pltpu.SemaphoreType.DMA((8,)),
+        ],
+        compiler_params=pltpu.CompilerParams(vmem_limit_bytes=VMEM_LIMIT),
+    )(
+        *[
+            pltpu.with_memory_space_constraint(value, pltpu.HBM)
+            for value in (
+                concentration,
+                stratum,
+                porosity[None],
+                dispersion_table.T,
+                transverse_table[None],
+                exchange_table[None],
+                decay_table[None],
+            )
+        ]
+    )
     groups = lax.axis_size("trans")
     up = [(i, i + 1) for i in range(groups - 1)]
     down = [(i + 1, i) for i in range(groups - 1)]
     next_lo = lax.ppermute(own_hi, "trans", up)
     next_hi = lax.ppermute(own_lo, "trans", down)
-
-    table = jnp.stack(
-        [
-            porosity,
-            dispersion_table[:, 0],
-            dispersion_table[:, 1],
-            transverse_table,
-            exchange_table,
-            decay_table,
-        ]
-    )
-    strata = porosity.shape[0]
-    table = jnp.pad(table, ((0, SUB - 6), (0, LANE - strata)), constant_values=0.5)
 
     pay_shape = (peers, QUANTITIES * rows, width)
     pay, edge, pass_a, drop_a, pass_b, drop_b, over, source_a, source_b = call(

time: 42.5 us -> 39.8 us (0.936)
  local copies, waits for them, and re-layouts: 2.84 us -> 0 us
  Pallas kernels: 6.19 us -> 7.61 us
  other arithmetic: 1.13 us -> 0 us
    unnamed x18 -> x0, local copies, waits for them, and re-layouts: 1.64 us -> none
    pallas_call x0 -> x1, Pallas kernels: none -> 1.43 us  [per_device(): pl.pallas_call(pack_kernel, out_shape=[jax.ShapeDtypeStruct(halo, jnp.flo...]
    slice x1 -> x0, local copies, waits for them, and re-layouts: 1.16 us -> none  [per_device(): own_hi = jnp.concatenate([concentration[:2, :, -1], numbered[None, :, -1]])]
    convert_element_type x1 -> x0, other arithmetic: 1.12 us -> none  [per_device(): numbered = (stratum + 1).astype(jnp.float32)]
where the time goes in v2:
time: 39.8 us; the launch traced here: 39.6 us
  blocking collectives  27.6 us (69%)
  Pallas kernels  7.61 us (19%)
  starting transfers between devices  4.32 us (11%)
    all_to_all x1, blocking collectives, per_device(): gathered = lax.all_to_all(pay, 'flow', 0, 0, tiled=True)  17.2 us
    all_to_all x1, blocking collectives, per_device(): currents = lax.all_to_all(currents, 'flow', 0, 0, tiled=True)  10.3 us
    pallas_call x1, Pallas kernels, per_device(): call(functools.partial(local_kernel, block), [pay_shape, (2, 6, n, planes...  3.74 us
    ppermute x1, starting transfers between devices, per_device(): next_lo = lax.ppermute(own_hi, 'trans', up)  3.03 us
    pallas_call x1, Pallas kernels, per_device(): call(functools.partial(final_kernel, block), [(4,) + cells], [cells] * 2)  2.14 us
    pallas_call x1, Pallas kernels, per_device(): pl.pallas_call(pack_kernel, out_shape=[jax.ShapeDtypeStruct(halo, jnp.flo...  1.43 us
    ppermute x1, starting transfers between devices, per_device(): next_hi = lax.ppermute(own_lo, 'trans', down)  1.29 us
  transfers between devices with their start and end apart: 2, of which 0 were waited for; matrix products, arithmetic and copies ran while one was open for 0% of the time, Pallas kernels for 9%

profile of v2, /device:TPU:0, one launch (start us, length us, event | category | flops | bytes accessed | tf_op | source)
XLA Modules:
  0.0 39.6 jit_solution(5404372524903275011)
XLA Ops:
  0.0 1.4 %shard_map.73 = (f32[3,16,256]{2,1,0:T(8,128)S(1)}, f32[3,16,256]{2,1,0:T(8,128)S(1)}, f32[16,128]{1,0:T(8,128)S(1)}, f32[4,16,16,256]{3,2,1,0:T(8,128)S(1)}, s32[16,16,256]{2,1,0:T(8,128)S(1)}) custom-call(f32[4,16,16,256]{3,2,1,0:T(8,128)} %conc_hbm.1, s32[16,16,256]{2,1,0:T(8,128)} %stratum_hbm.1, f32[1,16]{1,0:T(1,128)} %bitcast.6, f32[2,16]{1,0:T(2,128)} %bitcast.5, ...), custom_call_target="tpu_custom_call" | custom-call | tf_op jit(solution)/shard_map/pallas_call | solution.py:500
  1.4 1.3 %collective-permute-start.1 = (f32[3,16,256]{2,1,0:T(8,128)S(1)}, f32[3,16,256]{2,1,0:T(8,128)S(1)}, u32[]{:S(2)}, u32[]{:S(2)}) collective-permute-start(f32[3,16,256]{2,1,0:T(8,128)S(1)} %get-tuple-element.31.own_lo_ref), channel_id=1, source_target_pairs={{1,0},{2,1},{3,2},{5,4},{6,5},{7,6},{9,8},{10,9},{11,10},{13,12},{... | collective-permute-start | bytes 147464 | tf_op jit(solution)/shard_map/ppermute | solution.py:538
  2.7 3.0 %collective-permute-start = (f32[3,16,256]{2,1,0:T(8,128)S(1)}, f32[3,16,256]{2,1,0:T(8,128)S(1)}, u32[]{:S(2)}, u32[]{:S(2)}) collective-permute-start(f32[3,16,256]{2,1,0:T(8,128)S(1)} %get-tuple-element.32.own_hi_ref), channel_id=1, source_target_pairs={{0,1},{1,2},{2,3},{4,5},{5,6},{6,7},{8,9},{9,10},{10,11},{12,13},{... | collective-permute-start | bytes 147464 | tf_op jit(solution)/shard_map/ppermute | solution.py:537
  5.8 3.7 %shard_map.74 = (f32[8,28,256]{2,1,0:T(8,128)S(1)}, f32[2,6,16,256]{3,2,1,0:T(8,128)S(1)}, f32[16,16,256]{2,1,0:T(8,128)S(1)}, f32[16,16,256]{2,1,0:T(8,128)S(1)...) custom-call(f32[16,128]{1,0:T(8,128)S(1)} %get-tuple-element.21.tab_, ...), custom_call_target="tpu_custom_call" | custom-call | tf_op jit(solution)/shard_map/pallas_call | solution.py:541
  9.5 0.0 collective-permute-done.1.next_hi_ref
  9.5 0.0 collective-permute-done.next_lo_ref
  9.5 0.1 shard_map.75
  9.7 17.2 %all_to_all.10.pay_ref = f32[8,28,256]{2,1,0:T(8,128)S(1)} all-to-all(f32[8,28,256]{2,1,0:T(8,128)S(1)} %get-tuple-element.36), channel_id=1, replica_groups=mesh['flow'=8,'trans'=4] {'flow'}, dimensions={0} | all-to-all | bytes 458752 | tf_op jit(solution)/shard_map/all_to_all | solution.py:549
  26.9 0.2 shard_map.76
  27.1 10.3 %all_to_all.11.current_ref = f32[8,8,256]{2,1,0:T(8,128)S(1)} all-to-all(f32[8,8,256]{2,1,0:T(8,128)S(1)} %shard_map.76), channel_id=1, replica_groups=mesh['flow'=8,'trans'=4] {'flow'}, dimensions={0} | all-to-all | bytes 131072 | tf_op jit(solution)/shard_map/all_to_all | solution.py:553
  37.4 2.1 %shard_map.77 = f32[4,16,16,256]{3,2,1,0:T(8,128)} custom-call(f32[16,128]{1,0:T(8,128)S(1)} %get-tuple-element.21.tab_ref, s32[16,16,256]{2,1,0:T(8,128)S(1)} %get-tuple-element.22.stratum_ref, f32[4,16,16,256]{3,2,1,0:T(8,128)S(1)} %get-tuple-element.23.conc_ref, f32[16,16,256]{2,1,0:T(8,128)S(1)} %get-tuple-element.24.pass_a_ref, ...), custom_call_target="tpu_custom_call" | custom-call | tf_op jit(solution)/shard_map/pallas_call | solution.py:554
Async XLA Ops:
  1.4 8.1 %collective-permute-start.1 = (f32[3,16,256]{2,1,0:T(8,128)S(1)}, f32[3,16,256]{2,1,0:T(8,128)S(1)}, u32[]{:S(2)}, u32[]{:S(2)}) collective-permute-start(f32[3,16,256]{2,1,0:T(8,128)S(1)} %get-tuple-element.31.own_lo_ref), channel_id=1, source_target_pairs={{1,0},{2,1},{3,2},{5,4},{6,5},{7,6},{9,8},{10,9},{11,10},{13,12},{... | collective-permute-start | bytes 147464 | tf_op jit(solution)/shard_map/ppermute | solution.py:538
  2.7 6.8 %collective-permute-start = (f32[3,16,256]{2,1,0:T(8,128)S(1)}, f32[3,16,256]{2,1,0:T(8,128)S(1)}, u32[]{:S(2)}, u32[]{:S(2)}) collective-permute-start(f32[3,16,256]{2,1,0:T(8,128)S(1)} %get-tuple-element.32.own_hi_ref), channel_id=1, source_target_pairs={{0,1},{1,2},{2,3},{4,5},{5,6},{6,7},{8,9},{9,10},{10,11},{12,13},{... | collective-permute-start | bytes 147464 | tf_op jit(solution)/shard_map/ppermute | solution.py:537

commit v3 on v2

--- a/solution.py
+++ b/solution.py
@@ -92,10 +92,36 @@
     return 1, planes_y * planes_z // peers
 
 
-def chunk_place(which, block, planes_z):
+def chunk_rows(block):
+    return block[0] * block[1] // LANE
+
+
+def store_chunks(ref, q, value, block):
+    rows, width = block
+    across = value.shape[1] // width
+    base = q * chunk_rows(block)
+    for p in range(ref.shape[0]):
+        y, z = (p // across) * rows, (p % across) * width
+        for k in range(width // LANE):
+            low = z + k * LANE
+            ref[p, base + k * rows : base + (k + 1) * rows, :] = value[
+                y : y + rows, low : low + LANE
+            ]
+
+
+def load_chunks(ref, q, block, planes_z):
     rows, width = block
     across = planes_z // width
-    return (which // across) * rows, (which % across) * width
+    base = q * chunk_rows(block)
+    lines = []
+    for p in range(0, ref.shape[0], across):
+        pieces = [
+            ref[p + j, base + k * rows : base + (k + 1) * rows, :]
+            for j in range(across)
+            for k in range(width // LANE)
+        ]
+        lines.append(jnp.concatenate(pieces, axis=1))
+    return jnp.concatenate(lines, axis=0)
 
 
 def shifted_difference(value, axis):
@@ -161,7 +187,6 @@
 
 
 def local_kernel(
-    block,
     tab_ref,
     stratum_ref,
     conc_ref,
@@ -282,18 +307,16 @@
         *couple,
         *free,
     ]
-    rows, width = block
-    for p in range(pay_ref.shape[0]):
-        y, z = chunk_place(p, block, planes_z)
-        for q, value in enumerate(quantities):
-            pay_ref[p, q * rows : (q + 1) * rows, :] = value[y : y + rows, z : z + width]
+    half = planes_y // 2
+    for q, value in enumerate(quantities):
+        pay_ref[0, q] = value[:half]
+        pay_ref[1, q] = value[half:]
     for k, ref in enumerate((left_a, right_a, left_b, right_b, adj_l, adj_r)):
         edge_ref[0, k] = ref[:, 0, :]
         edge_ref[1, k] = ref[:, planes_y - 1, :]
 
 
 def border_kernel(
-    block,
     tab_ref,
     own_lo_ref,
     own_hi_ref,
@@ -304,9 +327,6 @@
     out_ref,
     flow_ref,
 ):
-    peers = pay_ref.shape[0]
-    rows, width = block
-    planes_z = own_lo_ref.shape[2]
     number = Numbers(tab_ref)
     out_ref[...] = pay_ref[...]
     for side, (own_ref, next_ref) in enumerate(
@@ -327,20 +347,65 @@
             FB_L: l_b * flow_b + w_l * flow_a,
             FB_R: r_b * flow_b + w_r * flow_a,
         }
-        across = planes_z // width
+        row = 0 if side == 0 else pay_ref.shape[2] - 1
         for q, change in changes.items():
             total = jnp.sum(change, axis=0, keepdims=True)
-            for part in range(across):
-                p = part if side == 0 else peers - across + part
-                row = q * rows + (0 if side == 0 else rows - 1)
-                out_ref[p, row : row + 1, :] = (
-                    pay_ref[p, row : row + 1, :] + total[:, part * width : (part + 1) * width]
-                )
+            out_ref[side, q, row : row + 1, :] = pay_ref[side, q, row : row + 1, :] + total
+
+
+def merge_kernel(block, pay_ref, out_ref, keep_ref):
+    one = [pay_ref[0, q] for q in range(QUANTITIES)]
+    two = [pay_ref[1, q] for q in range(QUANTITIES)]
+    over_a = recip(one[ZA_RR] + two[ZA_LL])
+    over_b = recip(one[ZB_RR] + two[ZB_LL])
+    across = one[C_RR] + two[C_LL]
+    free_a = over_a * (one[FA_R] - two[FA_L])
+    from_l, from_r = over_a * one[ZA_LR], over_a * two[ZA_LR]
+    free_b = over_b * (one[FB_R] - two[FB_L] - across * free_a)
+    from_l_b, from_r_b = over_b * one[ZB_LR], over_b * two[ZB_LR]
+    cross_l = over_b * (one[C_RL] - across * from_l)
+    cross_r = over_b * (two[C_LR] - across * from_r)
+    merged = {
+        ZA_LL: one[ZA_LL] - one[ZA_LR] * from_l,
+        ZA_LR: one[ZA_LR] * from_r,
+        ZA_RR: two[ZA_RR] - two[ZA_LR] * from_r,
+        ZB_LL: one[ZB_LL] - one[ZB_LR] * from_l_b,
+        ZB_LR: one[ZB_LR] * from_r_b,
+        ZB_RR: two[ZB_RR] - two[ZB_LR] * from_r_b,
+        C_LL: one[C_LL] - one[ZB_LR] * cross_l - one[C_LR] * from_l,
+        C_LR: one[ZB_LR] * cross_r + one[C_LR] * from_r,
+        C_RL: two[ZB_LR] * cross_l + two[C_RL] * from_l,
+        C_RR: two[C_RR] - two[ZB_LR] * cross_r - two[C_RL] * from_r,
+        FA_L: one[FA_L] - one[ZA_LR] * free_a,
+        FA_R: two[FA_R] + two[ZA_LR] * free_a,
+        FB_L: one[FB_L] - one[ZB_LR] * free_b - one[C_LR] * free_a,
+        FB_R: two[FB_R] + two[ZB_LR] * free_b + two[C_RL] * free_a,
+    }
+    for q, value in merged.items():
+        store_chunks(out_ref, q, value, block)
+    for k, value in enumerate(
+        (free_a, from_l, from_r, free_b, from_l_b, from_r_b, cross_l, cross_r)
+    ):
+        keep_ref[k] = value
+
+
+def split_kernel(block, current_ref, keep_ref, out_ref):
+    planes_z = keep_ref.shape[2]
+    l_a, r_a, l_b, r_b = [load_chunks(current_ref, q, block, planes_z) for q in range(CURRENTS)]
+    free_a, from_l, from_r, free_b, from_l_b, from_r_b, cross_l, cross_r = [
+        keep_ref[k] for k in range(8)
+    ]
+    middle_a = free_a + from_l * l_a - from_r * r_a
+    middle_b = free_b + from_l_b * l_b - from_r_b * r_b + cross_l * l_a - cross_r * r_a
+    for q, value in enumerate((l_a, -middle_a, l_b, -middle_b)):
+        out_ref[0, q] = value
+    for q, value in enumerate((middle_a, r_a, middle_b, r_b)):
+        out_ref[1, q] = value
 
 
 def chain_kernel(block, pay_ref, out_ref):
     peers = pay_ref.shape[0]
-    rows, width = block
+    rows = chunk_rows(block)
 
     def take(segment, q):
         return pay_ref[segment, q * rows : (q + 1) * rows, :]
@@ -368,7 +433,7 @@
         if k < count - 1:
             value = value + pass_a[k] * current_a[k + 1]
         current_a[k] = value
-    nothing = jnp.zeros((rows, width), jnp.float32)
+    nothing = jnp.zeros((rows, LANE), jnp.float32)
     into = [nothing] + current_a + [nothing]
     rhs_b = [None] * count
     for k in range(count):
@@ -396,7 +461,6 @@
 
 
 def final_kernel(
-    block,
     tab_ref,
     stratum_ref,
     conc_ref,
@@ -414,17 +478,10 @@
     gather_b,
 ):
     n, planes_y, planes_z = stratum_ref.shape
-    peers = current_ref.shape[0]
-    rows, width = block
     number = Numbers(tab_ref)
-    across = planes_z // width
 
     def plane(q):
-        lines = []
-        for p in range(0, peers, across):
-            pieces = [current_ref[p + j, q * rows : (q + 1) * rows, :] for j in range(across)]
-            lines.append(jnp.concatenate(pieces, axis=1) if across > 1 else pieces[0])
-        return jnp.concatenate(lines, axis=0)
+        return jnp.concatenate([current_ref[0, q], current_ref[1, q]], axis=0)
 
     line = lax.broadcasted_iota(jnp.int32, (planes_y, planes_z), 0)
     first_line, last_line = line == 0, line == planes_y - 1
@@ -490,8 +547,12 @@
 ):
     n, planes_y, planes_z = stratum.shape
     peers = lax.axis_size("flow")
-    block = chunk_of(peers, planes_y, planes_z)
-    rows, width = block
+    others = peers // 2
+    half = planes_y // 2
+    block = chunk_of(others, half, planes_z)
+    rows = chunk_rows(block)
+    pairs = [[2 * m, 2 * m + 1] for m in range(others)]
+    sides = [[2 * m + r for m in range(others)] for r in range(2)]
     cells = (n, planes_y, planes_z)
 
     halo = (3, n, planes_z)
@@ -537,23 +598,30 @@
     next_lo = lax.ppermute(own_hi, "trans", up)
     next_hi = lax.ppermute(own_lo, "trans", down)
 
-    pay_shape = (peers, QUANTITIES * rows, width)
+    pay_shape = (2, QUANTITIES, half, planes_z)
     pay, edge, pass_a, drop_a, pass_b, drop_b, over, source_a, source_b = call(
-        functools.partial(local_kernel, block),
+        local_kernel,
         [pay_shape, (2, 6, n, planes_z), cells, cells, cells, cells, (2, planes_y, planes_z), cells, cells],
         [cells] * 9,
     )(table, stratum, concentration)
-    pay, flow = call(
-        functools.partial(border_kernel, block), [pay_shape, (2, 2, n, planes_z)]
-    )(table, own_lo, own_hi, next_lo, next_hi, edge, pay)
-    gathered = lax.all_to_all(pay, "flow", 0, 0, tiled=True)
+    pay, flow = call(border_kernel, [pay_shape, (2, 2, n, planes_z)])(
+        table, own_lo, own_hi, next_lo, next_hi, edge, pay
+    )
+    pay = lax.all_to_all(pay, "flow", 0, 0, axis_index_groups=pairs, tiled=True)
+    pay, keep = call(
+        functools.partial(merge_kernel, block),
+        [(others, QUANTITIES * rows, LANE), (8, half, planes_z)],
+    )(pay)
+    pay = lax.all_to_all(pay, "flow", 0, 0, axis_index_groups=sides, tiled=True)
     (currents,) = call(
-        functools.partial(chain_kernel, block), [(peers, CURRENTS * rows, width)]
-    )(gathered)
-    currents = lax.all_to_all(currents, "flow", 0, 0, tiled=True)
-    (out,) = call(
-        functools.partial(final_kernel, block), [(4,) + cells], [cells] * 2
-    )(
+        functools.partial(chain_kernel, block), [(others, CURRENTS * rows, LANE)]
+    )(pay)
+    currents = lax.all_to_all(currents, "flow", 0, 0, axis_index_groups=sides, tiled=True)
+    (currents,) = call(
+        functools.partial(split_kernel, block), [(2, CURRENTS, half, planes_z)]
+    )(currents, keep)
+    currents = lax.all_to_all(currents, "flow", 0, 0, axis_index_groups=pairs, tiled=True)
+    (out,) = call(final_kernel, [(4,) + cells], [cells] * 2)(
         table,
         stratum,
         concentration,

time: 39.8 us -> 47.7 us (1.20)
  blocking collectives: 27.6 us -> 35.5 us
    all_to_all x2 -> x4, blocking collectives: 27.6 us -> 35.5 us  [the longest x1 10.6 us: per_device(): pay = lax.all_to_all(pay, 'flow', 0, 0, axis_index_groups=sides, tiled=True)]
    pallas_call x4 -> x6, Pallas kernels: 6.18 us -> 6.07 us  [the longest x1 3.7 us: per_device(): call(local_kernel, [pay_shape, (2, 6, n, planes_z), cells, cells, cells,...]
  transfers between devices with their start and end apart: 2 -> 2, of which waited for: 0 -> 0; matrix products, arithmetic and copies ran while one was open for 0% -> 0% of each run, Pallas kernels for 9% -> 8%
where the time goes in v3:
time: 47.7 us; the launch traced here: 47.3 us
  blocking collectives  35.5 us (74%)
  Pallas kernels  7.5 us (16%)
  starting transfers between devices  4.32 us (9%)
    all_to_all x1, blocking collectives, per_device(): pay = lax.all_to_all(pay, 'flow', 0, 0, axis_index_groups=sides, tiled=True)  10.6 us
    all_to_all x1, blocking collectives, per_device(): pay = lax.all_to_all(pay, 'flow', 0, 0, axis_index_groups=pairs, tiled=True)  10.2 us
    all_to_all x1, blocking collectives, per_device(): lax.all_to_all(currents, 'flow', 0, 0, axis_index_groups=sides, tiled=True)  8.2 us
    all_to_all x1, blocking collectives, per_device(): lax.all_to_all(currents, 'flow', 0, 0, axis_index_groups=pairs, tiled=True)  6.5 us
    pallas_call x1, Pallas kernels, per_device(): call(local_kernel, [pay_shape, (2, 6, n, planes_z), cells, cells, cells,...  3.7 us
    ppermute x1, starting transfers between devices, per_device(): next_lo = lax.ppermute(own_hi, 'trans', up)  3.03 us
    pallas_call x1, Pallas kernels, per_device(): call(final_kernel, [(4,) + cells], [cells] * 2)  2.14 us
    pallas_call x1, Pallas kernels, per_device(): pl.pallas_call(pack_kernel, out_shape=[jax.ShapeDtypeStruct(halo, jnp.flo...  1.43 us
  transfers between devices with their start and end apart: 2, of which 0 were waited for; matrix products, arithmetic and copies ran while one was open for 0% of the time, Pallas kernels for 8%

profile of v3, /device:TPU:0, one launch (start us, length us, event | category | flops | bytes accessed | tf_op | source)
XLA Modules:
  0.0 47.3 jit_solution(12720775725979141258)
XLA Ops:
  0.0 1.4 %shard_map.73 = (f32[3,16,256]{2,1,0:T(8,128)S(1)}, f32[3,16,256]{2,1,0:T(8,128)S(1)}, f32[16,128]{1,0:T(8,128)S(1)}, f32[4,16,16,256]{3,2,1,0:T(8,128)S(1)}, s32[16,16,256]{2,1,0:T(8,128)S(1)}) custom-call(f32[4,16,16,256]{3,2,1,0:T(8,128)} %conc_hbm.1, s32[16,16,256]{2,1,0:T(8,128)} %stratum_hbm.1, f32[1,16]{1,0:T(1,128)} %bitcast.6, f32[2,16]{1,0:T(2,128)} %bitcast.5, ...), custom_call_target="tpu_custom_call" | custom-call | tf_op jit(solution)/shard_map/pallas_call | solution.py:561
  1.4 1.3 %collective-permute-start.1 = (f32[3,16,256]{2,1,0:T(8,128)S(1)}, f32[3,16,256]{2,1,0:T(8,128)S(1)}, u32[]{:S(2)}, u32[]{:S(2)}) collective-permute-start(f32[3,16,256]{2,1,0:T(8,128)S(1)} %get-tuple-element.33.own_lo_ref), channel_id=1, source_target_pairs={{1,0},{2,1},{3,2},{5,4},{6,5},{7,6},{9,8},{10,9},{11,10},{13,12},{... | collective-permute-start | bytes 147464 | tf_op jit(solution)/shard_map/ppermute | solution.py:599
  2.7 3.0 %collective-permute-start = (f32[3,16,256]{2,1,0:T(8,128)S(1)}, f32[3,16,256]{2,1,0:T(8,128)S(1)}, u32[]{:S(2)}, u32[]{:S(2)}) collective-permute-start(f32[3,16,256]{2,1,0:T(8,128)S(1)} %get-tuple-element.34.own_hi_ref), channel_id=1, source_target_pairs={{0,1},{1,2},{2,3},{4,5},{5,6},{6,7},{8,9},{9,10},{10,11},{12,13},{... | collective-permute-start | bytes 147464 | tf_op jit(solution)/shard_map/ppermute | solution.py:598
  5.8 3.7 %shard_map.74 = (f32[2,14,8,256]{3,2,1,0:T(8,128)S(1)}, f32[2,6,16,256]{3,2,1,0:T(8,128)S(1)}, f32[16,16,256]{2,1,0:T(8,128)S(1)}, f32[16,16,256]{2,1,0:T(8,128)...) custom-call(f32[16,128]{1,0:T(8,128)S(1)} %get-tuple-element.23.tab_, ...), custom_call_target="tpu_custom_call" | custom-call | tf_op jit(solution)/shard_map/pallas_call | solution.py:602
  9.5 0.0 collective-permute-done.1.next_hi_ref
  9.5 0.0 collective-permute-done.next_lo_ref
  9.5 0.1 shard_map.75
  9.7 10.2 %all_to_all.20.pay_ref = f32[2,14,8,256]{3,2,1,0:T(8,128)S(1)} all-to-all(f32[2,14,8,256]{3,2,1,0:T(8,128)S(1)} %get-tuple-element.38), channel_id=1, replica_groups={{0,4},{8,12},{16,20},{24,28},{1,5},{9,13},{17,21},{25,29},{2,6},{10,14}..., dimensions={0} | all-to-all | bytes 458752 | tf_op jit(solution)/shard_map/all_to_all | solution.py:610
  19.9 10.6 %all_to_all.21.pay_ref = f32[4,56,128]{2,1,0:T(8,128)S(1)} all-to-all(f32[4,56,128]{2,1,0:T(8,128)S(1)} %get-tuple-element.39), channel_id=1, replica_groups={{0,8,16,24},{4,12,20,28},{1,9,17,25},{5,13,21,29},{2,10,18,26},{6,14,22..., dimensions={0} | all-to-all | bytes 229376 | tf_op jit(solution)/shard_map/all_to_all | solution.py:615
  30.5 8.2 %all_to_all.22.current_ref = f32[4,16,128]{2,1,0:T(8,128)S(1)} all-to-all(f32[4,16,128]{2,1,0:T(8,128)S(1)} %shard_map.77), channel_id=1, replica_groups={{0,8,16,24},{4,12,20,28},{1,9,17,25},{5,13,21,29},{2,10,18,26},{6,14,22..., dimensions={0} | all-to-all | bytes 65536 | tf_op jit(solution)/shard_map/all_to_all | solution.py:619
  38.7 6.5 %all_to_all.23.current_ref = f32[2,4,8,256]{3,2,1,0:T(8,128)S(1)} all-to-all(f32[2,4,8,256]{3,2,1,0:T(8,128)S(1)} %shard_map.78), channel_id=1, replica_groups={{0,4},{8,12},{16,20},{24,28},{1,5},{9,13},{17,21},{25,29},{2,6},{10,14}..., dimensions={0} | all-to-all | bytes 131072 | tf_op jit(solution)/shard_map/all_to_all | solution.py:623
  45.2 2.1 %shard_map.79 = f32[4,16,16,256]{3,2,1,0:T(8,128)} custom-call(f32[16,128]{1,0:T(8,128)S(1)} %get-tuple-element.23.tab_ref, s32[16,16,256]{2,1,0:T(8,128)S(1)} %get-tuple-element.24.stratum_ref, f32[4,16,16,256]{3,2,1,0:T(8,128)S(1)} %get-tuple-element.25.conc_ref, f32[16,16,256]{2,1,0:T(8,128)S(1)} %get-tuple-element.26.pass_a_ref, ...), custom_call_target="tpu_custom_call" | custom-call | tf_op jit(solution)/shard_map/pallas_call | solution.py:624
  (3 shorter events, 0.1 us)
Async XLA Ops:
  1.4 8.1 %collective-permute-start.1 = (f32[3,16,256]{2,1,0:T(8,128)S(1)}, f32[3,16,256]{2,1,0:T(8,128)S(1)}, u32[]{:S(2)}, u32[]{:S(2)}) collective-permute-start(f32[3,16,256]{2,1,0:T(8,128)S(1)} %get-tuple-element.33.own_lo_ref), channel_id=1, source_target_pairs={{1,0},{2,1},{3,2},{5,4},{6,5},{7,6},{9,8},{10,9},{11,10},{13,12},{... | collective-permute-start | bytes 147464 | tf_op jit(solution)/shard_map/ppermute | solution.py:599
  2.7 6.8 %collective-permute-start = (f32[3,16,256]{2,1,0:T(8,128)S(1)}, f32[3,16,256]{2,1,0:T(8,128)S(1)}, u32[]{:S(2)}, u32[]{:S(2)}) collective-permute-start(f32[3,16,256]{2,1,0:T(8,128)S(1)} %get-tuple-element.34.own_hi_ref), channel_id=1, source_target_pairs={{0,1},{1,2},{2,3},{4,5},{5,6},{6,7},{8,9},{9,10},{10,11},{12,13},{... | collective-permute-start | bytes 147464 | tf_op jit(solution)/shard_map/ppermute | solution.py:598

commit v4 on v3

--- a/solution.py
+++ b/solution.py
@@ -84,44 +84,6 @@
         k = NUMBERS.index(name)
         row = jnp.broadcast_to(self.tab_ref[k : k + 1, :], (SUB, LANE))
         return lookup(row, index)
-
-
-def chunk_of(peers, planes_y, planes_z):
-    if peers <= planes_y:
-        return planes_y // peers, planes_z
-    return 1, planes_y * planes_z // peers
-
-
-def chunk_rows(block):
-    return block[0] * block[1] // LANE
-
-
-def store_chunks(ref, q, value, block):
-    rows, width = block
-    across = value.shape[1] // width
-    base = q * chunk_rows(block)
-    for p in range(ref.shape[0]):
-        y, z = (p // across) * rows, (p % across) * width
-        for k in range(width // LANE):
-            low = z + k * LANE
-            ref[p, base + k * rows : base + (k + 1) * rows, :] = value[
-                y : y + rows, low : low + LANE
-            ]
-
-
-def load_chunks(ref, q, block, planes_z):
-    rows, width = block
-    across = planes_z // width
-    base = q * chunk_rows(block)
-    lines = []
-    for p in range(0, ref.shape[0], across):
-        pieces = [
-            ref[p + j, base + k * rows : base + (k + 1) * rows, :]
-            for j in range(across)
-            for k in range(width // LANE)
-        ]
-        lines.append(jnp.concatenate(pieces, axis=1))
-    return jnp.concatenate(lines, axis=0)
 
 
 def shifted_difference(value, axis):
@@ -307,13 +269,15 @@
         *couple,
         *free,
     ]
-    half = planes_y // 2
     for q, value in enumerate(quantities):
-        pay_ref[0, q] = value[:half]
-        pay_ref[1, q] = value[half:]
+        pay_ref[q] = value
     for k, ref in enumerate((left_a, right_a, left_b, right_b, adj_l, adj_r)):
         edge_ref[0, k] = ref[:, 0, :]
         edge_ref[1, k] = ref[:, planes_y - 1, :]
+
+
+def side_of(axis, stride):
+    return (lax.axis_index(axis) // stride) % 2 == 1
 
 
 def border_kernel(
@@ -324,19 +288,24 @@
     next_hi_ref,
     edge_ref,
     pay_ref,
-    out_ref,
+    keep_ref,
+    send_ref,
     flow_ref,
 ):
     number = Numbers(tab_ref)
-    out_ref[...] = pay_ref[...]
+    half = pay_ref.shape[1] // 2
+    second = side_of("flow", 1)
+    low, high = pay_ref[:, :half], pay_ref[:, half:]
+    keep_ref[...] = jnp.where(second, high, low)
+    send_ref[...] = jnp.where(second, low, high)
     for side, (own_ref, next_ref) in enumerate(
         ((own_lo_ref, next_lo_ref), (own_hi_ref, next_hi_ref))
     ):
         own_id = own_ref[2].astype(jnp.int32) - 1
         next_id = next_ref[2].astype(jnp.int32) - 1
         present = next_id >= 0
-        half = number("half_t", own_id) + number("half_t", jnp.maximum(next_id, 0))
-        face = jnp.where(present, recip(half), 0.0)
+        resist = number("half_t", own_id) + number("half_t", jnp.maximum(next_id, 0))
+        face = jnp.where(present, recip(resist), 0.0)
         flow_a = face * (next_ref[0] - own_ref[0])
         flow_b = face * (next_ref[1] - own_ref[1])
         flow_ref[side, 0], flow_ref[side, 1] = flow_a, flow_b
@@ -347,15 +316,20 @@
             FB_L: l_b * flow_b + w_l * flow_a,
             FB_R: r_b * flow_b + w_r * flow_a,
         }
-        row = 0 if side == 0 else pay_ref.shape[2] - 1
+        row = 0 if side == 0 else half - 1
+        kept = second if side == 1 else jnp.logical_not(second)
         for q, change in changes.items():
             total = jnp.sum(change, axis=0, keepdims=True)
-            out_ref[side, q, row : row + 1, :] = pay_ref[side, q, row : row + 1, :] + total
-
-
-def merge_kernel(block, pay_ref, out_ref, keep_ref):
-    one = [pay_ref[0, q] for q in range(QUANTITIES)]
-    two = [pay_ref[1, q] for q in range(QUANTITIES)]
+            keep_ref[q, row : row + 1, :] += jnp.where(kept, total, 0.0)
+            send_ref[q, row : row + 1, :] += jnp.where(kept, 0.0, total)
+
+
+FACE_L = (ZA_LL, ZB_LL, C_LL, FA_L, FB_L)
+FACE_R = (ZA_RR, ZB_RR, C_RR, FA_R, FB_R)
+KEPT = 8
+
+
+def merge(one, two):
     over_a = recip(one[ZA_RR] + two[ZA_LL])
     over_b = recip(one[ZB_RR] + two[ZB_LL])
     across = one[C_RR] + two[C_LL]
@@ -381,83 +355,66 @@
         FB_L: one[FB_L] - one[ZB_LR] * free_b - one[C_LR] * free_a,
         FB_R: two[FB_R] + two[ZB_LR] * free_b + two[C_RL] * free_a,
     }
-    for q, value in merged.items():
-        store_chunks(out_ref, q, value, block)
-    for k, value in enumerate(
-        (free_a, from_l, from_r, free_b, from_l_b, from_r_b, cross_l, cross_r)
-    ):
-        keep_ref[k] = value
-
-
-def split_kernel(block, current_ref, keep_ref, out_ref):
-    planes_z = keep_ref.shape[2]
-    l_a, r_a, l_b, r_b = [load_chunks(current_ref, q, block, planes_z) for q in range(CURRENTS)]
-    free_a, from_l, from_r, free_b, from_l_b, from_r_b, cross_l, cross_r = [
-        keep_ref[k] for k in range(8)
-    ]
+    return merged, (free_a, from_l, from_r, free_b, from_l_b, from_r_b, cross_l, cross_r)
+
+
+def between(kept, ends):
+    free_a, from_l, from_r, free_b, from_l_b, from_r_b, cross_l, cross_r = kept
+    l_a, r_a, l_b, r_b = ends
     middle_a = free_a + from_l * l_a - from_r * r_a
     middle_b = free_b + from_l_b * l_b - from_r_b * r_b + cross_l * l_a - cross_r * r_a
-    for q, value in enumerate((l_a, -middle_a, l_b, -middle_b)):
-        out_ref[0, q] = value
-    for q, value in enumerate((middle_a, r_a, middle_b, r_b)):
-        out_ref[1, q] = value
-
-
-def chain_kernel(block, pay_ref, out_ref):
-    peers = pay_ref.shape[0]
-    rows = chunk_rows(block)
-
-    def take(segment, q):
-        return pay_ref[segment, q * rows : (q + 1) * rows, :]
-
-    count = peers - 1
-    pass_a, over_a, rhs_a = [None] * count, [None] * count, [None] * count
-    pass_b, over_b = [None] * count, [None] * count
-    for k in range(count):
-        diag_a = take(k, ZA_RR) + take(k + 1, ZA_LL)
-        diag_b = take(k, ZB_RR) + take(k + 1, ZB_LL)
-        rhs = take(k, FA_R) - take(k + 1, FA_L)
-        if k > 0:
-            off_a, off_b = take(k, ZA_LR), take(k, ZB_LR)
-            ratio_a = off_a * over_a[k - 1]
-            pass_a[k - 1] = ratio_a
-            diag_a = diag_a - off_a * ratio_a
-            rhs = rhs + ratio_a * rhs_a[k - 1]
-            ratio_b = off_b * over_b[k - 1]
-            pass_b[k - 1] = ratio_b
-            diag_b = diag_b - off_b * ratio_b
-        over_a[k], over_b[k], rhs_a[k] = recip(diag_a), recip(diag_b), rhs
-    current_a = [None] * count
-    for k in reversed(range(count)):
-        value = rhs_a[k] * over_a[k]
-        if k < count - 1:
-            value = value + pass_a[k] * current_a[k + 1]
-        current_a[k] = value
-    nothing = jnp.zeros((rows, LANE), jnp.float32)
-    into = [nothing] + current_a + [nothing]
-    rhs_b = [None] * count
-    for k in range(count):
-        rhs = (
-            take(k, FB_R)
-            - take(k + 1, FB_L)
-            + take(k, C_RL) * into[k]
-            - (take(k, C_RR) + take(k + 1, C_LL)) * into[k + 1]
-            + take(k + 1, C_LR) * into[k + 2]
+    return middle_a, middle_b
+
+
+def merge_kernel(stride, last, own_ref, other_ref, out_ref, kept_ref, *face_ref):
+    second = side_of("flow", stride)
+    own = [own_ref[q] for q in range(QUANTITIES)]
+    other = [other_ref[q] for q in range(QUANTITIES)]
+    one = [jnp.where(second, b, a) for a, b in zip(own, other)]
+    two = [jnp.where(second, a, b) for a, b in zip(own, other)]
+    merged, kept = merge(one, two)
+    for q, value in merged.items():
+        out_ref[q] = value
+    for k, value in enumerate(kept):
+        kept_ref[k] = value
+    if last:
+        after = side_of("flow", 2 * stride)
+        for k, (l, r) in enumerate(zip(FACE_L, FACE_R)):
+            face_ref[0][k] = jnp.where(after, merged[l], merged[r])
+
+
+def close_kernel(strides, own_ref, other_ref, *refs):
+    kept_refs, mine_ref, send_ref = refs[:-2], refs[-2], refs[-1]
+    stride = strides[-1]
+    second = side_of("flow", stride)
+    own = [jnp.where(second, own_ref[l], own_ref[r]) for l, r in zip(FACE_L, FACE_R)]
+    z_a, z_b, couple, f_a, f_b = [own[k] + other_ref[k] for k in range(3)] + [
+        jnp.where(second, other_ref[k] - own[k], own[k] - other_ref[k]) for k in (3, 4)
+    ]
+    current_a = recip(z_a) * f_a
+    current_b = recip(z_b) * (f_b - couple * current_a)
+    nothing = jnp.zeros_like(current_a)
+
+    def side_ends(after, middle_a, middle_b, ends):
+        l_a, r_a, l_b, r_b = ends
+        return (
+            jnp.where(after, middle_a, l_a),
+            jnp.where(after, r_a, -middle_a),
+            jnp.where(after, middle_b, l_b),
+            jnp.where(after, r_b, -middle_b),
         )
-        if k > 0:
-            rhs = rhs + pass_b[k - 1] * rhs_b[k - 1]
-        rhs_b[k] = rhs
-    current_b = [None] * count
-    for k in reversed(range(count)):
-        value = rhs_b[k] * over_b[k]
-        if k < count - 1:
-            value = value + pass_b[k] * current_b[k + 1]
-        current_b[k] = value
-    into_b = [nothing] + current_b + [nothing]
-    for k in range(peers):
-        values = (into[k], -into[k + 1], into_b[k], -into_b[k + 1])
-        for q, value in enumerate(values):
-            out_ref[k, q * rows : (q + 1) * rows, :] = value
+
+    ends = side_ends(second, current_a, current_b, (nothing,) * 4)
+    for stride, kept_ref in reversed(list(zip(strides[:-1], kept_refs))):
+        middle_a, middle_b = between([kept_ref[k] for k in range(KEPT)], ends)
+        after = side_of("flow", stride)
+        if stride == 1:
+            other_ends = side_ends(jnp.logical_not(after), middle_a, middle_b, ends)
+            for q, value in enumerate(other_ends):
+                send_ref[q] = value
+        ends = side_ends(after, middle_a, middle_b, ends)
+    for q, value in enumerate(ends):
+        mine_ref[q] = value
 
 
 def final_kernel(
@@ -472,6 +429,7 @@
     source_a_ref,
     source_b_ref,
     flow_ref,
+    mine_ref,
     current_ref,
     out_ref,
     gather_a,
@@ -480,8 +438,12 @@
     n, planes_y, planes_z = stratum_ref.shape
     number = Numbers(tab_ref)
 
+    second = side_of("flow", 1)
+
     def plane(q):
-        return jnp.concatenate([current_ref[0, q], current_ref[1, q]], axis=0)
+        mine, other = mine_ref[q], current_ref[q]
+        halves = [jnp.where(second, other, mine), jnp.where(second, mine, other)]
+        return jnp.concatenate(halves, axis=0)
 
     line = lax.broadcasted_iota(jnp.int32, (planes_y, planes_z), 0)
     first_line, last_line = line == 0, line == planes_y - 1
@@ -547,12 +509,8 @@
 ):
     n, planes_y, planes_z = stratum.shape
     peers = lax.axis_size("flow")
-    others = peers // 2
     half = planes_y // 2
-    block = chunk_of(others, half, planes_z)
-    rows = chunk_rows(block)
-    pairs = [[2 * m, 2 * m + 1] for m in range(others)]
-    sides = [[2 * m + r for m in range(others)] for r in range(2)]
+    strides = [1 << k for k in range(peers.bit_length() - 1)]
     cells = (n, planes_y, planes_z)
 
     halo = (3, n, planes_z)
@@ -598,29 +556,39 @@
     next_lo = lax.ppermute(own_hi, "trans", up)
     next_hi = lax.ppermute(own_lo, "trans", down)
 
-    pay_shape = (2, QUANTITIES, half, planes_z)
+    def exchange(value, stride):
+        return lax.ppermute(value, "flow", [(i, i ^ stride) for i in range(peers)])
+
     pay, edge, pass_a, drop_a, pass_b, drop_b, over, source_a, source_b = call(
         local_kernel,
-        [pay_shape, (2, 6, n, planes_z), cells, cells, cells, cells, (2, planes_y, planes_z), cells, cells],
+        [
+            (QUANTITIES, planes_y, planes_z),
+            (2, 6, n, planes_z),
+            *[cells] * 4,
+            (2, planes_y, planes_z),
+            *[cells] * 2,
+        ],
         [cells] * 9,
     )(table, stratum, concentration)
-    pay, flow = call(border_kernel, [pay_shape, (2, 2, n, planes_z)])(
+    block_shape = (QUANTITIES, half, planes_z)
+    block, send, flow = call(border_kernel, [block_shape, block_shape, (2, 2, n, planes_z)])(
         table, own_lo, own_hi, next_lo, next_hi, edge, pay
     )
-    pay = lax.all_to_all(pay, "flow", 0, 0, axis_index_groups=pairs, tiled=True)
-    pay, keep = call(
-        functools.partial(merge_kernel, block),
-        [(others, QUANTITIES * rows, LANE), (8, half, planes_z)],
-    )(pay)
-    pay = lax.all_to_all(pay, "flow", 0, 0, axis_index_groups=sides, tiled=True)
-    (currents,) = call(
-        functools.partial(chain_kernel, block), [(others, CURRENTS * rows, LANE)]
-    )(pay)
-    currents = lax.all_to_all(currents, "flow", 0, 0, axis_index_groups=sides, tiled=True)
-    (currents,) = call(
-        functools.partial(split_kernel, block), [(2, CURRENTS, half, planes_z)]
-    )(currents, keep)
-    currents = lax.all_to_all(currents, "flow", 0, 0, axis_index_groups=pairs, tiled=True)
+    kept = []
+    for stride in strides[:-1]:
+        other = exchange(send, stride)
+        last = stride == strides[-2]
+        block, keep, *face = call(
+            functools.partial(merge_kernel, stride, last),
+            [block_shape, (KEPT, half, planes_z)] + [(5, half, planes_z)] * last,
+        )(block, other)
+        kept.append(keep)
+        send = face[0] if last else block
+    ends_shape = (CURRENTS, half, planes_z)
+    mine, send = call(functools.partial(close_kernel, strides), [ends_shape, ends_shape])(
+        block, exchange(send, strides[-1]), *kept
+    )
+    currents = exchange(send, 1)
     (out,) = call(final_kernel, [(4,) + cells], [cells] * 2)(
         table,
         stratum,
@@ -633,6 +601,7 @@
         source_a,
         source_b,
         flow,
+        mine,
         currents,
     )
     return out

time: 47.7 us -> 33.5 us (0.70)
  blocking collectives: 35.5 us -> 0 us
  waiting for transfers between devices: 0.01 us -> 11.2 us
  starting transfers between devices: 4.32 us -> 14.5 us
    all_to_all x4 -> x0, blocking collectives: 35.5 us -> none  [the longest x1 10.6 us: per_device(): pay = lax.all_to_all(pay, 'flow', 0, 0, axis_index_groups=sides, tiled=True)]
    ppermute x0 -> x4, waiting for transfers between devices: none -> 11.2 us  [exchange(): return lax.ppermute(value, 'flow', [(i, i ^ stride) for i in range(peers)])]
    ppermute x0 -> x4, starting transfers between devices: none -> 10.2 us  [exchange(): return lax.ppermute(value, 'flow', [(i, i ^ stride) for i in range(peers)])]
  transfers between devices with their start and end apart: 2 -> 6, of which waited for: 0 -> 4; matrix products, arithmetic and copies ran while one was open for 0% -> 0% of each run, Pallas kernels for 8% -> 11%
where the time goes in v4:
time: 33.5 us; the launch traced here: 33.4 us
  starting transfers between devices  14.5 us (43%)
  waiting for transfers between devices  11.2 us (33%)
  Pallas kernels  7.55 us (23%)
    ppermute x4, waiting for transfers between devices, exchange(): return lax.ppermute(value, 'flow', [(i, i ^ stride) for i in range(peers)])  11.2 us
    ppermute x4, starting transfers between devices, exchange(): return lax.ppermute(value, 'flow', [(i, i ^ stride) for i in range(peers)])  10.2 us
    pallas_call x1, Pallas kernels, per_device(): call(local_kernel, [(QUANTITIES, planes_y, planes_z), (2, 6, n, planes_z)...  3.7 us
    ppermute x1, starting transfers between devices, per_device(): next_lo = lax.ppermute(own_hi, 'trans', up)  3.03 us
    pallas_call x1, Pallas kernels, per_device(): call(final_kernel, [(4,) + cells], [cells] * 2)  2.14 us
    pallas_call x1, Pallas kernels, per_device(): pl.pallas_call(pack_kernel, out_shape=[jax.ShapeDtypeStruct(halo, jnp.flo...  1.43 us
    ppermute x1, starting transfers between devices, per_device(): next_hi = lax.ppermute(own_lo, 'trans', down)  1.29 us
  transfers between devices with their start and end apart: 6, of which 4 were waited for; matrix products, arithmetic and copies ran while one was open for 0% of the time, Pallas kernels for 11%

profile of v4, /device:TPU:0, one launch (start us, length us, event | category | flops | bytes accessed | tf_op | source)
XLA Modules:
  0.0 33.4 jit_solution(1746889290892800005)
XLA Ops:
  0.0 1.4 %shard_map.73 = (f32[3,16,256]{2,1,0:T(8,128)S(1)}, f32[3,16,256]{2,1,0:T(8,128)S(1)}, f32[16,128]{1,0:T(8,128)S(1)}, f32[4,16,16,256]{3,2,1,0:T(8,128)S(1)}, s32[16,16,256]{2,1,0:T(8,128)S(1)}) custom-call(f32[4,16,16,256]{3,2,1,0:T(8,128)} %conc_hbm.1, s32[16,16,256]{2,1,0:T(8,128)} %stratum_hbm.1, f32[1,16]{1,0:T(1,128)} %bitcast.6, f32[2,16]{1,0:T(2,128)} %bitcast.5, ...), custom_call_target="tpu_custom_call" | custom-call | tf_op jit(solution)/shard_map/pallas_call | solution.py:519
  1.4 1.3 %collective-permute-start.1 = (f32[3,16,256]{2,1,0:T(8,128)S(1)}, f32[3,16,256]{2,1,0:T(8,128)S(1)}, u32[]{:S(2)}, u32[]{:S(2)}) collective-permute-start(f32[3,16,256]{2,1,0:T(8,128)S(1)} %get-tuple-element.39.own_lo_ref), channel_id=1, source_target_pairs={{1,0},{2,1},{3,2},{5,4},{6,5},{7,6},{9,8},{10,9},{11,10},{13,12},{... | collective-permute-start | bytes 147464 | tf_op jit(solution)/shard_map/ppermute | solution.py:557
  2.7 3.0 %collective-permute-start = (f32[3,16,256]{2,1,0:T(8,128)S(1)}, f32[3,16,256]{2,1,0:T(8,128)S(1)}, u32[]{:S(2)}, u32[]{:S(2)}) collective-permute-start(f32[3,16,256]{2,1,0:T(8,128)S(1)} %get-tuple-element.40.own_hi_ref), channel_id=1, source_target_pairs={{0,1},{1,2},{2,3},{4,5},{5,6},{6,7},{8,9},{9,10},{10,11},{12,13},{... | collective-permute-start | bytes 147464 | tf_op jit(solution)/shard_map/ppermute | solution.py:556
  5.8 3.7 %shard_map.74 = (f32[14,16,256]{2,1,0:T(8,128)S(1)}, f32[2,6,16,256]{3,2,1,0:T(8,128)S(1)}, f32[16,16,256]{2,1,0:T(8,128)S(1)}, f32[16,16,256]{2,1,0:T(8,128)S(1...) custom-call(f32[16,128]{1,0:T(8,128)S(1)} %get-tuple-element.29.tab_, ...), custom_call_target="tpu_custom_call" | custom-call | tf_op jit(solution)/shard_map/pallas_call | solution.py:562
  9.5 0.0 collective-permute-done.1.next_hi_ref
  9.5 0.0 collective-permute-done.next_lo_ref
  9.5 0.1 shard_map.75
  9.7 3.0 %collective-permute-start.2 = (f32[14,8,256]{2,1,0:T(8,128)S(1)}, f32[14,8,256]{2,1,0:T(8,128)S(1)}, u32[]{:S(2)}, u32[]{:S(2)}) collective-permute-start(f32[14,8,256]{2,1,0:T(8,128)S(1)} %get-tuple-element.45), channel_id=1, source_target_pairs={{0,4},{4,0},{8,12},{12,8},{16,20},{20,16},{24,28},{28,24},{1,5},{5... | collective-permute-start | bytes 344072 | tf_op jit(solution)/shard_map/ppermute | solution.py:560
  12.7 3.4 %collective-permute-done.2.other_ref = f32[14,8,256]{2,1,0:T(8,128)S(1)} collective-permute-done((f32[14,8,256]{2,1,0:T(8,128)S(1)}, f32[14,8,256]{2,1,0:T(8,128)S(1)}, u32[]{:S(2)}, u32[]{:S(2)}) %collective-permute-start.2) | collective-permute-done | bytes 114720 | tf_op jit(solution)/shard_map/ppermute | solution.py:560
  16.2 2.6 %collective-permute-start.3 = (f32[14,8,256]{2,1,0:T(8,128)S(1)}, f32[14,8,256]{2,1,0:T(8,128)S(1)}, u32[]{:S(2)}, u32[]{:S(2)}) collective-permute-start(f32[14,8,256]{2,1,0:T(8,128)S(1)} %get-tuple-element.46.own_ref), channel_id=1, source_target_pairs={{0,8},{4,12},{8,0},{12,4},{16,24},{20,28},{24,16},{28,20},{1,9},{5... | collective-permute-start | bytes 344072 | tf_op jit(solution)/shard_map/ppermute | solution.py:560
  18.7 3.4 %collective-permute-done.3.other_ref = f32[14,8,256]{2,1,0:T(8,128)S(1)} collective-permute-done((f32[14,8,256]{2,1,0:T(8,128)S(1)}, f32[14,8,256]{2,1,0:T(8,128)S(1)}, u32[]{:S(2)}, u32[]{:S(2)}) %collective-permute-start.3) | collective-permute-done | bytes 114720 | tf_op jit(solution)/shard_map/ppermute | solution.py:560
  22.2 2.8 %collective-permute-start.4 = (f32[5,8,256]{2,1,0:T(8,128)S(1)}, f32[5,8,256]{2,1,0:T(8,128)S(1)}, u32[]{:S(2)}, u32[]{:S(2)}) collective-permute-start(f32[5,8,256]{2,1,0:T(8,128)S(1)} %get-tuple-element.48), channel_id=1, source_target_pairs={{0,16},{4,20},{8,24},{12,28},{16,0},{20,4},{24,8},{28,12},{1,17},{... | collective-permute-start | bytes 122888 | tf_op jit(solution)/shard_map/ppermute | solution.py:560
  25.0 2.1 %collective-permute-done.4.other_ref = f32[5,8,256]{2,1,0:T(8,128)S(1)} collective-permute-done((f32[5,8,256]{2,1,0:T(8,128)S(1)}, f32[5,8,256]{2,1,0:T(8,128)S(1)}, u32[]{:S(2)}, u32[]{:S(2)}) %collective-permute-start.4) | collective-permute-done | bytes 40992 | tf_op jit(solution)/shard_map/ppermute | solution.py:560
  27.2 1.7 %collective-permute-start.5 = (f32[4,8,256]{2,1,0:T(8,128)S(1)}, f32[4,8,256]{2,1,0:T(8,128)S(1)}, u32[]{:S(2)}, u32[]{:S(2)}) collective-permute-start(f32[4,8,256]{2,1,0:T(8,128)S(1)} %get-tuple-element.52), channel_id=1, source_target_pairs={{0,4},{4,0},{8,12},{12,8},{16,20},{20,16},{24,28},{28,24},{1,5},{5... | collective-permute-start | bytes 98312 | tf_op jit(solution)/shard_map/ppermute | solution.py:560
  29.0 2.2 %collective-permute-done.5.current_ref = f32[4,8,256]{2,1,0:T(8,128)S(1)} collective-permute-done((f32[4,8,256]{2,1,0:T(8,128)S(1)}, f32[4,8,256]{2,1,0:T(8,128)S(1)}, u32[]{:S(2)}, u32[]{:S(2)}) %collective-permute-start.5) | collective-permute-done | bytes 32800 | tf_op jit(solution)/shard_map/ppermute | solution.py:560
  31.2 2.1 %shard_map.79 = f32[4,16,16,256]{3,2,1,0:T(8,128)} custom-call(f32[16,128]{1,0:T(8,128)S(1)} %get-tuple-element.29.tab_ref, s32[16,16,256]{2,1,0:T(8,128)S(1)} %get-tuple-element.30.stratum_ref, f32[4,16,16,256]{3,2,1,0:T(8,128)S(1)} %get-tuple-element.31.conc_ref, f32[16,16,256]{2,1,0:T(8,128)S(1)} %get-tuple-element.32.pass_a_ref, ...), custom_call_target="tpu_custom_call" | custom-call | tf_op jit(solution)/shard_map/pallas_call | solution.py:592
  (3 shorter events, 0.1 us)
Async XLA Ops:
  1.4 8.1 %collective-permute-start.1 = (f32[3,16,256]{2,1,0:T(8,128)S(1)}, f32[3,16,256]{2,1,0:T(8,128)S(1)}, u32[]{:S(2)}, u32[]{:S(2)}) collective-permute-start(f32[3,16,256]{2,1,0:T(8,128)S(1)} %get-tuple-element.39.own_lo_ref), channel_id=1, source_target_pairs={{1,0},{2,1},{3,2},{5,4},{6,5},{7,6},{9,8},{10,9},{11,10},{13,12},{... | collective-permute-start | bytes 147464 | tf_op jit(solution)/shard_map/ppermute | solution.py:557
  2.7 6.8 %collective-permute-start = (f32[3,16,256]{2,1,0:T(8,128)S(1)}, f32[3,16,256]{2,1,0:T(8,128)S(1)}, u32[]{:S(2)}, u32[]{:S(2)}) collective-permute-start(f32[3,16,256]{2,1,0:T(8,128)S(1)} %get-tuple-element.40.own_hi_ref), channel_id=1, source_target_pairs={{0,1},{1,2},{2,3},{4,5},{5,6},{6,7},{8,9},{9,10},{10,11},{12,13},{... | collective-permute-start | bytes 147464 | tf_op jit(solution)/shard_map/ppermute | solution.py:556
  9.7 6.4 %collective-permute-start.2 = (f32[14,8,256]{2,1,0:T(8,128)S(1)}, f32[14,8,256]{2,1,0:T(8,128)S(1)}, u32[]{:S(2)}, u32[]{:S(2)}) collective-permute-start(f32[14,8,256]{2,1,0:T(8,128)S(1)} %get-tuple-element.45), channel_id=1, source_target_pairs={{0,4},{4,0},{8,12},{12,8},{16,20},{20,16},{24,28},{28,24},{1,5},{5... | collective-permute-start | bytes 344072 | tf_op jit(solution)/shard_map/ppermute | solution.py:560
  16.2 6.0 %collective-permute-start.3 = (f32[14,8,256]{2,1,0:T(8,128)S(1)}, f32[14,8,256]{2,1,0:T(8,128)S(1)}, u32[]{:S(2)}, u32[]{:S(2)}) collective-permute-start(f32[14,8,256]{2,1,0:T(8,128)S(1)} %get-tuple-element.46.own_ref), channel_id=1, source_target_pairs={{0,8},{4,12},{8,0},{12,4},{16,24},{20,28},{24,16},{28,20},{1,9},{5... | collective-permute-start | bytes 344072 | tf_op jit(solution)/shard_map/ppermute | solution.py:560
  22.2 5.0 %collective-permute-start.4 = (f32[5,8,256]{2,1,0:T(8,128)S(1)}, f32[5,8,256]{2,1,0:T(8,128)S(1)}, u32[]{:S(2)}, u32[]{:S(2)}) collective-permute-start(f32[5,8,256]{2,1,0:T(8,128)S(1)} %get-tuple-element.48), channel_id=1, source_target_pairs={{0,16},{4,20},{8,24},{12,28},{16,0},{20,4},{24,8},{28,12},{1,17},{... | collective-permute-start | bytes 122888 | tf_op jit(solution)/shard_map/ppermute | solution.py:560
  27.2 4.0 %collective-permute-start.5 = (f32[4,8,256]{2,1,0:T(8,128)S(1)}, f32[4,8,256]{2,1,0:T(8,128)S(1)}, u32[]{:S(2)}, u32[]{:S(2)}) collective-permute-start(f32[4,8,256]{2,1,0:T(8,128)S(1)} %get-tuple-element.52), channel_id=1, source_target_pairs={{0,4},{4,0},{8,12},{12,8},{16,20},{20,16},{24,28},{28,24},{1,5},{5... | collective-permute-start | bytes 98312 | tf_op jit(solution)/shard_map/ppermute | solution.py:560

commit v5 on v4

--- a/solution.py
+++ b/solution.py
@@ -90,6 +90,10 @@
     return pltpu.roll(value, value.shape[axis] - 1, axis) - value
 
 
+def side_of(axis, stride):
+    return (lax.axis_index(axis) // stride) % 2 == 1
+
+
 def pack_kernel(
     conc_hbm,
     stratum_hbm,
@@ -98,8 +102,8 @@
     trans_hbm,
     exch_hbm,
     decay_hbm,
-    lo_ref,
-    hi_ref,
+    early_ref,
+    late_ref,
     tab_ref,
     conc_ref,
     stratum_ref,
@@ -137,14 +141,19 @@
     for k, name in enumerate(NUMBERS):
         tab_ref[k : k + 1, :] = made[name]
     tab_ref[len(NUMBERS) : 2 * SUB, :] = raw[0 : 2 * SUB - len(NUMBERS), :]
+    odd = side_of("trans", 1)
+    last = stratum_ref.shape[1] - 1
+
+    def put(k, low, high):
+        early_ref[k] = jnp.where(odd, low, high)
+        late_ref[k] = jnp.where(odd, high, low)
+
     copies[0].wait()
-    last = stratum_ref.shape[1] - 1
-    for ref, y in ((lo_ref, 0), (hi_ref, last)):
-        ref[2] = (stratum_ref[:, y, :] + 1).astype(jnp.float32)
+    numbered = [(stratum_ref[:, y, :] + 1).astype(jnp.float32) for y in (0, last)]
+    put(2, *numbered)
     copies[1].wait()
-    for ref, y in ((lo_ref, 0), (hi_ref, last)):
-        ref[0] = conc_ref[0, :, y, :]
-        ref[1] = conc_ref[1, :, y, :]
+    for k in (0, 1):
+        put(k, conc_ref[k, :, 0, :], conc_ref[k, :, last, :])
     copies[7].wait()
 
 
@@ -276,16 +285,12 @@
         edge_ref[1, k] = ref[:, planes_y - 1, :]
 
 
-def side_of(axis, stride):
-    return (lax.axis_index(axis) // stride) % 2 == 1
-
-
 def border_kernel(
     tab_ref,
-    own_lo_ref,
-    own_hi_ref,
-    next_lo_ref,
-    next_hi_ref,
+    early_ref,
+    late_ref,
+    beyond_early_ref,
+    beyond_late_ref,
     edge_ref,
     pay_ref,
     keep_ref,
@@ -298,16 +303,18 @@
     low, high = pay_ref[:, :half], pay_ref[:, half:]
     keep_ref[...] = jnp.where(second, high, low)
     send_ref[...] = jnp.where(second, low, high)
-    for side, (own_ref, next_ref) in enumerate(
-        ((own_lo_ref, next_lo_ref), (own_hi_ref, next_hi_ref))
-    ):
-        own_id = own_ref[2].astype(jnp.int32) - 1
-        next_id = next_ref[2].astype(jnp.int32) - 1
+    odd = side_of("trans", 1)
+    for side in range(2):
+        early = odd if side == 0 else jnp.logical_not(odd)
+        own = jnp.where(early, early_ref[...], late_ref[...])
+        beyond = jnp.where(early, beyond_early_ref[...], beyond_late_ref[...])
+        own_id = own[2].astype(jnp.int32) - 1
+        next_id = beyond[2].astype(jnp.int32) - 1
         present = next_id >= 0
         resist = number("half_t", own_id) + number("half_t", jnp.maximum(next_id, 0))
         face = jnp.where(present, recip(resist), 0.0)
-        flow_a = face * (next_ref[0] - own_ref[0])
-        flow_b = face * (next_ref[1] - own_ref[1])
+        flow_a = face * (beyond[0] - own[0])
+        flow_b = face * (beyond[1] - own[1])
         flow_ref[side, 0], flow_ref[side, 1] = flow_a, flow_b
         l_a, r_a, l_b, r_b, w_l, w_r = [edge_ref[side, k] for k in range(6)]
         changes = {
@@ -516,7 +523,7 @@
     halo = (3, n, planes_z)
     strata = porosity.shape[0]
     hbm = pl.BlockSpec(memory_space=pltpu.HBM)
-    own_lo, own_hi, table, concentration, stratum = pl.pallas_call(
+    early, late, table, concentration, stratum = pl.pallas_call(
         pack_kernel,
         out_shape=[
             jax.ShapeDtypeStruct(halo, jnp.float32),
@@ -551,10 +558,12 @@
         ]
     )
     groups = lax.axis_size("trans")
-    up = [(i, i + 1) for i in range(groups - 1)]
-    down = [(i + 1, i) for i in range(groups - 1)]
-    next_lo = lax.ppermute(own_hi, "trans", up)
-    next_hi = lax.ppermute(own_lo, "trans", down)
+    def swap(value, start):
+        low = range(start, groups - 1, 2)
+        pairs = [(i, i + 1) for i in low] + [(i + 1, i) for i in low]
+        return lax.ppermute(value, "trans", pairs)
+
+    beyond_early, beyond_late = swap(early, 0), swap(late, 1)
 
     def exchange(value, stride):
         return lax.ppermute(value, "flow", [(i, i ^ stride) for i in range(peers)])
@@ -572,7 +581,7 @@
     )(table, stratum, concentration)
     block_shape = (QUANTITIES, half, planes_z)
     block, send, flow = call(border_kernel, [block_shape, block_shape, (2, 2, n, planes_z)])(
-        table, own_lo, own_hi, next_lo, next_hi, edge, pay
+        table, early, late, beyond_early, beyond_late, edge, pay
     )
     kept = []
     for stride in strides[:-1]:

time: 33.5 us -> 29.6 us (0.88)
  the two profiles are of different devices: /device:TPU:0 before, /device:TPU:18 now
where the time goes in v5:
time: 29.6 us; the launch traced here: 29.4 us
  waiting for transfers between devices  14.3 us (48%)
  Pallas kernels  7.56 us (26%)
  starting transfers between devices  7.49 us (25%)
    ppermute x4, waiting for transfers between devices, exchange(): return lax.ppermute(value, 'flow', [(i, i ^ stride) for i in range(peers)])  14.3 us
    ppermute x4, starting transfers between devices, exchange(): return lax.ppermute(value, 'flow', [(i, i ^ stride) for i in range(peers)])  4.88 us
    pallas_call x1, Pallas kernels, per_device(): call(local_kernel, [(QUANTITIES, planes_y, planes_z), (2, 6, n, planes_z)...  3.7 us
    ppermute x2, starting transfers between devices, swap(): return lax.ppermute(value, 'trans', pairs)  2.6 us
    pallas_call x1, Pallas kernels, per_device(): call(final_kernel, [(4,) + cells], [cells] * 2)  2.14 us
    pallas_call x1, Pallas kernels, per_device(): pl.pallas_call(pack_kernel, out_shape=[jax.ShapeDtypeStruct(halo, jnp.flo...  1.43 us
  transfers between devices with their start and end apart: 6, of which 4 were waited for; matrix products, arithmetic and copies ran while one was open for 0% of the time, Pallas kernels for 13%

profile of v5, /device:TPU:18, one launch (start us, length us, event | category | flops | bytes accessed | tf_op | source)
XLA Modules:
  0.0 29.4 jit_solution(14646111612208067336)
XLA Ops:
  0.0 1.4 %shard_map.73 = (f32[3,16,256]{2,1,0:T(8,128)S(1)}, f32[3,16,256]{2,1,0:T(8,128)S(1)}, f32[16,128]{1,0:T(8,128)S(1)}, f32[4,16,16,256]{3,2,1,0:T(8,128)S(1)}, s32[16,16,256]{2,1,0:T(8,128)S(1)}) custom-call(f32[4,16,16,256]{3,2,1,0:T(8,128)} %conc_hbm.1, s32[16,16,256]{2,1,0:T(8,128)} %stratum_hbm.1, f32[1,16]{1,0:T(1,128)} %bitcast.6, f32[2,16]{1,0:T(2,128)} %bitcast.5, ...), custom_call_target="tpu_custom_call" | custom-call | tf_op jit(solution)/shard_map/pallas_call | solution.py:526
  1.4 0.1 collective-permute-start
  1.5 2.5 %collective-permute-start.1 = (f32[3,16,256]{2,1,0:T(8,128)S(1)}, f32[3,16,256]{2,1,0:T(8,128)S(1)}, u32[]{:S(2)}, u32[]{:S(2)}) collective-permute-start(f32[3,16,256]{2,1,0:T(8,128)S(1)} %get-tuple-element.40.late_ref), channel_id=1, source_target_pairs={{1,2},{2,1},{5,6},{6,5},{9,10},{10,9},{13,14},{14,13},{17,18},{18,... | collective-permute-start | bytes 147464 | tf_op jit(solution)/shard_map/ppermute | solution.py:564
  4.1 3.7 %shard_map.74 = (f32[14,16,256]{2,1,0:T(8,128)S(1)}, f32[2,6,16,256]{3,2,1,0:T(8,128)S(1)}, f32[16,16,256]{2,1,0:T(8,128)S(1)}, f32[16,16,256]{2,1,0:T(8,128)S(1...) custom-call(f32[16,128]{1,0:T(8,128)S(1)} %get-tuple-element.29.tab_, ...), custom_call_target="tpu_custom_call" | custom-call | tf_op jit(solution)/shard_map/pallas_call | solution.py:571
  7.8 0.0 collective-permute-done.beyond_early_ref
  7.8 0.0 collective-permute-done.1.beyond_late_ref
  7.8 0.2 shard_map.75
  8.0 1.6 %collective-permute-start.2 = (f32[14,8,256]{2,1,0:T(8,128)S(1)}, f32[14,8,256]{2,1,0:T(8,128)S(1)}, u32[]{:S(2)}, u32[]{:S(2)}) collective-permute-start(f32[14,8,256]{2,1,0:T(8,128)S(1)} %get-tuple-element.45), channel_id=1, source_target_pairs={{0,4},{4,0},{8,12},{12,8},{16,20},{20,16},{24,28},{28,24},{1,5},{5... | collective-permute-start | bytes 344072 | tf_op jit(solution)/shard_map/ppermute | solution.py:569
  9.5 3.3 %collective-permute-done.2.other_ref = f32[14,8,256]{2,1,0:T(8,128)S(1)} collective-permute-done((f32[14,8,256]{2,1,0:T(8,128)S(1)}, f32[14,8,256]{2,1,0:T(8,128)S(1)}, u32[]{:S(2)}, u32[]{:S(2)}) %collective-permute-start.2) | collective-permute-done | bytes 114720 | tf_op jit(solution)/shard_map/ppermute | solution.py:569
  12.9 1.6 %collective-permute-start.3 = (f32[14,8,256]{2,1,0:T(8,128)S(1)}, f32[14,8,256]{2,1,0:T(8,128)S(1)}, u32[]{:S(2)}, u32[]{:S(2)}) collective-permute-start(f32[14,8,256]{2,1,0:T(8,128)S(1)} %get-tuple-element.46.own_ref), channel_id=1, source_target_pairs={{0,8},{4,12},{8,0},{12,4},{16,24},{20,28},{24,16},{28,20},{1,9},{5... | collective-permute-start | bytes 344072 | tf_op jit(solution)/shard_map/ppermute | solution.py:569
  14.5 3.7 %collective-permute-done.3.other_ref = f32[14,8,256]{2,1,0:T(8,128)S(1)} collective-permute-done((f32[14,8,256]{2,1,0:T(8,128)S(1)}, f32[14,8,256]{2,1,0:T(8,128)S(1)}, u32[]{:S(2)}, u32[]{:S(2)}) %collective-permute-start.3) | collective-permute-done | bytes 114720 | tf_op jit(solution)/shard_map/ppermute | solution.py:569
  18.2 0.1 collective-permute-start.4
  18.3 5.0 %collective-permute-done.4.other_ref = f32[5,8,256]{2,1,0:T(8,128)S(1)} collective-permute-done((f32[5,8,256]{2,1,0:T(8,128)S(1)}, f32[5,8,256]{2,1,0:T(8,128)S(1)}, u32[]{:S(2)}, u32[]{:S(2)}) %collective-permute-start.4) | collective-permute-done | bytes 40992 | tf_op jit(solution)/shard_map/ppermute | solution.py:569
  23.3 1.6 %collective-permute-start.5 = (f32[4,8,256]{2,1,0:T(8,128)S(1)}, f32[4,8,256]{2,1,0:T(8,128)S(1)}, u32[]{:S(2)}, u32[]{:S(2)}) collective-permute-start(f32[4,8,256]{2,1,0:T(8,128)S(1)} %get-tuple-element.52), channel_id=1, source_target_pairs={{0,4},{4,0},{8,12},{12,8},{16,20},{20,16},{24,28},{28,24},{1,5},{5... | collective-permute-start | bytes 98312 | tf_op jit(solution)/shard_map/ppermute | solution.py:569
  24.9 2.4 %collective-permute-done.5.current_ref = f32[4,8,256]{2,1,0:T(8,128)S(1)} collective-permute-done((f32[4,8,256]{2,1,0:T(8,128)S(1)}, f32[4,8,256]{2,1,0:T(8,128)S(1)}, u32[]{:S(2)}, u32[]{:S(2)}) %collective-permute-start.5) | collective-permute-done | bytes 32800 | tf_op jit(solution)/shard_map/ppermute | solution.py:569
  27.3 2.1 %shard_map.79 = f32[4,16,16,256]{3,2,1,0:T(8,128)} custom-call(f32[16,128]{1,0:T(8,128)S(1)} %get-tuple-element.29.tab_ref, s32[16,16,256]{2,1,0:T(8,128)S(1)} %get-tuple-element.30.stratum_ref, f32[4,16,16,256]{3,2,1,0:T(8,128)S(1)} %get-tuple-element.31.conc_ref, f32[16,16,256]{2,1,0:T(8,128)S(1)} %get-tuple-element.32.pass_a_ref, ...), custom_call_target="tpu_custom_call" | custom-call | tf_op jit(solution)/shard_map/pallas_call | solution.py:601
  (3 shorter events, 0.1 us)
Async XLA Ops:
  1.4 6.3 %collective-permute-start = (f32[3,16,256]{2,1,0:T(8,128)S(1)}, f32[3,16,256]{2,1,0:T(8,128)S(1)}, u32[]{:S(2)}, u32[]{:S(2)}) collective-permute-start(f32[3,16,256]{2,1,0:T(8,128)S(1)} %get-tuple-element.39.early_ref), channel_id=1, source_target_pairs={{0,1},{2,3},{1,0},{3,2},{4,5},{6,7},{5,4},{7,6},{8,9},{10,11},{9,8... | collective-permute-start | bytes 147464 | tf_op jit(solution)/shard_map/ppermute | solution.py:564
  1.5 6.3 %collective-permute-start.1 = (f32[3,16,256]{2,1,0:T(8,128)S(1)}, f32[3,16,256]{2,1,0:T(8,128)S(1)}, u32[]{:S(2)}, u32[]{:S(2)}) collective-permute-start(f32[3,16,256]{2,1,0:T(8,128)S(1)} %get-tuple-element.40.late_ref), channel_id=1, source_target_pairs={{1,2},{2,1},{5,6},{6,5},{9,10},{10,9},{13,14},{14,13},{17,18},{18,... | collective-permute-start | bytes 147464 | tf_op jit(solution)/shard_map/ppermute | solution.py:564
  8.0 4.9 %collective-permute-start.2 = (f32[14,8,256]{2,1,0:T(8,128)S(1)}, f32[14,8,256]{2,1,0:T(8,128)S(1)}, u32[]{:S(2)}, u32[]{:S(2)}) collective-permute-start(f32[14,8,256]{2,1,0:T(8,128)S(1)} %get-tuple-element.45), channel_id=1, source_target_pairs={{0,4},{4,0},{8,12},{12,8},{16,20},{20,16},{24,28},{28,24},{1,5},{5... | collective-permute-start | bytes 344072 | tf_op jit(solution)/shard_map/ppermute | solution.py:569
  12.9 5.3 %collective-permute-start.3 = (f32[14,8,256]{2,1,0:T(8,128)S(1)}, f32[14,8,256]{2,1,0:T(8,128)S(1)}, u32[]{:S(2)}, u32[]{:S(2)}) collective-permute-start(f32[14,8,256]{2,1,0:T(8,128)S(1)} %get-tuple-element.46.own_ref), channel_id=1, source_target_pairs={{0,8},{4,12},{8,0},{12,4},{16,24},{20,28},{24,16},{28,20},{1,9},{5... | collective-permute-start | bytes 344072 | tf_op jit(solution)/shard_map/ppermute | solution.py:569
  18.2 5.1 %collective-permute-start.4 = (f32[5,8,256]{2,1,0:T(8,128)S(1)}, f32[5,8,256]{2,1,0:T(8,128)S(1)}, u32[]{:S(2)}, u32[]{:S(2)}) collective-permute-start(f32[5,8,256]{2,1,0:T(8,128)S(1)} %get-tuple-element.48), channel_id=1, source_target_pairs={{0,16},{4,20},{8,24},{12,28},{16,0},{20,4},{24,8},{28,12},{1,17},{... | collective-permute-start | bytes 122888 | tf_op jit(solution)/shard_map/ppermute | solution.py:569
  23.3 4.0 %collective-permute-start.5 = (f32[4,8,256]{2,1,0:T(8,128)S(1)}, f32[4,8,256]{2,1,0:T(8,128)S(1)}, u32[]{:S(2)}, u32[]{:S(2)}) collective-permute-start(f32[4,8,256]{2,1,0:T(8,128)S(1)} %get-tuple-element.52), channel_id=1, source_target_pairs={{0,4},{4,0},{8,12},{12,8},{16,20},{20,16},{24,28},{28,24},{1,5},{5... | collective-permute-start | bytes 98312 | tf_op jit(solution)/shard_map/ppermute | solution.py:569

commit v6 on v5

--- a/solution.py
+++ b/solution.py
@@ -157,7 +157,13 @@
     copies[7].wait()
 
 
+def half_of(kept):
+    second = lax.axis_index("flow") % 2
+    return second if kept else 1 - second
+
+
 def local_kernel(
+    kept,
     tab_ref,
     stratum_ref,
     conc_ref,
@@ -181,11 +187,15 @@
     adj_r,
 ):
     n, planes_y, planes_z = stratum_ref.shape
+    half = planes_y // 2
+    which = half_of(kept)
+    rows = pl.ds(pl.multiple_of(which * half, half), half)
+    other_rows = pl.ds(pl.multiple_of((1 - which) * half, half), half)
     number = Numbers(tab_ref)
 
     cond_a = cond_b = half_a = half_b = through_a = through_b = None
     for i in range(n):
-        index = stratum_ref[i]
+        index = stratum_ref[i, rows, :]
         shunt_a, shunt_b = number("shunt_a", index), number("shunt_b", index)
         new_a, new_b = number("half_a", index), number("half_b", index)
         kappa_ref[i] = number("kappa", index)
@@ -230,9 +240,11 @@
         g_l, g_r = s_l, s_r
         adj_l[i], adj_r[i] = g_l, g_r
 
-    lane = lax.broadcasted_iota(jnp.int32, (planes_y, planes_z), 1)
-    line = lax.broadcasted_iota(jnp.int32, (planes_y, planes_z), 0)
-    inside = (line < planes_y - 1, lane < planes_z - 1)
+    lane = lax.broadcasted_iota(jnp.int32, (half, planes_z), 1)
+    line = lax.broadcasted_iota(jnp.int32, (half, planes_z), 0)
+    inside = (line < half - 1, lane < planes_z - 1)
+    meets = line == (half - 1) * (1 - which)
+    shift = jnp.where(which == 0, half - 1, 1)
     w_l, w_r = adj_l[n - 1] * over_a, adj_r[n - 1] * over_a
     free = [None] * 4
     for i in reversed(range(n)):
@@ -240,10 +252,10 @@
             pass_a, drop_a = pass_a_ref[i + 1], drop_a_ref[i + 1]
             w_l, w_r = pass_a * w_l + drop_a * adj_l[i], pass_a * w_r + drop_a * adj_r[i]
         adj_l[i], adj_r[i] = w_l, w_r
-        index = stratum_ref[i]
+        index = stratum_ref[i, rows, :]
         half_t = number("half_t", index)
         por = number("por", index)
-        c0, c1, c2, c3 = [conc_ref[k, i] for k in range(4)]
+        c0, c1, c2, c3 = [conc_ref[k, i, rows, :] for k in range(4)]
         source_a = por * c0 + number("alpha_a", index) * c2
         source_b = (
             por * c1
@@ -259,6 +271,10 @@
             flow_b = face * shifted_difference(c1, axis)
             source_a = source_a + (flow_a - pltpu.roll(flow_a, 1, axis))
             source_b = source_b + (flow_b - pltpu.roll(flow_b, 1, axis))
+        beyond_t = pltpu.roll(number("half_t", stratum_ref[i, other_rows, :]), shift, 0)
+        face = jnp.where(meets, recip(half_t + beyond_t), 0.0)
+        source_a = source_a + face * (pltpu.roll(conc_ref[0, i, other_rows, :], shift, 0) - c0)
+        source_b = source_b + face * (pltpu.roll(conc_ref[1, i, other_rows, :], shift, 0) - c1)
         source_a_ref[i], source_b_ref[i] = source_a, source_b
         terms = [
             left_a[i] * source_a,
@@ -281,11 +297,11 @@
     for q, value in enumerate(quantities):
         pay_ref[q] = value
     for k, ref in enumerate((left_a, right_a, left_b, right_b, adj_l, adj_r)):
-        edge_ref[0, k] = ref[:, 0, :]
-        edge_ref[1, k] = ref[:, planes_y - 1, :]
+        edge_ref[k] = jnp.where(which == 0, ref[:, 0, :], ref[:, half - 1, :])
 
 
 def border_kernel(
+    kept,
     tab_ref,
     early_ref,
     late_ref,
@@ -293,42 +309,37 @@
     beyond_late_ref,
     edge_ref,
     pay_ref,
-    keep_ref,
-    send_ref,
+    out_ref,
     flow_ref,
 ):
     number = Numbers(tab_ref)
-    half = pay_ref.shape[1] // 2
-    second = side_of("flow", 1)
-    low, high = pay_ref[:, :half], pay_ref[:, half:]
-    keep_ref[...] = jnp.where(second, high, low)
-    send_ref[...] = jnp.where(second, low, high)
-    odd = side_of("trans", 1)
-    for side in range(2):
-        early = odd if side == 0 else jnp.logical_not(odd)
-        own = jnp.where(early, early_ref[...], late_ref[...])
-        beyond = jnp.where(early, beyond_early_ref[...], beyond_late_ref[...])
-        own_id = own[2].astype(jnp.int32) - 1
-        next_id = beyond[2].astype(jnp.int32) - 1
-        present = next_id >= 0
-        resist = number("half_t", own_id) + number("half_t", jnp.maximum(next_id, 0))
-        face = jnp.where(present, recip(resist), 0.0)
-        flow_a = face * (beyond[0] - own[0])
-        flow_b = face * (beyond[1] - own[1])
-        flow_ref[side, 0], flow_ref[side, 1] = flow_a, flow_b
-        l_a, r_a, l_b, r_b, w_l, w_r = [edge_ref[side, k] for k in range(6)]
-        changes = {
-            FA_L: l_a * flow_a,
-            FA_R: r_a * flow_a,
-            FB_L: l_b * flow_b + w_l * flow_a,
-            FB_R: r_b * flow_b + w_r * flow_a,
-        }
-        row = 0 if side == 0 else half - 1
-        kept = second if side == 1 else jnp.logical_not(second)
-        for q, change in changes.items():
-            total = jnp.sum(change, axis=0, keepdims=True)
-            keep_ref[q, row : row + 1, :] += jnp.where(kept, total, 0.0)
-            send_ref[q, row : row + 1, :] += jnp.where(kept, 0.0, total)
+    half = pay_ref.shape[1]
+    low = half_of(kept) == 0
+    early = side_of("trans", 1) == low
+    own = jnp.where(early, early_ref[...], late_ref[...])
+    beyond = jnp.where(early, beyond_early_ref[...], beyond_late_ref[...])
+    own_id = own[2].astype(jnp.int32) - 1
+    next_id = beyond[2].astype(jnp.int32) - 1
+    resist = number("half_t", own_id) + number("half_t", jnp.maximum(next_id, 0))
+    face = jnp.where(next_id >= 0, recip(resist), 0.0)
+    flow_a = face * (beyond[0] - own[0])
+    flow_b = face * (beyond[1] - own[1])
+    flow_ref[0], flow_ref[1] = flow_a, flow_b
+    l_a, r_a, l_b, r_b, w_l, w_r = [edge_ref[k] for k in range(6)]
+    changes = {
+        FA_L: l_a * flow_a,
+        FA_R: r_a * flow_a,
+        FB_L: l_b * flow_b + w_l * flow_a,
+        FB_R: r_b * flow_b + w_r * flow_a,
+    }
+    line = lax.broadcasted_iota(jnp.int32, pay_ref.shape[1:], 0)
+    outer = line == jnp.where(low, 0, half - 1)
+    for q in range(QUANTITIES):
+        value = pay_ref[q]
+        if q in changes:
+            total = jnp.sum(changes[q], axis=0, keepdims=True)
+            value = value + jnp.where(outer, total, 0.0)
+        out_ref[q] = value
 
 
 FACE_L = (ZA_LL, ZB_LL, C_LL, FA_L, FB_L)
@@ -425,6 +436,7 @@
 
 
 def final_kernel(
+    kept,
     tab_ref,
     stratum_ref,
     conc_ref,
@@ -436,64 +448,61 @@
     source_a_ref,
     source_b_ref,
     flow_ref,
-    mine_ref,
     current_ref,
-    out_ref,
-    gather_a,
-    gather_b,
+    *refs,
 ):
+    out_hbm, gather_a, gather_b, made, sems = refs[-5:]
     n, planes_y, planes_z = stratum_ref.shape
+    half = planes_y // 2
+    which = half_of(kept)
+    rows = pl.ds(pl.multiple_of(which * half, half), half)
     number = Numbers(tab_ref)
-
-    second = side_of("flow", 1)
-
-    def plane(q):
-        mine, other = mine_ref[q], current_ref[q]
-        halves = [jnp.where(second, other, mine), jnp.where(second, mine, other)]
-        return jnp.concatenate(halves, axis=0)
-
-    line = lax.broadcasted_iota(jnp.int32, (planes_y, planes_z), 0)
-    first_line, last_line = line == 0, line == planes_y - 1
+    line = lax.broadcasted_iota(jnp.int32, (half, planes_z), 0)
+    outer = line == (half - 1) * which
 
     def with_border(source, component, i):
-        low = jnp.broadcast_to(flow_ref[0, component, i : i + 1, :], source.shape)
-        high = jnp.broadcast_to(flow_ref[1, component, i : i + 1, :], source.shape)
-        return source + jnp.where(first_line, low, jnp.where(last_line, high, 0.0))
-
-    value = plane(0)
+        flow = jnp.broadcast_to(flow_ref[component, i : i + 1, :], source.shape)
+        return source + jnp.where(outer, flow, 0.0)
+
+    l_a, r_a, l_b, r_b = [current_ref[q] for q in range(CURRENTS)]
+    value = l_a
     for i in range(n):
         value = with_border(source_a_ref[i], 0, i) + value
         if i < n - 1:
             gather_a[i] = value
             value = pass_a_ref[i + 1] * value
-    x = (value + plane(1)) * over_ref[0]
+    x = (value + r_a) * over_ref[0]
     for i in reversed(range(n)):
         if i < n - 1:
             x = pass_a_ref[i + 1] * x + drop_a_ref[i + 1] * gather_a[i]
-        out_ref[0, i] = x
-    value = plane(2)
+        made[0, i] = x
+    value = l_b
     for i in range(n):
-        kappa = number("kappa", stratum_ref[i])
-        value = with_border(source_b_ref[i], 1, i) + kappa * out_ref[0, i] + value
+        kappa = number("kappa", stratum_ref[i, rows, :])
+        value = with_border(source_b_ref[i], 1, i) + kappa * made[0, i] + value
         if i < n - 1:
             gather_b[i] = value
             value = pass_b_ref[i + 1] * value
-    x = (value + plane(3)) * over_ref[1]
+    x = (value + r_b) * over_ref[1]
+    copies = []
     for i in reversed(range(n)):
         if i < n - 1:
             x = pass_b_ref[i + 1] * x + drop_b_ref[i + 1] * gather_b[i]
-        out_ref[1, i] = x
-        index = stratum_ref[i]
-        x2 = (
-            number("beta", index) * conc_ref[2, i]
-            + number("gamma", index) * out_ref[0, i]
-        )
-        out_ref[2, i] = x2
-        out_ref[3, i] = (
-            number("free_b", index) * conc_ref[3, i]
+        made[1, i] = x
+        index = stratum_ref[i, rows, :]
+        x2 = number("beta", index) * conc_ref[2, i, rows, :] + number("gamma", index) * made[0, i]
+        made[2, i] = x2
+        made[3, i] = (
+            number("free_b", index) * conc_ref[3, i, rows, :]
             + number("share_b", index) * x
             + number("decay_b", index) * x2
         )
+        copies.append(
+            pltpu.make_async_copy(made.at[:, i], out_hbm.at[:, i, rows, :], sems.at[i])
+        )
+        copies[-1].start()
+    for copy in copies:
+        copy.wait()
 
 
 def call(kernel, outs, scratch=()):
@@ -568,21 +577,28 @@
     def exchange(value, stride):
         return lax.ppermute(value, "flow", [(i, i ^ stride) for i in range(peers)])
 
-    pay, edge, pass_a, drop_a, pass_b, drop_b, over, source_a, source_b = call(
-        local_kernel,
-        [
-            (QUANTITIES, planes_y, planes_z),
-            (2, 6, n, planes_z),
-            *[cells] * 4,
-            (2, planes_y, planes_z),
-            *[cells] * 2,
-        ],
-        [cells] * 9,
-    )(table, stratum, concentration)
+    half_cells = (n, half, planes_z)
     block_shape = (QUANTITIES, half, planes_z)
-    block, send, flow = call(border_kernel, [block_shape, block_shape, (2, 2, n, planes_z)])(
-        table, early, late, beyond_early, beyond_late, edge, pay
-    )
+
+    def local(kept):
+        pay, edge, *rest = call(
+            functools.partial(local_kernel, kept),
+            [
+                block_shape,
+                (6, n, planes_z),
+                *[half_cells] * 4,
+                (2, half, planes_z),
+                *[half_cells] * 2,
+            ],
+            [half_cells] * 9,
+        )(table, stratum, concentration)
+        pay, flow = call(
+            functools.partial(border_kernel, kept), [block_shape, (2, n, planes_z)]
+        )(table, early, late, beyond_early, beyond_late, edge, pay)
+        return pay, (*rest, flow)
+
+    send, sent_rest = local(False)
+    block, kept_rest = local(True)
     kept = []
     for stride in strides[:-1]:
         other = exchange(send, stride)
@@ -598,22 +614,26 @@
         block, exchange(send, strides[-1]), *kept
     )
     currents = exchange(send, 1)
-    (out,) = call(final_kernel, [(4,) + cells], [cells] * 2)(
-        table,
-        stratum,
-        concentration,
-        pass_a,
-        drop_a,
-        pass_b,
-        drop_b,
-        over,
-        source_a,
-        source_b,
-        flow,
-        mine,
-        currents,
-    )
-    return out
+    def final(kept, rest, currents, *before):
+        whole = jax.ShapeDtypeStruct((4,) + cells, jnp.float32)
+        vmem = pl.BlockSpec(memory_space=pltpu.VMEM)
+        return pl.pallas_call(
+            functools.partial(final_kernel, kept),
+            out_shape=whole,
+            in_specs=[vmem] * 12 + [hbm] * len(before),
+            out_specs=hbm,
+            scratch_shapes=[
+                pltpu.VMEM(half_cells, jnp.float32),
+                pltpu.VMEM(half_cells, jnp.float32),
+                pltpu.VMEM((4,) + half_cells, jnp.float32),
+                pltpu.SemaphoreType.DMA((n,)),
+            ],
+            input_output_aliases={12: 0} if before else {},
+            compiler_params=pltpu.CompilerParams(vmem_limit_bytes=VMEM_LIMIT),
+        )(table, stratum, concentration, *rest, currents, *before)
+
+    out = final(True, kept_rest, mine)
+    return final(False, sent_rest, currents, out)
 
 
 def solution(mesh):

time: 29.6 us -> 27.8 us (0.939)
  the two profiles are of different devices: /device:TPU:18 before, /device:TPU:22 now
where the time goes in v6:
time: 27.8 us; the launch traced here: 27.7 us
  waiting for transfers between devices  11.9 us (43%)
  Pallas kernels  9.86 us (35%)
  starting transfers between devices  5.79 us (21%)
    ppermute x4, waiting for transfers between devices, exchange(): return lax.ppermute(value, 'flow', [(i, i ^ stride) for i in range(peers)])  11.8 us
    pallas_call x2, Pallas kernels, local(): call(functools.partial(local_kernel, kept), [block_shape, (6, n, planes_z...  5.48 us
    ppermute x4, starting transfers between devices, exchange(): return lax.ppermute(value, 'flow', [(i, i ^ stride) for i in range(peers)])  3.19 us
    ppermute x2, starting transfers between devices, swap(): return lax.ppermute(value, 'trans', pairs)  2.6 us
    pallas_call x2, Pallas kernels, final(): pl.pallas_call(functools.partial(final_kernel, kept), out_shape=whole, in...  2.58 us
    pallas_call x1, Pallas kernels, per_device(): pl.pallas_call(pack_kernel, out_shape=[jax.ShapeDtypeStruct(halo, jnp.flo...  1.43 us
  transfers between devices with their start and end apart: 6, of which 5 were waited for; matrix products, arithmetic and copies ran while one was open for 0% of the time, Pallas kernels for 25%

profile of v6, /device:TPU:22, one launch (start us, length us, event | category | flops | bytes accessed | tf_op | source)
XLA Modules:
  0.0 27.7 jit_solution(5512602704868020263)
XLA Ops:
  0.0 1.4 %shard_map.73 = (f32[3,16,256]{2,1,0:T(8,128)S(1)}, f32[3,16,256]{2,1,0:T(8,128)S(1)}, f32[16,128]{1,0:T(8,128)S(1)}, f32[4,16,16,256]{3,2,1,0:T(8,128)S(1)}, s32[16,16,256]{2,1,0:T(8,128)S(1)}) custom-call(f32[4,16,16,256]{3,2,1,0:T(8,128)} %conc_hbm.1, s32[16,16,256]{2,1,0:T(8,128)} %stratum_hbm.1, f32[1,16]{1,0:T(1,128)} %bitcast.6, f32[2,16]{1,0:T(2,128)} %bitcast.5, ...), custom_call_target="tpu_custom_call" | custom-call | tf_op jit(solution)/shard_map/pallas_call | solution.py:535
  1.4 0.1 collective-permute-start
  1.5 2.5 %collective-permute-start.1 = (f32[3,16,256]{2,1,0:T(8,128)S(1)}, f32[3,16,256]{2,1,0:T(8,128)S(1)}, u32[]{:S(2)}, u32[]{:S(2)}) collective-permute-start(f32[3,16,256]{2,1,0:T(8,128)S(1)} %get-tuple-element.50.late_ref), channel_id=1, source_target_pairs={{1,2},{2,1},{5,6},{6,5},{9,10},{10,9},{13,14},{14,13},{17,18},{18,... | collective-permute-start | bytes 147464 | tf_op jit(solution)/shard_map/ppermute | solution.py:573
  4.1 2.7 %shard_map.74 = (f32[14,8,256]{2,1,0:T(8,128)S(1)}, f32[6,16,256]{2,1,0:T(8,128)S(1)}, f32[16,8,256]{2,1,0:T(8,128)S(1)}, f32[16,8,256]{2,1,0:T(8,128)S(1)}, f32...) custom-call(f32[16,128]{1,0:T(8,128)S(1)} %get-tuple-element.39.tab_, ...), custom_call_target="tpu_custom_call" | custom-call | tf_op jit(solution)/shard_map/pallas_call | solution.py:584
  6.8 0.0 collective-permute-done.beyond_early_ref
  6.8 0.1 collective-permute-done.1.beyond_late_ref
  6.9 0.1 shard_map.75
  7.0 0.6 %collective-permute-start.2 = (f32[14,8,256]{2,1,0:T(8,128)S(1)}, f32[14,8,256]{2,1,0:T(8,128)S(1)}, u32[]{:S(2)}, u32[]{:S(2)}) collective-permute-start(f32[14,8,256]{2,1,0:T(8,128)S(1)} %get-tuple-element.57), channel_id=1, source_target_pairs={{0,4},{4,0},{8,12},{12,8},{16,20},{20,16},{24,28},{28,24},{1,5},{5... | collective-permute-start | bytes 344072 | tf_op jit(solution)/shard_map/ppermute | solution.py:578
  7.6 2.7 %shard_map.76 = (f32[14,8,256]{2,1,0:T(8,128)S(1)}, f32[6,16,256]{2,1,0:T(8,128)S(1)}, f32[16,8,256]{2,1,0:T(8,128)S(1)}, f32[16,8,256]{2,1,0:T(8,128)S(1)}, f32...) custom-call(f32[16,128]{1,0:T(8,128)S(1)} %get-tuple-element.39.tab_, ...), custom_call_target="tpu_custom_call" | custom-call | tf_op jit(solution)/shard_map/pallas_call | solution.py:584
  10.4 0.1 shard_map.77
  10.5 1.4 %collective-permute-done.2.other_ref = f32[14,8,256]{2,1,0:T(8,128)S(1)} collective-permute-done((f32[14,8,256]{2,1,0:T(8,128)S(1)}, f32[14,8,256]{2,1,0:T(8,128)S(1)}, u32[]{:S(2)}, u32[]{:S(2)}) %collective-permute-start.2) | collective-permute-done | bytes 114720 | tf_op jit(solution)/shard_map/ppermute | solution.py:578
  11.9 1.6 %collective-permute-start.3 = (f32[14,8,256]{2,1,0:T(8,128)S(1)}, f32[14,8,256]{2,1,0:T(8,128)S(1)}, u32[]{:S(2)}, u32[]{:S(2)}) collective-permute-start(f32[14,8,256]{2,1,0:T(8,128)S(1)} %get-tuple-element.58.own_ref), channel_id=1, source_target_pairs={{0,8},{4,12},{8,0},{12,4},{16,24},{20,28},{24,16},{28,20},{1,9},{5... | collective-permute-start | bytes 344072 | tf_op jit(solution)/shard_map/ppermute | solution.py:578
  13.6 3.7 %collective-permute-done.3.other_ref = f32[14,8,256]{2,1,0:T(8,128)S(1)} collective-permute-done((f32[14,8,256]{2,1,0:T(8,128)S(1)}, f32[14,8,256]{2,1,0:T(8,128)S(1)}, u32[]{:S(2)}, u32[]{:S(2)}) %collective-permute-start.3) | collective-permute-done | bytes 114720 | tf_op jit(solution)/shard_map/ppermute | solution.py:578
  17.3 0.4 %collective-permute-start.4 = (f32[5,8,256]{2,1,0:T(8,128)S(1)}, f32[5,8,256]{2,1,0:T(8,128)S(1)}, u32[]{:S(2)}, u32[]{:S(2)}) collective-permute-start(f32[5,8,256]{2,1,0:T(8,128)S(1)} %get-tuple-element.60), channel_id=1, source_target_pairs={{0,16},{4,20},{8,24},{12,28},{16,0},{20,4},{24,8},{28,12},{1,17},{... | collective-permute-start | bytes 122888 | tf_op jit(solution)/shard_map/ppermute | solution.py:578
  17.7 4.7 %collective-permute-done.4.other_ref = f32[5,8,256]{2,1,0:T(8,128)S(1)} collective-permute-done((f32[5,8,256]{2,1,0:T(8,128)S(1)}, f32[5,8,256]{2,1,0:T(8,128)S(1)}, u32[]{:S(2)}, u32[]{:S(2)}) %collective-permute-start.4) | collective-permute-done | bytes 40992 | tf_op jit(solution)/shard_map/ppermute | solution.py:578
  22.4 0.6 %collective-permute-start.5 = (f32[4,8,256]{2,1,0:T(8,128)S(1)}, f32[4,8,256]{2,1,0:T(8,128)S(1)}, u32[]{:S(2)}, u32[]{:S(2)}) collective-permute-start(f32[4,8,256]{2,1,0:T(8,128)S(1)} %get-tuple-element.63), channel_id=1, source_target_pairs={{0,4},{4,0},{8,12},{12,8},{16,20},{20,16},{24,28},{28,24},{1,5},{5... | collective-permute-start | bytes 98312 | tf_op jit(solution)/shard_map/ppermute | solution.py:578
  23.0 1.3 %shard_map.81.refs_0_ = f32[4,16,16,256]{3,2,1,0:T(8,128)} custom-call(f32[16,128]{1,0:T(8,128)S(1)} %get-tuple-element.39.tab_ref, s32[16,16,256]{2,1,0:T(8,128)S(1)} %get-tuple-element.40.stratum_ref, f32[4,16,16,256]{3,2,1,0:T(8,128)S(1)} %get-tuple-element.41.conc_ref, f32[16,8,256]{2,1,0:T(8,128)S(1)} %get-tuple-element.64.pass_a_ref, ...), custom_call_target="tpu_custom_call" | custom-call | tf_op jit(solution)/shard_map/pallas_call | solution.py:620
  24.3 2.1 %collective-permute-done.5.current_ref = f32[4,8,256]{2,1,0:T(8,128)S(1)} collective-permute-done((f32[4,8,256]{2,1,0:T(8,128)S(1)}, f32[4,8,256]{2,1,0:T(8,128)S(1)}, u32[]{:S(2)}, u32[]{:S(2)}) %collective-permute-start.5) | collective-permute-done | bytes 32800 | tf_op jit(solution)/shard_map/ppermute | solution.py:578
  26.4 1.3 %shard_map.82 = f32[4,16,16,256]{3,2,1,0:T(8,128)} custom-call(f32[16,128]{1,0:T(8,128)S(1)} %get-tuple-element.39.tab_ref, s32[16,16,256]{2,1,0:T(8,128)S(1)} %get-tuple-element.40.stratum_ref, f32[4,16,16,256]{3,2,1,0:T(8,128)S(1)} %get-tuple-element.41.conc_ref, f32[16,8,256]{2,1,0:T(8,128)S(1)} %get-tuple-element.42.pass_a_ref, ...), custom_call_target="tpu_custom_call", output_to_operand_aliasing={{}: (12, {})} | custom-call | tf_op jit(solution)/shard_map/pallas_call | solution.py:620
  (3 shorter events, 0.1 us)
Async XLA Ops:
  1.4 5.4 %collective-permute-start = (f32[3,16,256]{2,1,0:T(8,128)S(1)}, f32[3,16,256]{2,1,0:T(8,128)S(1)}, u32[]{:S(2)}, u32[]{:S(2)}) collective-permute-start(f32[3,16,256]{2,1,0:T(8,128)S(1)} %get-tuple-element.49.early_ref), channel_id=1, source_target_pairs={{0,1},{2,3},{1,0},{3,2},{4,5},{6,7},{5,4},{7,6},{8,9},{10,11},{9,8... | collective-permute-start | bytes 147464 | tf_op jit(solution)/shard_map/ppermute | solution.py:573
  1.5 5.4 %collective-permute-start.1 = (f32[3,16,256]{2,1,0:T(8,128)S(1)}, f32[3,16,256]{2,1,0:T(8,128)S(1)}, u32[]{:S(2)}, u32[]{:S(2)}) collective-permute-start(f32[3,16,256]{2,1,0:T(8,128)S(1)} %get-tuple-element.50.late_ref), channel_id=1, source_target_pairs={{1,2},{2,1},{5,6},{6,5},{9,10},{10,9},{13,14},{14,13},{17,18},{18,... | collective-permute-start | bytes 147464 | tf_op jit(solution)/shard_map/ppermute | solution.py:573
  7.0 4.9 %collective-permute-start.2 = (f32[14,8,256]{2,1,0:T(8,128)S(1)}, f32[14,8,256]{2,1,0:T(8,128)S(1)}, u32[]{:S(2)}, u32[]{:S(2)}) collective-permute-start(f32[14,8,256]{2,1,0:T(8,128)S(1)} %get-tuple-element.57), channel_id=1, source_target_pairs={{0,4},{4,0},{8,12},{12,8},{16,20},{20,16},{24,28},{28,24},{1,5},{5... | collective-permute-start | bytes 344072 | tf_op jit(solution)/shard_map/ppermute | solution.py:578
  11.9 5.3 %collective-permute-start.3 = (f32[14,8,256]{2,1,0:T(8,128)S(1)}, f32[14,8,256]{2,1,0:T(8,128)S(1)}, u32[]{:S(2)}, u32[]{:S(2)}) collective-permute-start(f32[14,8,256]{2,1,0:T(8,128)S(1)} %get-tuple-element.58.own_ref), channel_id=1, source_target_pairs={{0,8},{4,12},{8,0},{12,4},{16,24},{20,28},{24,16},{28,20},{1,9},{5... | collective-permute-start | bytes 344072 | tf_op jit(solution)/shard_map/ppermute | solution.py:578
  17.3 5.1 %collective-permute-start.4 = (f32[5,8,256]{2,1,0:T(8,128)S(1)}, f32[5,8,256]{2,1,0:T(8,128)S(1)}, u32[]{:S(2)}, u32[]{:S(2)}) collective-permute-start(f32[5,8,256]{2,1,0:T(8,128)S(1)} %get-tuple-element.60), channel_id=1, source_target_pairs={{0,16},{4,20},{8,24},{12,28},{16,0},{20,4},{24,8},{28,12},{1,17},{... | collective-permute-start | bytes 122888 | tf_op jit(solution)/shard_map/ppermute | solution.py:578
  22.4 4.0 %collective-permute-start.5 = (f32[4,8,256]{2,1,0:T(8,128)S(1)}, f32[4,8,256]{2,1,0:T(8,128)S(1)}, u32[]{:S(2)}, u32[]{:S(2)}) collective-permute-start(f32[4,8,256]{2,1,0:T(8,128)S(1)} %get-tuple-element.63), channel_id=1, source_target_pairs={{0,4},{4,0},{8,12},{12,8},{16,20},{20,16},{24,28},{28,24},{1,5},{5... | collective-permute-start | bytes 98312 | tf_op jit(solution)/shard_map/ppermute | solution.py:578

commit v7 on v6

--- a/solution.py
+++ b/solution.py
@@ -11,6 +11,8 @@
 ZA_LL, ZA_LR, ZA_RR, ZB_LL, ZB_LR, ZB_RR, C_LL, C_LR, C_RL, C_RR, FA_L, FA_R, FB_L, FB_R = range(14)
 QUANTITIES = 14
 CURRENTS = 4
+KEPT = 8
+PIECES = 2
 VMEM_LIMIT = 40 * 1024 * 1024
 
 
@@ -193,109 +195,123 @@
     other_rows = pl.ds(pl.multiple_of((1 - which) * half, half), half)
     number = Numbers(tab_ref)
 
-    cond_a = cond_b = half_a = half_b = through_a = through_b = None
-    for i in range(n):
-        index = stratum_ref[i, rows, :]
-        shunt_a, shunt_b = number("shunt_a", index), number("shunt_b", index)
-        new_a, new_b = number("half_a", index), number("half_b", index)
-        kappa_ref[i] = number("kappa", index)
-        if i == 0:
-            first_half_a, first_half_b = new_a, new_b
-            cond_a, cond_b = shunt_a, shunt_b
-            through_a = through_b = jnp.ones_like(shunt_a)
-        else:
-            face_a, face_b = half_a + new_a, half_b + new_b
-            pass_a, pass_b = recip(1.0 + face_a * cond_a), recip(1.0 + face_b * cond_b)
-            cond_a, cond_b = shunt_a + cond_a * pass_a, shunt_b + cond_b * pass_b
-            pass_a_ref[i], pass_b_ref[i] = pass_a, pass_b
-            drop_a_ref[i], drop_b_ref[i] = face_a * pass_a, face_b * pass_b
-            through_a, through_b = through_a * pass_a, through_b * pass_b
-        head_a[i], head_b[i] = through_a, through_b
-        half_a, half_b = new_a, new_b
-    over_a, over_b = recip(cond_a), recip(cond_b)
-    over_ref[0], over_ref[1] = over_a, over_b
-
-    r_a, r_b = over_a, over_b
-    l_a, l_b = through_a * over_a, through_b * over_b
-    couple = [None] * 4
-    for i in reversed(range(n)):
-        if i < n - 1:
-            pass_a, pass_b = pass_a_ref[i + 1], pass_b_ref[i + 1]
-            l_a = pass_a * l_a + drop_a_ref[i + 1] * head_a[i]
-            l_b = pass_b * l_b + drop_b_ref[i + 1] * head_b[i]
-            r_a, r_b = pass_a * r_a, pass_b * r_b
-        left_a[i], right_a[i], left_b[i], right_b[i] = l_a, r_a, l_b, r_b
-        kappa = kappa_ref[i]
-        k_l, k_r = kappa * l_a, kappa * r_a
-        terms = [l_b * k_l, l_b * k_r, r_b * k_l, r_b * k_r]
-        couple = [t if c is None else c + t for c, t in zip(couple, terms)]
-
-    g_l = g_r = None
-    for i in range(n):
-        kappa = kappa_ref[i]
-        s_l, s_r = kappa * left_b[i], kappa * right_b[i]
-        if i > 0:
-            pass_a = pass_a_ref[i]
-            s_l, s_r = s_l + pass_a * g_l, s_r + pass_a * g_r
-        g_l, g_r = s_l, s_r
-        adj_l[i], adj_r[i] = g_l, g_r
+    pieces = range(PIECES)
+    m = n // PIECES
+    firsts, lasts = [s * m for s in pieces], [s * m + m - 1 for s in pieces]
+
+    cond_a, cond_b, half_a, half_b, through_a, through_b = [[None] * PIECES for _ in range(6)]
+    first_half_a, first_half_b = [None] * PIECES, [None] * PIECES
+    for j in range(m):
+        for s in pieces:
+            i = firsts[s] + j
+            index = stratum_ref[i, rows, :]
+            shunt_a, shunt_b = number("shunt_a", index), number("shunt_b", index)
+            new_a, new_b = number("half_a", index), number("half_b", index)
+            kappa_ref[i] = number("kappa", index)
+            if j == 0:
+                first_half_a[s], first_half_b[s] = new_a, new_b
+                cond_a[s], cond_b[s] = shunt_a, shunt_b
+                through_a[s] = through_b[s] = jnp.ones_like(shunt_a)
+            else:
+                face_a, face_b = half_a[s] + new_a, half_b[s] + new_b
+                pass_a, pass_b = recip(1.0 + face_a * cond_a[s]), recip(1.0 + face_b * cond_b[s])
+                cond_a[s], cond_b[s] = shunt_a + cond_a[s] * pass_a, shunt_b + cond_b[s] * pass_b
+                pass_a_ref[i], pass_b_ref[i] = pass_a, pass_b
+                drop_a_ref[i], drop_b_ref[i] = face_a * pass_a, face_b * pass_b
+                through_a[s], through_b[s] = through_a[s] * pass_a, through_b[s] * pass_b
+            head_a[i], head_b[i] = through_a[s], through_b[s]
+            half_a[s], half_b[s] = new_a, new_b
+    over_a, over_b = [recip(c) for c in cond_a], [recip(c) for c in cond_b]
+    for s in pieces:
+        over_ref[0, s], over_ref[1, s] = over_a[s], over_b[s]
+
+    r_a, r_b = list(over_a), list(over_b)
+    l_a = [t * o for t, o in zip(through_a, over_a)]
+    l_b = [t * o for t, o in zip(through_b, over_b)]
+    couple = [[None] * 4 for _ in pieces]
+    for j in reversed(range(m)):
+        for s in pieces:
+            i = firsts[s] + j
+            if j < m - 1:
+                pass_a, pass_b = pass_a_ref[i + 1], pass_b_ref[i + 1]
+                l_a[s] = pass_a * l_a[s] + drop_a_ref[i + 1] * head_a[i]
+                l_b[s] = pass_b * l_b[s] + drop_b_ref[i + 1] * head_b[i]
+                r_a[s], r_b[s] = pass_a * r_a[s], pass_b * r_b[s]
+            left_a[i], right_a[i], left_b[i], right_b[i] = l_a[s], r_a[s], l_b[s], r_b[s]
+            kappa = kappa_ref[i]
+            k_l, k_r = kappa * l_a[s], kappa * r_a[s]
+            terms = [l_b[s] * k_l, l_b[s] * k_r, r_b[s] * k_l, r_b[s] * k_r]
+            couple[s] = [t if c is None else c + t for c, t in zip(couple[s], terms)]
+
+    g_l, g_r = [None] * PIECES, [None] * PIECES
+    for j in range(m):
+        for s in pieces:
+            i = firsts[s] + j
+            kappa = kappa_ref[i]
+            s_l, s_r = kappa * left_b[i], kappa * right_b[i]
+            if j > 0:
+                pass_a = pass_a_ref[i]
+                s_l, s_r = s_l + pass_a * g_l[s], s_r + pass_a * g_r[s]
+            g_l[s], g_r[s] = s_l, s_r
+            adj_l[i], adj_r[i] = s_l, s_r
 
     lane = lax.broadcasted_iota(jnp.int32, (half, planes_z), 1)
     line = lax.broadcasted_iota(jnp.int32, (half, planes_z), 0)
     inside = (line < half - 1, lane < planes_z - 1)
     meets = line == (half - 1) * (1 - which)
     shift = jnp.where(which == 0, half - 1, 1)
-    w_l, w_r = adj_l[n - 1] * over_a, adj_r[n - 1] * over_a
-    free = [None] * 4
-    for i in reversed(range(n)):
-        if i < n - 1:
-            pass_a, drop_a = pass_a_ref[i + 1], drop_a_ref[i + 1]
-            w_l, w_r = pass_a * w_l + drop_a * adj_l[i], pass_a * w_r + drop_a * adj_r[i]
-        adj_l[i], adj_r[i] = w_l, w_r
-        index = stratum_ref[i, rows, :]
-        half_t = number("half_t", index)
-        por = number("por", index)
-        c0, c1, c2, c3 = [conc_ref[k, i, rows, :] for k in range(4)]
-        source_a = por * c0 + number("alpha_a", index) * c2
-        source_b = (
-            por * c1
-            + number("alpha_b", index) * c3
-            + number("delta", index) * c2
-        )
-        for axis in (0, 1):
-            last = half_t.shape[axis] - 1
-            face = jnp.where(
-                inside[axis], recip(half_t + pltpu.roll(half_t, last, axis)), 0.0
-            )
-            flow_a = face * shifted_difference(c0, axis)
-            flow_b = face * shifted_difference(c1, axis)
-            source_a = source_a + (flow_a - pltpu.roll(flow_a, 1, axis))
-            source_b = source_b + (flow_b - pltpu.roll(flow_b, 1, axis))
-        beyond_t = pltpu.roll(number("half_t", stratum_ref[i, other_rows, :]), shift, 0)
-        face = jnp.where(meets, recip(half_t + beyond_t), 0.0)
-        source_a = source_a + face * (pltpu.roll(conc_ref[0, i, other_rows, :], shift, 0) - c0)
-        source_b = source_b + face * (pltpu.roll(conc_ref[1, i, other_rows, :], shift, 0) - c1)
-        source_a_ref[i], source_b_ref[i] = source_a, source_b
-        terms = [
-            left_a[i] * source_a,
-            right_a[i] * source_a,
-            left_b[i] * source_b + w_l * source_a,
-            right_b[i] * source_b + w_r * source_a,
+    w_l = [adj_l[lasts[s]] * over_a[s] for s in pieces]
+    w_r = [adj_r[lasts[s]] * over_a[s] for s in pieces]
+    free = [[None] * 4 for _ in pieces]
+    for j in reversed(range(m)):
+        for s in pieces:
+            i = firsts[s] + j
+            if j < m - 1:
+                pass_a, drop_a = pass_a_ref[i + 1], drop_a_ref[i + 1]
+                w_l[s] = pass_a * w_l[s] + drop_a * adj_l[i]
+                w_r[s] = pass_a * w_r[s] + drop_a * adj_r[i]
+            adj_l[i], adj_r[i] = w_l[s], w_r[s]
+            index = stratum_ref[i, rows, :]
+            half_t = number("half_t", index)
+            por = number("por", index)
+            c0, c1, c2, c3 = [conc_ref[k, i, rows, :] for k in range(4)]
+            source_a = por * c0 + number("alpha_a", index) * c2
+            source_b = por * c1 + number("alpha_b", index) * c3 + number("delta", index) * c2
+            for axis in (0, 1):
+                last = half_t.shape[axis] - 1
+                face = jnp.where(
+                    inside[axis], recip(half_t + pltpu.roll(half_t, last, axis)), 0.0
+                )
+                flow_a = face * shifted_difference(c0, axis)
+                flow_b = face * shifted_difference(c1, axis)
+                source_a = source_a + (flow_a - pltpu.roll(flow_a, 1, axis))
+                source_b = source_b + (flow_b - pltpu.roll(flow_b, 1, axis))
+            beyond_t = pltpu.roll(number("half_t", stratum_ref[i, other_rows, :]), shift, 0)
+            face = jnp.where(meets, recip(half_t + beyond_t), 0.0)
+            source_a = source_a + face * (pltpu.roll(conc_ref[0, i, other_rows, :], shift, 0) - c0)
+            source_b = source_b + face * (pltpu.roll(conc_ref[1, i, other_rows, :], shift, 0) - c1)
+            source_a_ref[i], source_b_ref[i] = source_a, source_b
+            terms = [
+                left_a[i] * source_a,
+                right_a[i] * source_a,
+                left_b[i] * source_b + w_l[s] * source_a,
+                right_b[i] * source_b + w_r[s] * source_a,
+            ]
+            free[s] = [t if f is None else f + t for f, t in zip(free[s], terms)]
+
+    for s in pieces:
+        quantities = [
+            l_a[s] + first_half_a[s],
+            r_a[s],
+            over_a[s] + half_a[s],
+            l_b[s] + first_half_b[s],
+            r_b[s],
+            over_b[s] + half_b[s],
+            *couple[s],
+            *free[s],
         ]
-        free = [t if f is None else f + t for f, t in zip(free, terms)]
-
-    quantities = [
-        left_a[0] + first_half_a,
-        right_a[0],
-        over_a + half_a,
-        left_b[0] + first_half_b,
-        right_b[0],
-        over_b + half_b,
-        *couple,
-        *free,
-    ]
-    for q, value in enumerate(quantities):
-        pay_ref[q] = value
+        for q, value in enumerate(quantities):
+            pay_ref[s, q] = value
     for k, ref in enumerate((left_a, right_a, left_b, right_b, adj_l, adj_r)):
         edge_ref[k] = jnp.where(which == 0, ref[:, 0, :], ref[:, half - 1, :])
 
@@ -310,18 +326,22 @@
     edge_ref,
     pay_ref,
     out_ref,
+    kept_ref,
     flow_ref,
 ):
     number = Numbers(tab_ref)
-    half = pay_ref.shape[1]
+    n, planes_z = edge_ref.shape[1:]
+    m = n // PIECES
+    half = pay_ref.shape[2]
     low = half_of(kept) == 0
     early = side_of("trans", 1) == low
     own = jnp.where(early, early_ref[...], late_ref[...])
     beyond = jnp.where(early, beyond_early_ref[...], beyond_late_ref[...])
     own_id = own[2].astype(jnp.int32) - 1
     next_id = beyond[2].astype(jnp.int32) - 1
-    resist = number("half_t", own_id) + number("half_t", jnp.maximum(next_id, 0))
-    face = jnp.where(next_id >= 0, recip(resist), 0.0)
+    resist = number("half_t", own_id) + number("half_t", next_id)
+    end = jnp.where(low, 0, lax.axis_size("trans") - 1)
+    face = jnp.where(lax.axis_index("trans") != end, recip(resist), 0.0)
     flow_a = face * (beyond[0] - own[0])
     flow_b = face * (beyond[1] - own[1])
     flow_ref[0], flow_ref[1] = flow_a, flow_b
@@ -332,19 +352,31 @@
         FB_L: l_b * flow_b + w_l * flow_a,
         FB_R: r_b * flow_b + w_r * flow_a,
     }
-    line = lax.broadcasted_iota(jnp.int32, pay_ref.shape[1:], 0)
+    line = lax.broadcasted_iota(jnp.int32, (half, planes_z), 0)
     outer = line == jnp.where(low, 0, half - 1)
+    blocks = []
+    for s in range(PIECES):
+        values = {q: pay_ref[s, q] for q in range(QUANTITIES)}
+        for q, change in changes.items():
+            total = jnp.sum(change[s * m : (s + 1) * m], axis=0, keepdims=True)
+            values[q] = values[q] + jnp.where(outer, total, 0.0)
+        blocks.append(values)
+    slot = 0
+    while len(blocks) > 1:
+        joined = []
+        for one, two in zip(blocks[::2], blocks[1::2]):
+            merged, parts = merge(one, two)
+            for k, value in enumerate(parts):
+                kept_ref[slot, k] = value
+            slot += 1
+            joined.append(merged)
+        blocks = joined
     for q in range(QUANTITIES):
-        value = pay_ref[q]
-        if q in changes:
-            total = jnp.sum(changes[q], axis=0, keepdims=True)
-            value = value + jnp.where(outer, total, 0.0)
-        out_ref[q] = value
+        out_ref[q] = blocks[0][q]
 
 
 FACE_L = (ZA_LL, ZB_LL, C_LL, FA_L, FB_L)
 FACE_R = (ZA_RR, ZB_RR, C_RR, FA_R, FB_R)
-KEPT = 8
 
 
 def merge(one, two):
@@ -447,6 +479,7 @@
     over_ref,
     source_a_ref,
     source_b_ref,
+    kept_ref,
     flow_ref,
     current_ref,
     *refs,
@@ -464,43 +497,66 @@
         flow = jnp.broadcast_to(flow_ref[component, i : i + 1, :], source.shape)
         return source + jnp.where(outer, flow, 0.0)
 
-    l_a, r_a, l_b, r_b = [current_ref[q] for q in range(CURRENTS)]
-    value = l_a
-    for i in range(n):
-        value = with_border(source_a_ref[i], 0, i) + value
-        if i < n - 1:
-            gather_a[i] = value
-            value = pass_a_ref[i + 1] * value
-    x = (value + r_a) * over_ref[0]
-    for i in reversed(range(n)):
-        if i < n - 1:
-            x = pass_a_ref[i + 1] * x + drop_a_ref[i + 1] * gather_a[i]
-        made[0, i] = x
-    value = l_b
-    for i in range(n):
-        kappa = number("kappa", stratum_ref[i, rows, :])
-        value = with_border(source_b_ref[i], 1, i) + kappa * made[0, i] + value
-        if i < n - 1:
-            gather_b[i] = value
-            value = pass_b_ref[i + 1] * value
-    x = (value + r_b) * over_ref[1]
+    ends = [tuple(current_ref[q] for q in range(CURRENTS))]
+    slot = PIECES - 1
+    while len(ends) < PIECES:
+        slot -= len(ends)
+        parts = []
+        for k, (l_a, r_a, l_b, r_b) in enumerate(ends):
+            values = [kept_ref[slot + k, v] for v in range(KEPT)]
+            middle_a, middle_b = between(values, (l_a, r_a, l_b, r_b))
+            parts += [(l_a, -middle_a, l_b, -middle_b), (middle_a, r_a, middle_b, r_b)]
+        ends = parts
+
+    pieces = range(PIECES)
+    m = n // PIECES
+    values = [ends[s][0] for s in pieces]
+    for j in range(m):
+        for s in pieces:
+            i = s * m + j
+            values[s] = with_border(source_a_ref[i], 0, i) + values[s]
+            if j < m - 1:
+                gather_a[i] = values[s]
+                values[s] = pass_a_ref[i + 1] * values[s]
+    x = [(values[s] + ends[s][1]) * over_ref[0, s] for s in pieces]
+    for j in reversed(range(m)):
+        for s in pieces:
+            i = s * m + j
+            if j < m - 1:
+                x[s] = pass_a_ref[i + 1] * x[s] + drop_a_ref[i + 1] * gather_a[i]
+            made[0, i] = x[s]
+    values = [ends[s][2] for s in pieces]
+    for j in range(m):
+        for s in pieces:
+            i = s * m + j
+            kappa = number("kappa", stratum_ref[i, rows, :])
+            values[s] = with_border(source_b_ref[i], 1, i) + kappa * made[0, i] + values[s]
+            if j < m - 1:
+                gather_b[i] = values[s]
+                values[s] = pass_b_ref[i + 1] * values[s]
+    x = [(values[s] + ends[s][3]) * over_ref[1, s] for s in pieces]
     copies = []
-    for i in reversed(range(n)):
-        if i < n - 1:
-            x = pass_b_ref[i + 1] * x + drop_b_ref[i + 1] * gather_b[i]
-        made[1, i] = x
-        index = stratum_ref[i, rows, :]
-        x2 = number("beta", index) * conc_ref[2, i, rows, :] + number("gamma", index) * made[0, i]
-        made[2, i] = x2
-        made[3, i] = (
-            number("free_b", index) * conc_ref[3, i, rows, :]
-            + number("share_b", index) * x
-            + number("decay_b", index) * x2
-        )
-        copies.append(
-            pltpu.make_async_copy(made.at[:, i], out_hbm.at[:, i, rows, :], sems.at[i])
-        )
-        copies[-1].start()
+    for j in reversed(range(m)):
+        for s in pieces:
+            i = s * m + j
+            if j < m - 1:
+                x[s] = pass_b_ref[i + 1] * x[s] + drop_b_ref[i + 1] * gather_b[i]
+            made[1, i] = x[s]
+            index = stratum_ref[i, rows, :]
+            x2 = (
+                number("beta", index) * conc_ref[2, i, rows, :]
+                + number("gamma", index) * made[0, i]
+            )
+            made[2, i] = x2
+            made[3, i] = (
+                number("free_b", index) * conc_ref[3, i, rows, :]
+                + number("share_b", index) * x[s]
+                + number("decay_b", index) * x2
+            )
+            copies.append(
+                pltpu.make_async_copy(made.at[:, i], out_hbm.at[:, i, rows, :], sems.at[i])
+            )
+            copies[-1].start()
     for copy in copies:
         copy.wait()
 
@@ -570,6 +626,8 @@
     def swap(value, start):
         low = range(start, groups - 1, 2)
         pairs = [(i, i + 1) for i in low] + [(i + 1, i) for i in low]
+        if start:
+            pairs += [(0, groups - 1), (groups - 1, 0)]
         return lax.ppermute(value, "trans", pairs)
 
     beyond_early, beyond_late = swap(early, 0), swap(late, 1)
@@ -584,18 +642,19 @@
         pay, edge, *rest = call(
             functools.partial(local_kernel, kept),
             [
-                block_shape,
+                (PIECES,) + block_shape,
                 (6, n, planes_z),
                 *[half_cells] * 4,
-                (2, half, planes_z),
+                (2, PIECES, half, planes_z),
                 *[half_cells] * 2,
             ],
             [half_cells] * 9,
         )(table, stratum, concentration)
-        pay, flow = call(
-            functools.partial(border_kernel, kept), [block_shape, (2, n, planes_z)]
+        pay, parts, flow = call(
+            functools.partial(border_kernel, kept),
+            [block_shape, (PIECES - 1, KEPT, half, planes_z), (2, n, planes_z)],
         )(table, early, late, beyond_early, beyond_late, edge, pay)
-        return pay, (*rest, flow)
+        return pay, (*rest, parts, flow)
 
     send, sent_rest = local(False)
     block, kept_rest = local(True)
@@ -620,7 +679,7 @@
         return pl.pallas_call(
             functools.partial(final_kernel, kept),
             out_shape=whole,
-            in_specs=[vmem] * 12 + [hbm] * len(before),
+            in_specs=[vmem] * 13 + [hbm] * len(before),
             out_specs=hbm,
             scratch_shapes=[
                 pltpu.VMEM(half_cells, jnp.float32),
@@ -628,7 +687,7 @@
                 pltpu.VMEM((4,) + half_cells, jnp.float32),
                 pltpu.SemaphoreType.DMA((n,)),
             ],
-            input_output_aliases={12: 0} if before else {},
+            input_output_aliases={13: 0} if before else {},
             compiler_params=pltpu.CompilerParams(vmem_limit_bytes=VMEM_LIMIT),
         )(table, stratum, concentration, *rest, currents, *before)
 

time: 27.8 us -> 28 us (level)
  the two profiles are of different devices: /device:TPU:22 before, /device:TPU:0 now
where the time goes in v7:
time: 28 us; the launch traced here: 27.9 us
  starting transfers between devices  10.6 us (38%)
  Pallas kernels  9.86 us (35%)
  waiting for transfers between devices  7.33 us (26%)
    ppermute x4, starting transfers between devices, exchange(): return lax.ppermute(value, 'flow', [(i, i ^ stride) for i in range(peers)])  7.48 us
    ppermute x4, waiting for transfers between devices, exchange(): return lax.ppermute(value, 'flow', [(i, i ^ stride) for i in range(peers)])  7.33 us
    pallas_call x2, Pallas kernels, local(): call(functools.partial(local_kernel, kept), [(PIECES,) + block_shape, (6,...  5.42 us
    ppermute x2, starting transfers between devices, swap(): return lax.ppermute(value, 'trans', pairs)  3.13 us
    pallas_call x2, Pallas kernels, final(): pl.pallas_call(functools.partial(final_kernel, kept), out_shape=whole, in...  2.59 us
    pallas_call x1, Pallas kernels, per_device(): pl.pallas_call(pack_kernel, out_shape=[jax.ShapeDtypeStruct(halo, jnp.flo...  1.43 us
  transfers between devices with their start and end apart: 6, of which 4 were waited for; matrix products, arithmetic and copies ran while one was open for 0% of the time, Pallas kernels for 25%

profile of v7, /device:TPU:0, one launch (start us, length us, event | category | flops | bytes accessed | tf_op | source)
XLA Modules:
  0.0 27.9 jit_solution(11748728004407730886)
XLA Ops:
  0.0 1.4 %shard_map.73 = (f32[3,16,256]{2,1,0:T(8,128)S(1)}, f32[3,16,256]{2,1,0:T(8,128)S(1)}, f32[16,128]{1,0:T(8,128)S(1)}, f32[4,16,16,256]{3,2,1,0:T(8,128)S(1)}, s32[16,16,256]{2,1,0:T(8,128)S(1)}) custom-call(f32[4,16,16,256]{3,2,1,0:T(8,128)} %conc_hbm.1, s32[16,16,256]{2,1,0:T(8,128)} %stratum_hbm.1, f32[1,16]{1,0:T(1,128)} %bitcast.6, f32[2,16]{1,0:T(2,128)} %bitcast.5, ...), custom_call_target="tpu_custom_call" | custom-call | tf_op jit(solution)/shard_map/pallas_call | solution.py:591
  1.4 0.5 %collective-permute-start = (f32[3,16,256]{2,1,0:T(8,128)S(1)}, f32[3,16,256]{2,1,0:T(8,128)S(1)}, u32[]{:S(2)}, u32[]{:S(2)}) collective-permute-start(f32[3,16,256]{2,1,0:T(8,128)S(1)} %get-tuple-element.51.early_ref), channel_id=1, source_target_pairs={{0,1},{2,3},{1,0},{3,2},{4,5},{6,7},{5,4},{7,6},{8,9},{10,11},{9,8... | collective-permute-start | bytes 147464 | tf_op jit(solution)/shard_map/ppermute | solution.py:631
  2.0 2.6 %collective-permute-start.1 = (f32[3,16,256]{2,1,0:T(8,128)S(1)}, f32[3,16,256]{2,1,0:T(8,128)S(1)}, u32[]{:S(2)}, u32[]{:S(2)}) collective-permute-start(f32[3,16,256]{2,1,0:T(8,128)S(1)} %get-tuple-element.52.late_ref), channel_id=1, source_target_pairs={{1,2},{2,1},{0,3},{3,0},{5,6},{6,5},{4,7},{7,4},{9,10},{10,9},{8,1... | collective-permute-start | bytes 147464 | tf_op jit(solution)/shard_map/ppermute | solution.py:631
  4.6 2.7 %shard_map.74 = (f32[2,14,8,256]{3,2,1,0:T(8,128)S(1)}, f32[6,16,256]{2,1,0:T(8,128)S(1)}, f32[16,8,256]{2,1,0:T(8,128)S(1)}, f32[16,8,256]{2,1,0:T(8,128)S(1)},...) custom-call(f32[16,128]{1,0:T(8,128)S(1)} %get-tuple-element.41.tab_, ...), custom_call_target="tpu_custom_call" | custom-call | tf_op jit(solution)/shard_map/pallas_call | solution.py:642
  7.3 0.0 collective-permute-done.beyond_early_ref
  7.3 0.0 collective-permute-done.1.beyond_late_ref
  7.3 0.1 shard_map.75
  7.5 1.6 %collective-permute-start.2 = (f32[14,8,256]{2,1,0:T(8,128)S(1)}, f32[14,8,256]{2,1,0:T(8,128)S(1)}, u32[]{:S(2)}, u32[]{:S(2)}) collective-permute-start(f32[14,8,256]{2,1,0:T(8,128)S(1)} %get-tuple-element.60), channel_id=1, source_target_pairs={{0,4},{4,0},{8,12},{12,8},{16,20},{20,16},{24,28},{28,24},{1,5},{5... | collective-permute-start | bytes 344072 | tf_op jit(solution)/shard_map/ppermute | solution.py:636
  9.1 2.7 %shard_map.76 = (f32[2,14,8,256]{3,2,1,0:T(8,128)S(1)}, f32[6,16,256]{2,1,0:T(8,128)S(1)}, f32[16,8,256]{2,1,0:T(8,128)S(1)}, f32[16,8,256]{2,1,0:T(8,128)S(1)},...) custom-call(f32[16,128]{1,0:T(8,128)S(1)} %get-tuple-element.41.tab_, ...), custom_call_target="tpu_custom_call" | custom-call | tf_op jit(solution)/shard_map/pallas_call | solution.py:642
  11.8 0.1 shard_map.77
  11.9 0.7 %collective-permute-done.2.other_ref = f32[14,8,256]{2,1,0:T(8,128)S(1)} collective-permute-done((f32[14,8,256]{2,1,0:T(8,128)S(1)}, f32[14,8,256]{2,1,0:T(8,128)S(1)}, u32[]{:S(2)}, u32[]{:S(2)}) %collective-permute-start.2) | collective-permute-done | bytes 114720 | tf_op jit(solution)/shard_map/ppermute | solution.py:636
  12.7 1.6 %collective-permute-start.3 = (f32[14,8,256]{2,1,0:T(8,128)S(1)}, f32[14,8,256]{2,1,0:T(8,128)S(1)}, u32[]{:S(2)}, u32[]{:S(2)}) collective-permute-start(f32[14,8,256]{2,1,0:T(8,128)S(1)} %get-tuple-element.61.own_ref), channel_id=1, source_target_pairs={{0,8},{4,12},{8,0},{12,4},{16,24},{20,28},{24,16},{28,20},{1,9},{5... | collective-permute-start | bytes 344072 | tf_op jit(solution)/shard_map/ppermute | solution.py:636
  14.3 3.2 %collective-permute-done.3.other_ref = f32[14,8,256]{2,1,0:T(8,128)S(1)} collective-permute-done((f32[14,8,256]{2,1,0:T(8,128)S(1)}, f32[14,8,256]{2,1,0:T(8,128)S(1)}, u32[]{:S(2)}, u32[]{:S(2)}) %collective-permute-start.3) | collective-permute-done | bytes 114720 | tf_op jit(solution)/shard_map/ppermute | solution.py:636
  17.6 2.7 %collective-permute-start.4 = (f32[5,8,256]{2,1,0:T(8,128)S(1)}, f32[5,8,256]{2,1,0:T(8,128)S(1)}, u32[]{:S(2)}, u32[]{:S(2)}) collective-permute-start(f32[5,8,256]{2,1,0:T(8,128)S(1)} %get-tuple-element.63), channel_id=1, source_target_pairs={{0,16},{4,20},{8,24},{12,28},{16,0},{20,4},{24,8},{28,12},{1,17},{... | collective-permute-start | bytes 122888 | tf_op jit(solution)/shard_map/ppermute | solution.py:636
  20.3 2.3 %collective-permute-done.4.other_ref = f32[5,8,256]{2,1,0:T(8,128)S(1)} collective-permute-done((f32[5,8,256]{2,1,0:T(8,128)S(1)}, f32[5,8,256]{2,1,0:T(8,128)S(1)}, u32[]{:S(2)}, u32[]{:S(2)}) %collective-permute-start.4) | collective-permute-done | bytes 40992 | tf_op jit(solution)/shard_map/ppermute | solution.py:636
  22.6 1.6 %collective-permute-start.5 = (f32[4,8,256]{2,1,0:T(8,128)S(1)}, f32[4,8,256]{2,1,0:T(8,128)S(1)}, u32[]{:S(2)}, u32[]{:S(2)}) collective-permute-start(f32[4,8,256]{2,1,0:T(8,128)S(1)} %get-tuple-element.66), channel_id=1, source_target_pairs={{0,4},{4,0},{8,12},{12,8},{16,20},{20,16},{24,28},{28,24},{1,5},{5... | collective-permute-start | bytes 98312 | tf_op jit(solution)/shard_map/ppermute | solution.py:636
  24.2 1.3 %shard_map.81.refs_0_ = f32[4,16,16,256]{3,2,1,0:T(8,128)} custom-call(f32[16,128]{1,0:T(8,128)S(1)} %get-tuple-element.41.tab_ref, s32[16,16,256]{2,1,0:T(8,128)S(1)} %get-tuple-element.42.stratum_ref, f32[4,16,16,256]{3,2,1,0:T(8,128)S(1)} %get-tuple-element.43.conc_ref, f32[16,8,256]{2,1,0:T(8,128)S(1)} %get-tuple-element.67.pass_a_ref, ...), custom_call_target="tpu_custom_call" | custom-call | tf_op jit(solution)/shard_map/pallas_call | solution.py:679
  25.5 1.1 %collective-permute-done.5.current_ref = f32[4,8,256]{2,1,0:T(8,128)S(1)} collective-permute-done((f32[4,8,256]{2,1,0:T(8,128)S(1)}, f32[4,8,256]{2,1,0:T(8,128)S(1)}, u32[]{:S(2)}, u32[]{:S(2)}) %collective-permute-start.5) | collective-permute-done | bytes 32800 | tf_op jit(solution)/shard_map/ppermute | solution.py:636
  26.6 1.3 %shard_map.82 = f32[4,16,16,256]{3,2,1,0:T(8,128)} custom-call(f32[16,128]{1,0:T(8,128)S(1)} %get-tuple-element.41.tab_ref, s32[16,16,256]{2,1,0:T(8,128)S(1)} %get-tuple-element.42.stratum_ref, f32[4,16,16,256]{3,2,1,0:T(8,128)S(1)} %get-tuple-element.43.conc_ref, f32[16,8,256]{2,1,0:T(8,128)S(1)} %get-tuple-element.44.pass_a_ref, ...), custom_call_target="tpu_custom_call", output_to_operand_aliasing={{}: (13, {})} | custom-call | tf_op jit(solution)/shard_map/pallas_call | solution.py:679
  (3 shorter events, 0.1 us)
Async XLA Ops:
  1.4 5.9 %collective-permute-start = (f32[3,16,256]{2,1,0:T(8,128)S(1)}, f32[3,16,256]{2,1,0:T(8,128)S(1)}, u32[]{:S(2)}, u32[]{:S(2)}) collective-permute-start(f32[3,16,256]{2,1,0:T(8,128)S(1)} %get-tuple-element.51.early_ref), channel_id=1, source_target_pairs={{0,1},{2,3},{1,0},{3,2},{4,5},{6,7},{5,4},{7,6},{8,9},{10,11},{9,8... | collective-permute-start | bytes 147464 | tf_op jit(solution)/shard_map/ppermute | solution.py:631
  2.0 5.3 %collective-permute-start.1 = (f32[3,16,256]{2,1,0:T(8,128)S(1)}, f32[3,16,256]{2,1,0:T(8,128)S(1)}, u32[]{:S(2)}, u32[]{:S(2)}) collective-permute-start(f32[3,16,256]{2,1,0:T(8,128)S(1)} %get-tuple-element.52.late_ref), channel_id=1, source_target_pairs={{1,2},{2,1},{0,3},{3,0},{5,6},{6,5},{4,7},{7,4},{9,10},{10,9},{8,1... | collective-permute-start | bytes 147464 | tf_op jit(solution)/shard_map/ppermute | solution.py:631
  7.5 5.2 %collective-permute-start.2 = (f32[14,8,256]{2,1,0:T(8,128)S(1)}, f32[14,8,256]{2,1,0:T(8,128)S(1)}, u32[]{:S(2)}, u32[]{:S(2)}) collective-permute-start(f32[14,8,256]{2,1,0:T(8,128)S(1)} %get-tuple-element.60), channel_id=1, source_target_pairs={{0,4},{4,0},{8,12},{12,8},{16,20},{20,16},{24,28},{28,24},{1,5},{5... | collective-permute-start | bytes 344072 | tf_op jit(solution)/shard_map/ppermute | solution.py:636
  12.7 4.9 %collective-permute-start.3 = (f32[14,8,256]{2,1,0:T(8,128)S(1)}, f32[14,8,256]{2,1,0:T(8,128)S(1)}, u32[]{:S(2)}, u32[]{:S(2)}) collective-permute-start(f32[14,8,256]{2,1,0:T(8,128)S(1)} %get-tuple-element.61.own_ref), channel_id=1, source_target_pairs={{0,8},{4,12},{8,0},{12,4},{16,24},{20,28},{24,16},{28,20},{1,9},{5... | collective-permute-start | bytes 344072 | tf_op jit(solution)/shard_map/ppermute | solution.py:636
  17.6 5.0 %collective-permute-start.4 = (f32[5,8,256]{2,1,0:T(8,128)S(1)}, f32[5,8,256]{2,1,0:T(8,128)S(1)}, u32[]{:S(2)}, u32[]{:S(2)}) collective-permute-start(f32[5,8,256]{2,1,0:T(8,128)S(1)} %get-tuple-element.63), channel_id=1, source_target_pairs={{0,16},{4,20},{8,24},{12,28},{16,0},{20,4},{24,8},{28,12},{1,17},{... | collective-permute-start | bytes 122888 | tf_op jit(solution)/shard_map/ppermute | solution.py:636
  22.6 4.0 %collective-permute-start.5 = (f32[4,8,256]{2,1,0:T(8,128)S(1)}, f32[4,8,256]{2,1,0:T(8,128)S(1)}, u32[]{:S(2)}, u32[]{:S(2)}) collective-permute-start(f32[4,8,256]{2,1,0:T(8,128)S(1)} %get-tuple-element.66), channel_id=1, source_target_pairs={{0,4},{4,0},{8,12},{12,8},{16,20},{20,16},{24,28},{28,24},{1,5},{5... | collective-permute-start | bytes 98312 | tf_op jit(solution)/shard_map/ppermute | solution.py:636

commit v8 on v7

--- a/solution.py
+++ b/solution.py
@@ -12,7 +12,7 @@
 QUANTITIES = 14
 CURRENTS = 4
 KEPT = 8
-PIECES = 2
+PIECES = 4
 VMEM_LIMIT = 40 * 1024 * 1024
 
 
@@ -197,80 +197,83 @@
 
     pieces = range(PIECES)
     m = n // PIECES
-    firsts, lasts = [s * m for s in pieces], [s * m + m - 1 for s in pieces]
-
-    cond_a, cond_b, half_a, half_b, through_a, through_b = [[None] * PIECES for _ in range(6)]
-    first_half_a, first_half_b = [None] * PIECES, [None] * PIECES
-    for j in range(m):
-        for s in pieces:
-            i = firsts[s] + j
+    shape = (half, planes_z)
+    zero, one = jnp.zeros(shape, jnp.float32), jnp.ones(shape, jnp.float32)
+
+    def from_left(j, carry):
+        after = []
+        for s, (cond_a, cond_b, half_a, half_b, through_a, through_b) in zip(pieces, carry):
+            i = s * m + j
             index = stratum_ref[i, rows, :]
-            shunt_a, shunt_b = number("shunt_a", index), number("shunt_b", index)
             new_a, new_b = number("half_a", index), number("half_b", index)
+            face_a, face_b = half_a + new_a, half_b + new_b
+            pass_a, pass_b = recip(1.0 + face_a * cond_a), recip(1.0 + face_b * cond_b)
+            cond_a = number("shunt_a", index) + cond_a * pass_a
+            cond_b = number("shunt_b", index) + cond_b * pass_b
+            through_a, through_b = through_a * pass_a, through_b * pass_b
             kappa_ref[i] = number("kappa", index)
-            if j == 0:
-                first_half_a[s], first_half_b[s] = new_a, new_b
-                cond_a[s], cond_b[s] = shunt_a, shunt_b
-                through_a[s] = through_b[s] = jnp.ones_like(shunt_a)
-            else:
-                face_a, face_b = half_a[s] + new_a, half_b[s] + new_b
-                pass_a, pass_b = recip(1.0 + face_a * cond_a[s]), recip(1.0 + face_b * cond_b[s])
-                cond_a[s], cond_b[s] = shunt_a + cond_a[s] * pass_a, shunt_b + cond_b[s] * pass_b
-                pass_a_ref[i], pass_b_ref[i] = pass_a, pass_b
-                drop_a_ref[i], drop_b_ref[i] = face_a * pass_a, face_b * pass_b
-                through_a[s], through_b[s] = through_a[s] * pass_a, through_b[s] * pass_b
-            head_a[i], head_b[i] = through_a[s], through_b[s]
-            half_a[s], half_b[s] = new_a, new_b
-    over_a, over_b = [recip(c) for c in cond_a], [recip(c) for c in cond_b]
+            pass_a_ref[i], pass_b_ref[i] = pass_a, pass_b
+            drop_a_ref[i], drop_b_ref[i] = face_a * pass_a, face_b * pass_b
+            head_a[i], head_b[i] = through_a, through_b
+            after.append((cond_a, cond_b, new_a, new_b, through_a, through_b))
+        return after
+
+    ahead = lax.fori_loop(0, m, from_left, [(zero, zero, zero, zero, one, one)] * PIECES)
+    over_a, over_b = [recip(c[0]) for c in ahead], [recip(c[1]) for c in ahead]
     for s in pieces:
         over_ref[0, s], over_ref[1, s] = over_a[s], over_b[s]
 
-    r_a, r_b = list(over_a), list(over_b)
-    l_a = [t * o for t, o in zip(through_a, over_a)]
-    l_b = [t * o for t, o in zip(through_b, over_b)]
-    couple = [[None] * 4 for _ in pieces]
-    for j in reversed(range(m)):
-        for s in pieces:
-            i = firsts[s] + j
-            if j < m - 1:
-                pass_a, pass_b = pass_a_ref[i + 1], pass_b_ref[i + 1]
-                l_a[s] = pass_a * l_a[s] + drop_a_ref[i + 1] * head_a[i]
-                l_b[s] = pass_b * l_b[s] + drop_b_ref[i + 1] * head_b[i]
-                r_a[s], r_b[s] = pass_a * r_a[s], pass_b * r_b[s]
-            left_a[i], right_a[i], left_b[i], right_b[i] = l_a[s], r_a[s], l_b[s], r_b[s]
+    def from_right(back, carry):
+        after = []
+        for s, (next_pass, next_drop, next_pass_b, next_drop_b, l_a, r_a, l_b, r_b, *couple) in zip(
+            pieces, carry
+        ):
+            i = s * m + (m - 1 - back)
+            l_a = next_pass * l_a + next_drop * head_a[i]
+            l_b = next_pass_b * l_b + next_drop_b * head_b[i]
+            r_a, r_b = next_pass * r_a, next_pass_b * r_b
+            left_a[i], right_a[i], left_b[i], right_b[i] = l_a, r_a, l_b, r_b
             kappa = kappa_ref[i]
-            k_l, k_r = kappa * l_a[s], kappa * r_a[s]
-            terms = [l_b[s] * k_l, l_b[s] * k_r, r_b[s] * k_l, r_b[s] * k_r]
-            couple[s] = [t if c is None else c + t for c, t in zip(couple[s], terms)]
-
-    g_l, g_r = [None] * PIECES, [None] * PIECES
-    for j in range(m):
-        for s in pieces:
-            i = firsts[s] + j
-            kappa = kappa_ref[i]
-            s_l, s_r = kappa * left_b[i], kappa * right_b[i]
-            if j > 0:
-                pass_a = pass_a_ref[i]
-                s_l, s_r = s_l + pass_a * g_l[s], s_r + pass_a * g_r[s]
-            g_l[s], g_r[s] = s_l, s_r
-            adj_l[i], adj_r[i] = s_l, s_r
-
-    lane = lax.broadcasted_iota(jnp.int32, (half, planes_z), 1)
-    line = lax.broadcasted_iota(jnp.int32, (half, planes_z), 0)
+            k_l, k_r = kappa * l_a, kappa * r_a
+            terms = [l_b * k_l, l_b * k_r, r_b * k_l, r_b * k_r]
+            couple = [c + t for c, t in zip(couple, terms)]
+            passes = (pass_a_ref[i], drop_a_ref[i], pass_b_ref[i], drop_b_ref[i])
+            after.append((*passes, l_a, r_a, l_b, r_b, *couple))
+        return after
+
+    responses = lax.fori_loop(
+        0,
+        m,
+        from_right,
+        [(one, a, one, b, zero, a, zero, b, zero, zero, zero, zero) for a, b in zip(over_a, over_b)],
+    )
+
+    def share(j, carry):
+        after = []
+        for s, (g_l, g_r) in zip(pieces, carry):
+            i = s * m + j
+            kappa, pass_a = kappa_ref[i], pass_a_ref[i]
+            g_l = kappa * left_b[i] + pass_a * g_l
+            g_r = kappa * right_b[i] + pass_a * g_r
+            adj_l[i], adj_r[i] = g_l, g_r
+            after.append((g_l, g_r))
+        return after
+
+    lax.fori_loop(0, m, share, [(zero, zero)] * PIECES)
+
+    lane = lax.broadcasted_iota(jnp.int32, shape, 1)
+    line = lax.broadcasted_iota(jnp.int32, shape, 0)
     inside = (line < half - 1, lane < planes_z - 1)
     meets = line == (half - 1) * (1 - which)
     shift = jnp.where(which == 0, half - 1, 1)
-    w_l = [adj_l[lasts[s]] * over_a[s] for s in pieces]
-    w_r = [adj_r[lasts[s]] * over_a[s] for s in pieces]
-    free = [[None] * 4 for _ in pieces]
-    for j in reversed(range(m)):
-        for s in pieces:
-            i = firsts[s] + j
-            if j < m - 1:
-                pass_a, drop_a = pass_a_ref[i + 1], drop_a_ref[i + 1]
-                w_l[s] = pass_a * w_l[s] + drop_a * adj_l[i]
-                w_r[s] = pass_a * w_r[s] + drop_a * adj_r[i]
-            adj_l[i], adj_r[i] = w_l[s], w_r[s]
+
+    def sources(back, carry):
+        after = []
+        for s, (next_pass, next_drop, w_l, w_r, *free) in zip(pieces, carry):
+            i = s * m + (m - 1 - back)
+            w_l = next_pass * w_l + next_drop * adj_l[i]
+            w_r = next_pass * w_r + next_drop * adj_r[i]
+            adj_l[i], adj_r[i] = w_l, w_r
             index = stratum_ref[i, rows, :]
             half_t = number("half_t", index)
             por = number("por", index)
@@ -288,27 +291,34 @@
                 source_b = source_b + (flow_b - pltpu.roll(flow_b, 1, axis))
             beyond_t = pltpu.roll(number("half_t", stratum_ref[i, other_rows, :]), shift, 0)
             face = jnp.where(meets, recip(half_t + beyond_t), 0.0)
-            source_a = source_a + face * (pltpu.roll(conc_ref[0, i, other_rows, :], shift, 0) - c0)
-            source_b = source_b + face * (pltpu.roll(conc_ref[1, i, other_rows, :], shift, 0) - c1)
+            beyond_a = pltpu.roll(conc_ref[0, i, other_rows, :], shift, 0)
+            beyond_b = pltpu.roll(conc_ref[1, i, other_rows, :], shift, 0)
+            source_a = source_a + face * (beyond_a - c0)
+            source_b = source_b + face * (beyond_b - c1)
             source_a_ref[i], source_b_ref[i] = source_a, source_b
             terms = [
                 left_a[i] * source_a,
                 right_a[i] * source_a,
-                left_b[i] * source_b + w_l[s] * source_a,
-                right_b[i] * source_b + w_r[s] * source_a,
+                left_b[i] * source_b + w_l * source_a,
+                right_b[i] * source_b + w_r * source_a,
             ]
-            free[s] = [t if f is None else f + t for f, t in zip(free[s], terms)]
-
+            free = [f + t for f, t in zip(free, terms)]
+            after.append((pass_a_ref[i], drop_a_ref[i], w_l, w_r, *free))
+        return after
+
+    totals = lax.fori_loop(0, m, sources, [(one, a) + (zero,) * 6 for a in over_a])
     for s in pieces:
+        l_a, r_a, l_b, r_b, *couple = responses[s][4:]
+        first = stratum_ref[s * m, rows, :]
         quantities = [
-            l_a[s] + first_half_a[s],
-            r_a[s],
-            over_a[s] + half_a[s],
-            l_b[s] + first_half_b[s],
-            r_b[s],
-            over_b[s] + half_b[s],
-            *couple[s],
-            *free[s],
+            l_a + number("half_a", first),
+            r_a,
+            over_a[s] + ahead[s][2],
+            l_b + number("half_b", first),
+            r_b,
+            over_b[s] + ahead[s][3],
+            *couple,
+            *totals[s][4:],
         ]
         for q, value in enumerate(quantities):
             pay_ref[s, q] = value
@@ -494,7 +504,7 @@
     outer = line == (half - 1) * which
 
     def with_border(source, component, i):
-        flow = jnp.broadcast_to(flow_ref[component, i : i + 1, :], source.shape)
+        flow = jnp.broadcast_to(flow_ref[component, pl.ds(i, 1), :], source.shape)
         return source + jnp.where(outer, flow, 0.0)
 
     ends = [tuple(current_ref[q] for q in range(CURRENTS))]
@@ -510,38 +520,44 @@
 
     pieces = range(PIECES)
     m = n // PIECES
-    values = [ends[s][0] for s in pieces]
-    for j in range(m):
-        for s in pieces:
+    one = jnp.ones((half, planes_z), jnp.float32)
+
+    def collect_a(j, carry):
+        after = []
+        for s, value in zip(pieces, carry):
             i = s * m + j
-            values[s] = with_border(source_a_ref[i], 0, i) + values[s]
-            if j < m - 1:
-                gather_a[i] = values[s]
-                values[s] = pass_a_ref[i + 1] * values[s]
-    x = [(values[s] + ends[s][1]) * over_ref[0, s] for s in pieces]
-    for j in reversed(range(m)):
-        for s in pieces:
-            i = s * m + j
-            if j < m - 1:
-                x[s] = pass_a_ref[i + 1] * x[s] + drop_a_ref[i + 1] * gather_a[i]
-            made[0, i] = x[s]
-    values = [ends[s][2] for s in pieces]
-    for j in range(m):
-        for s in pieces:
+            gather_a[i] = with_border(source_a_ref[i], 0, i) + pass_a_ref[i] * value
+            after.append(gather_a[i])
+        return after
+
+    def solve_a(back, carry):
+        after = []
+        for s, (next_pass, next_drop, x) in zip(pieces, carry):
+            i = s * m + (m - 1 - back)
+            x = next_pass * x + next_drop * gather_a[i]
+            made[0, i] = x
+            after.append((pass_a_ref[i], drop_a_ref[i], x))
+        return after
+
+    def collect_b(j, carry):
+        after = []
+        for s, value in zip(pieces, carry):
             i = s * m + j
             kappa = number("kappa", stratum_ref[i, rows, :])
-            values[s] = with_border(source_b_ref[i], 1, i) + kappa * made[0, i] + values[s]
-            if j < m - 1:
-                gather_b[i] = values[s]
-                values[s] = pass_b_ref[i + 1] * values[s]
-    x = [(values[s] + ends[s][3]) * over_ref[1, s] for s in pieces]
-    copies = []
-    for j in reversed(range(m)):
-        for s in pieces:
-            i = s * m + j
-            if j < m - 1:
-                x[s] = pass_b_ref[i + 1] * x[s] + drop_b_ref[i + 1] * gather_b[i]
-            made[1, i] = x[s]
+            source = with_border(source_b_ref[i], 1, i) + kappa * made[0, i]
+            gather_b[i] = source + pass_b_ref[i] * value
+            after.append(gather_b[i])
+        return after
+
+    def result(i):
+        return pltpu.make_async_copy(made.at[:, i], out_hbm.at[:, i, rows, :], sems.at[i])
+
+    def solve_b(back, carry):
+        after = []
+        for s, (next_pass, next_drop, x) in zip(pieces, carry):
+            i = s * m + (m - 1 - back)
+            x = next_pass * x + next_drop * gather_b[i]
+            made[1, i] = x
             index = stratum_ref[i, rows, :]
             x2 = (
                 number("beta", index) * conc_ref[2, i, rows, :]
@@ -550,15 +566,22 @@
             made[2, i] = x2
             made[3, i] = (
                 number("free_b", index) * conc_ref[3, i, rows, :]
-                + number("share_b", index) * x[s]
+                + number("share_b", index) * x
                 + number("decay_b", index) * x2
             )
-            copies.append(
-                pltpu.make_async_copy(made.at[:, i], out_hbm.at[:, i, rows, :], sems.at[i])
-            )
-            copies[-1].start()
-    for copy in copies:
-        copy.wait()
+            after.append((pass_b_ref[i], drop_b_ref[i], x))
+        for s in pieces:
+            result(s * m + (m - 1 - back)).start()
+        return after
+
+    lax.fori_loop(0, m, collect_a, [ends[s][0] for s in pieces])
+    start = [(one, over_ref[0, s], ends[s][1] * over_ref[0, s]) for s in pieces]
+    lax.fori_loop(0, m, solve_a, start)
+    lax.fori_loop(0, m, collect_b, [ends[s][2] for s in pieces])
+    start = [(one, over_ref[1, s], ends[s][3] * over_ref[1, s]) for s in pieces]
+    lax.fori_loop(0, m, solve_b, start)
+    for i in range(n):
+        result(i).wait()
 
 
 def call(kernel, outs, scratch=()):

time: 28 us -> 28.2 us (level)
  Pallas kernels: 9.86 us -> 10.3 us
  waiting for transfers between devices: 7.33 us -> 7.04 us
    pallas_call x2, Pallas kernels: 2.59 us -> 3.8 us  [final(): pl.pallas_call(functools.partial(final_kernel, kept), out_shape=whole, in...]
    pallas_call x2, Pallas kernels: 5.42 us -> 4.57 us  [local(): call(functools.partial(local_kernel, kept), [(PIECES,) + block_shape, (6,...]
    ppermute x4, waiting for transfers between devices: 7.33 us -> 7.04 us  [exchange(): return lax.ppermute(value, 'flow', [(i, i ^ stride) for i in range(peers)])]
  transfers between devices with their start and end apart: 6 -> 6, of which waited for: 4 -> 4; matrix products, arithmetic and copies ran while one was open for 0% -> 0% of each run, Pallas kernels for 25% -> 24%
where the time goes in v8:
time: 28.2 us; the launch traced here: 28.1 us
  starting transfers between devices  10.7 us (38%)
  Pallas kernels  10.3 us (37%)
  waiting for transfers between devices  7.04 us (25%)
    ppermute x4, starting transfers between devices, exchange(): return lax.ppermute(value, 'flow', [(i, i ^ stride) for i in range(peers)])  7.56 us
    ppermute x4, waiting for transfers between devices, exchange(): return lax.ppermute(value, 'flow', [(i, i ^ stride) for i in range(peers)])  7.04 us
    pallas_call x2, Pallas kernels, local(): call(functools.partial(local_kernel, kept), [(PIECES,) + block_shape, (6,...  4.57 us
    pallas_call x2, Pallas kernels, final(): pl.pallas_call(functools.partial(final_kernel, kept), out_shape=whole, in...  3.8 us
    ppermute x2, starting transfers between devices, swap(): return lax.ppermute(value, 'trans', pairs)  3.13 us
    pallas_call x1, Pallas kernels, per_device(): pl.pallas_call(pack_kernel, out_shape=[jax.ShapeDtypeStruct(halo, jnp.flo...  1.43 us
  transfers between devices with their start and end apart: 6, of which 4 were waited for; matrix products, arithmetic and copies ran while one was open for 0% of the time, Pallas kernels for 24%

profile of v8, /device:TPU:0, one launch (start us, length us, event | category | flops | bytes accessed | tf_op | source)
XLA Modules:
  0.0 28.1 jit_solution(6930115442984071786)
XLA Ops:
  0.0 1.4 %shard_map.73 = (f32[3,16,256]{2,1,0:T(8,128)S(1)}, f32[3,16,256]{2,1,0:T(8,128)S(1)}, f32[16,128]{1,0:T(8,128)S(1)}, f32[4,16,16,256]{3,2,1,0:T(8,128)S(1)}, s32[16,16,256]{2,1,0:T(8,128)S(1)}) custom-call(f32[4,16,16,256]{3,2,1,0:T(8,128)} %conc_hbm.1, s32[16,16,256]{2,1,0:T(8,128)} %stratum_hbm.1, f32[1,16]{1,0:T(1,128)} %bitcast.6, f32[2,16]{1,0:T(2,128)} %bitcast.5, ...), custom_call_target="tpu_custom_call" | custom-call | tf_op jit(solution)/shard_map/pallas_call | solution.py:614
  1.4 0.5 %collective-permute-start = (f32[3,16,256]{2,1,0:T(8,128)S(1)}, f32[3,16,256]{2,1,0:T(8,128)S(1)}, u32[]{:S(2)}, u32[]{:S(2)}) collective-permute-start(f32[3,16,256]{2,1,0:T(8,128)S(1)} %get-tuple-element.51.early_ref), channel_id=1, source_target_pairs={{0,1},{2,3},{1,0},{3,2},{4,5},{6,7},{5,4},{7,6},{8,9},{10,11},{9,8... | collective-permute-start | bytes 147464 | tf_op jit(solution)/shard_map/ppermute | solution.py:654
  2.0 2.6 %collective-permute-start.1 = (f32[3,16,256]{2,1,0:T(8,128)S(1)}, f32[3,16,256]{2,1,0:T(8,128)S(1)}, u32[]{:S(2)}, u32[]{:S(2)}) collective-permute-start(f32[3,16,256]{2,1,0:T(8,128)S(1)} %get-tuple-element.52.late_ref), channel_id=1, source_target_pairs={{1,2},{2,1},{0,3},{3,0},{5,6},{6,5},{4,7},{7,4},{9,10},{10,9},{8,1... | collective-permute-start | bytes 147464 | tf_op jit(solution)/shard_map/ppermute | solution.py:654
  4.6 2.3 %shard_map.74 = (f32[4,14,8,256]{3,2,1,0:T(8,128)S(1)}, f32[6,16,256]{2,1,0:T(8,128)S(1)}, f32[16,8,256]{2,1,0:T(8,128)S(1)}, f32[16,8,256]{2,1,0:T(8,128)S(1)},...) custom-call(f32[16,128]{1,0:T(8,128)S(1)} %get-tuple-element.41.tab_, ...), custom_call_target="tpu_custom_call" | custom-call | tf_op jit(solution)/shard_map/pallas_call | solution.py:665
  6.9 0.0 collective-permute-done.beyond_early_ref
  6.9 0.0 collective-permute-done.1.beyond_late_ref
  6.9 0.2 shard_map.75
  7.1 1.6 %collective-permute-start.2 = (f32[14,8,256]{2,1,0:T(8,128)S(1)}, f32[14,8,256]{2,1,0:T(8,128)S(1)}, u32[]{:S(2)}, u32[]{:S(2)}) collective-permute-start(f32[14,8,256]{2,1,0:T(8,128)S(1)} %get-tuple-element.60), channel_id=1, source_target_pairs={{0,4},{4,0},{8,12},{12,8},{16,20},{20,16},{24,28},{28,24},{1,5},{5... | collective-permute-start | bytes 344072 | tf_op jit(solution)/shard_map/ppermute | solution.py:659
  8.7 2.3 %shard_map.76 = (f32[4,14,8,256]{3,2,1,0:T(8,128)S(1)}, f32[6,16,256]{2,1,0:T(8,128)S(1)}, f32[16,8,256]{2,1,0:T(8,128)S(1)}, f32[16,8,256]{2,1,0:T(8,128)S(1)},...) custom-call(f32[16,128]{1,0:T(8,128)S(1)} %get-tuple-element.41.tab_, ...), custom_call_target="tpu_custom_call" | custom-call | tf_op jit(solution)/shard_map/pallas_call | solution.py:665
  10.9 0.2 shard_map.77
  11.1 1.1 %collective-permute-done.2.other_ref = f32[14,8,256]{2,1,0:T(8,128)S(1)} collective-permute-done((f32[14,8,256]{2,1,0:T(8,128)S(1)}, f32[14,8,256]{2,1,0:T(8,128)S(1)}, u32[]{:S(2)}, u32[]{:S(2)}) %collective-permute-start.2) | collective-permute-done | bytes 114720 | tf_op jit(solution)/shard_map/ppermute | solution.py:659
  12.3 1.7 %collective-permute-start.3 = (f32[14,8,256]{2,1,0:T(8,128)S(1)}, f32[14,8,256]{2,1,0:T(8,128)S(1)}, u32[]{:S(2)}, u32[]{:S(2)}) collective-permute-start(f32[14,8,256]{2,1,0:T(8,128)S(1)} %get-tuple-element.61.own_ref), channel_id=1, source_target_pairs={{0,8},{4,12},{8,0},{12,4},{16,24},{20,28},{24,16},{28,20},{1,9},{5... | collective-permute-start | bytes 344072 | tf_op jit(solution)/shard_map/ppermute | solution.py:659
  14.0 3.2 %collective-permute-done.3.other_ref = f32[14,8,256]{2,1,0:T(8,128)S(1)} collective-permute-done((f32[14,8,256]{2,1,0:T(8,128)S(1)}, f32[14,8,256]{2,1,0:T(8,128)S(1)}, u32[]{:S(2)}, u32[]{:S(2)}) %collective-permute-start.3) | collective-permute-done | bytes 114720 | tf_op jit(solution)/shard_map/ppermute | solution.py:659
  17.2 2.7 %collective-permute-start.4 = (f32[5,8,256]{2,1,0:T(8,128)S(1)}, f32[5,8,256]{2,1,0:T(8,128)S(1)}, u32[]{:S(2)}, u32[]{:S(2)}) collective-permute-start(f32[5,8,256]{2,1,0:T(8,128)S(1)} %get-tuple-element.63), channel_id=1, source_target_pairs={{0,16},{4,20},{8,24},{12,28},{16,0},{20,4},{24,8},{28,12},{1,17},{... | collective-permute-start | bytes 122888 | tf_op jit(solution)/shard_map/ppermute | solution.py:659
  19.9 2.3 %collective-permute-done.4.other_ref = f32[5,8,256]{2,1,0:T(8,128)S(1)} collective-permute-done((f32[5,8,256]{2,1,0:T(8,128)S(1)}, f32[5,8,256]{2,1,0:T(8,128)S(1)}, u32[]{:S(2)}, u32[]{:S(2)}) %collective-permute-start.4) | collective-permute-done | bytes 40992 | tf_op jit(solution)/shard_map/ppermute | solution.py:659
  22.2 1.6 %collective-permute-start.5 = (f32[4,8,256]{2,1,0:T(8,128)S(1)}, f32[4,8,256]{2,1,0:T(8,128)S(1)}, u32[]{:S(2)}, u32[]{:S(2)}) collective-permute-start(f32[4,8,256]{2,1,0:T(8,128)S(1)} %get-tuple-element.66), channel_id=1, source_target_pairs={{0,4},{4,0},{8,12},{12,8},{16,20},{20,16},{24,28},{28,24},{1,5},{5... | collective-permute-start | bytes 98312 | tf_op jit(solution)/shard_map/ppermute | solution.py:659
  23.8 1.9 %shard_map.81.refs_0_ = f32[4,16,16,256]{3,2,1,0:T(8,128)} custom-call(f32[16,128]{1,0:T(8,128)S(1)} %get-tuple-element.41.tab_ref, s32[16,16,256]{2,1,0:T(8,128)S(1)} %get-tuple-element.42.stratum_ref, f32[4,16,16,256]{3,2,1,0:T(8,128)S(1)} %get-tuple-element.43.conc_ref, f32[16,8,256]{2,1,0:T(8,128)S(1)} %get-tuple-element.67.pass_a_ref, ...), custom_call_target="tpu_custom_call" | custom-call | tf_op jit(solution)/shard_map/pallas_call | solution.py:702
  25.7 0.5 %collective-permute-done.5.current_ref = f32[4,8,256]{2,1,0:T(8,128)S(1)} collective-permute-done((f32[4,8,256]{2,1,0:T(8,128)S(1)}, f32[4,8,256]{2,1,0:T(8,128)S(1)}, u32[]{:S(2)}, u32[]{:S(2)}) %collective-permute-start.5) | collective-permute-done | bytes 32800 | tf_op jit(solution)/shard_map/ppermute | solution.py:659
  26.2 1.9 %shard_map.82 = f32[4,16,16,256]{3,2,1,0:T(8,128)} custom-call(f32[16,128]{1,0:T(8,128)S(1)} %get-tuple-element.41.tab_ref, s32[16,16,256]{2,1,0:T(8,128)S(1)} %get-tuple-element.42.stratum_ref, f32[4,16,16,256]{3,2,1,0:T(8,128)S(1)} %get-tuple-element.43.conc_ref, f32[16,8,256]{2,1,0:T(8,128)S(1)} %get-tuple-element.44.pass_a_ref, ...), custom_call_target="tpu_custom_call", output_to_operand_aliasing={{}: (13, {})} | custom-call | tf_op jit(solution)/shard_map/pallas_call | solution.py:702
  (3 shorter events, 0.1 us)
Async XLA Ops:
  1.4 5.4 %collective-permute-start = (f32[3,16,256]{2,1,0:T(8,128)S(1)}, f32[3,16,256]{2,1,0:T(8,128)S(1)}, u32[]{:S(2)}, u32[]{:S(2)}) collective-permute-start(f32[3,16,256]{2,1,0:T(8,128)S(1)} %get-tuple-element.51.early_ref), channel_id=1, source_target_pairs={{0,1},{2,3},{1,0},{3,2},{4,5},{6,7},{5,4},{7,6},{8,9},{10,11},{9,8... | collective-permute-start | bytes 147464 | tf_op jit(solution)/shard_map/ppermute | solution.py:654
  2.0 4.9 %collective-permute-start.1 = (f32[3,16,256]{2,1,0:T(8,128)S(1)}, f32[3,16,256]{2,1,0:T(8,128)S(1)}, u32[]{:S(2)}, u32[]{:S(2)}) collective-permute-start(f32[3,16,256]{2,1,0:T(8,128)S(1)} %get-tuple-element.52.late_ref), channel_id=1, source_target_pairs={{1,2},{2,1},{0,3},{3,0},{5,6},{6,5},{4,7},{7,4},{9,10},{10,9},{8,1... | collective-permute-start | bytes 147464 | tf_op jit(solution)/shard_map/ppermute | solution.py:654
  7.1 5.2 %collective-permute-start.2 = (f32[14,8,256]{2,1,0:T(8,128)S(1)}, f32[14,8,256]{2,1,0:T(8,128)S(1)}, u32[]{:S(2)}, u32[]{:S(2)}) collective-permute-start(f32[14,8,256]{2,1,0:T(8,128)S(1)} %get-tuple-element.60), channel_id=1, source_target_pairs={{0,4},{4,0},{8,12},{12,8},{16,20},{20,16},{24,28},{28,24},{1,5},{5... | collective-permute-start | bytes 344072 | tf_op jit(solution)/shard_map/ppermute | solution.py:659
  12.3 4.9 %collective-permute-start.3 = (f32[14,8,256]{2,1,0:T(8,128)S(1)}, f32[14,8,256]{2,1,0:T(8,128)S(1)}, u32[]{:S(2)}, u32[]{:S(2)}) collective-permute-start(f32[14,8,256]{2,1,0:T(8,128)S(1)} %get-tuple-element.61.own_ref), channel_id=1, source_target_pairs={{0,8},{4,12},{8,0},{12,4},{16,24},{20,28},{24,16},{28,20},{1,9},{5... | collective-permute-start | bytes 344072 | tf_op jit(solution)/shard_map/ppermute | solution.py:659
  17.2 5.0 %collective-permute-start.4 = (f32[5,8,256]{2,1,0:T(8,128)S(1)}, f32[5,8,256]{2,1,0:T(8,128)S(1)}, u32[]{:S(2)}, u32[]{:S(2)}) collective-permute-start(f32[5,8,256]{2,1,0:T(8,128)S(1)} %get-tuple-element.63), channel_id=1, source_target_pairs={{0,16},{4,20},{8,24},{12,28},{16,0},{20,4},{24,8},{28,12},{1,17},{... | collective-permute-start | bytes 122888 | tf_op jit(solution)/shard_map/ppermute | solution.py:659
  22.2 4.0 %collective-permute-start.5 = (f32[4,8,256]{2,1,0:T(8,128)S(1)}, f32[4,8,256]{2,1,0:T(8,128)S(1)}, u32[]{:S(2)}, u32[]{:S(2)}) collective-permute-start(f32[4,8,256]{2,1,0:T(8,128)S(1)} %get-tuple-element.66), channel_id=1, source_target_pairs={{0,4},{4,0},{8,12},{12,8},{16,20},{20,16},{24,28},{28,24},{1,5},{5... | collective-permute-start | bytes 98312 | tf_op jit(solution)/shard_map/ppermute | solution.py:659

commit v9 on v8

--- a/solution.py
+++ b/solution.py
@@ -331,8 +331,8 @@
     tab_ref,
     early_ref,
     late_ref,
+    beyond_late_ref,
     beyond_early_ref,
-    beyond_late_ref,
     edge_ref,
     pay_ref,
     out_ref,
@@ -520,44 +520,38 @@
 
     pieces = range(PIECES)
     m = n // PIECES
-    one = jnp.ones((half, planes_z), jnp.float32)
-
-    def collect_a(j, carry):
-        after = []
-        for s, value in zip(pieces, carry):
+    values = [ends[s][0] for s in pieces]
+    for j in range(m):
+        for s in pieces:
             i = s * m + j
-            gather_a[i] = with_border(source_a_ref[i], 0, i) + pass_a_ref[i] * value
-            after.append(gather_a[i])
-        return after
-
-    def solve_a(back, carry):
-        after = []
-        for s, (next_pass, next_drop, x) in zip(pieces, carry):
-            i = s * m + (m - 1 - back)
-            x = next_pass * x + next_drop * gather_a[i]
-            made[0, i] = x
-            after.append((pass_a_ref[i], drop_a_ref[i], x))
-        return after
-
-    def collect_b(j, carry):
-        after = []
-        for s, value in zip(pieces, carry):
+            values[s] = with_border(source_a_ref[i], 0, i) + values[s]
+            if j < m - 1:
+                gather_a[i] = values[s]
+                values[s] = pass_a_ref[i + 1] * values[s]
+    x = [(values[s] + ends[s][1]) * over_ref[0, s] for s in pieces]
+    for j in reversed(range(m)):
+        for s in pieces:
+            i = s * m + j
+            if j < m - 1:
+                x[s] = pass_a_ref[i + 1] * x[s] + drop_a_ref[i + 1] * gather_a[i]
+            made[0, i] = x[s]
+    values = [ends[s][2] for s in pieces]
+    for j in range(m):
+        for s in pieces:
             i = s * m + j
             kappa = number("kappa", stratum_ref[i, rows, :])
-            source = with_border(source_b_ref[i], 1, i) + kappa * made[0, i]
-            gather_b[i] = source + pass_b_ref[i] * value
-            after.append(gather_b[i])
-        return after
-
-    def result(i):
-        return pltpu.make_async_copy(made.at[:, i], out_hbm.at[:, i, rows, :], sems.at[i])
-
-    def solve_b(back, carry):
-        after = []
-        for s, (next_pass, next_drop, x) in zip(pieces, carry):
-            i = s * m + (m - 1 - back)
-            x = next_pass * x + next_drop * gather_b[i]
-            made[1, i] = x
+            values[s] = with_border(source_b_ref[i], 1, i) + kappa * made[0, i] + values[s]
+            if j < m - 1:
+                gather_b[i] = values[s]
+                values[s] = pass_b_ref[i + 1] * values[s]
+    x = [(values[s] + ends[s][3]) * over_ref[1, s] for s in pieces]
+    copies = []
+    for j in reversed(range(m)):
+        for s in pieces:
+            i = s * m + j
+            if j < m - 1:
+                x[s] = pass_b_ref[i + 1] * x[s] + drop_b_ref[i + 1] * gather_b[i]
+            made[1, i] = x[s]
             index = stratum_ref[i, rows, :]
             x2 = (
                 number("beta", index) * conc_ref[2, i, rows, :]
@@ -566,22 +560,15 @@
             made[2, i] = x2
             made[3, i] = (
                 number("free_b", index) * conc_ref[3, i, rows, :]
-                + number("share_b", index) * x
+                + number("share_b", index) * x[s]
                 + number("decay_b", index) * x2
             )
-            after.append((pass_b_ref[i], drop_b_ref[i], x))
-        for s in pieces:
-            result(s * m + (m - 1 - back)).start()
-        return after
-
-    lax.fori_loop(0, m, collect_a, [ends[s][0] for s in pieces])
-    start = [(one, over_ref[0, s], ends[s][1] * over_ref[0, s]) for s in pieces]
-    lax.fori_loop(0, m, solve_a, start)
-    lax.fori_loop(0, m, collect_b, [ends[s][2] for s in pieces])
-    start = [(one, over_ref[1, s], ends[s][3] * over_ref[1, s]) for s in pieces]
-    lax.fori_loop(0, m, solve_b, start)
-    for i in range(n):
-        result(i).wait()
+            copies.append(
+                pltpu.make_async_copy(made.at[:, i], out_hbm.at[:, i, rows, :], sems.at[i])
+            )
+            copies[-1].start()
+    for copy in copies:
+        copy.wait()
 
 
 def call(kernel, outs, scratch=()):
@@ -653,7 +640,8 @@
             pairs += [(0, groups - 1), (groups - 1, 0)]
         return lax.ppermute(value, "trans", pairs)
 
-    beyond_early, beyond_late = swap(early, 0), swap(late, 1)
+    beyond_late = swap(late, 1)
+    beyond_early = swap(early, 0)
 
     def exchange(value, stride):
         return lax.ppermute(value, "flow", [(i, i ^ stride) for i in range(peers)])
@@ -676,7 +664,7 @@
         pay, parts, flow = call(
             functools.partial(border_kernel, kept),
             [block_shape, (PIECES - 1, KEPT, half, planes_z), (2, n, planes_z)],
-        )(table, early, late, beyond_early, beyond_late, edge, pay)
+        )(table, early, late, beyond_late, beyond_early, edge, pay)
         return pay, (*rest, parts, flow)
 
     send, sent_rest = local(False)

time: 28.2 us -> 27.6 us (0.979)
  Pallas kernels: 10.3 us -> 9.09 us
  starting transfers between devices: 10.7 us -> 11.2 us
    pallas_call x2, Pallas kernels: 3.8 us -> 2.6 us  [final(): pl.pallas_call(functools.partial(final_kernel, kept), out_shape=whole, in...]
    ppermute x4, starting transfers between devices: 7.56 us -> 8.05 us  [exchange(): return lax.ppermute(value, 'flow', [(i, i ^ stride) for i in range(peers)])]
  transfers between devices with their start and end apart: 6 -> 6, of which waited for: 4 -> 4; matrix products, arithmetic and copies ran while one was open for 0% -> 0% of each run, Pallas kernels for 24% -> 22%
where the time goes in v9:
time: 27.6 us; the launch traced here: 27.4 us
  starting transfers between devices  11.2 us (41%)
  Pallas kernels  9.09 us (33%)
  waiting for transfers between devices  7.1 us (26%)
    ppermute x4, starting transfers between devices, exchange(): return lax.ppermute(value, 'flow', [(i, i ^ stride) for i in range(peers)])  8.05 us
    ppermute x4, waiting for transfers between devices, exchange(): return lax.ppermute(value, 'flow', [(i, i ^ stride) for i in range(peers)])  7.09 us
    pallas_call x2, Pallas kernels, local(): call(functools.partial(local_kernel, kept), [(PIECES,) + block_shape, (6,...  4.57 us
    ppermute x2, starting transfers between devices, swap(): return lax.ppermute(value, 'trans', pairs)  3.12 us
    pallas_call x2, Pallas kernels, final(): pl.pallas_call(functools.partial(final_kernel, kept), out_shape=whole, in...  2.6 us
    pallas_call x1, Pallas kernels, per_device(): pl.pallas_call(pack_kernel, out_shape=[jax.ShapeDtypeStruct(halo, jnp.flo...  1.43 us
  transfers between devices with their start and end apart: 6, of which 4 were waited for; matrix products, arithmetic and copies ran while one was open for 0% of the time, Pallas kernels for 22%

profile of v9, /device:TPU:0, one launch (start us, length us, event | category | flops | bytes accessed | tf_op | source)
XLA Modules:
  0.0 27.4 jit_solution(16986405759119277928)
XLA Ops:
  0.0 1.4 %shard_map.73 = (f32[3,16,256]{2,1,0:T(8,128)S(1)}, f32[3,16,256]{2,1,0:T(8,128)S(1)}, f32[16,128]{1,0:T(8,128)S(1)}, f32[4,16,16,256]{3,2,1,0:T(8,128)S(1)}, s32[16,16,256]{2,1,0:T(8,128)S(1)}) custom-call(f32[4,16,16,256]{3,2,1,0:T(8,128)} %conc_hbm.1, s32[16,16,256]{2,1,0:T(8,128)} %stratum_hbm.1, f32[1,16]{1,0:T(1,128)} %bitcast.6, f32[2,16]{1,0:T(2,128)} %bitcast.5, ...), custom_call_target="tpu_custom_call" | custom-call | tf_op jit(solution)/shard_map/pallas_call | solution.py:601
  1.4 2.4 %collective-permute-start = (f32[3,16,256]{2,1,0:T(8,128)S(1)}, f32[3,16,256]{2,1,0:T(8,128)S(1)}, u32[]{:S(2)}, u32[]{:S(2)}) collective-permute-start(f32[3,16,256]{2,1,0:T(8,128)S(1)} %get-tuple-element.52.late_ref), channel_id=1, source_target_pairs={{1,2},{2,1},{0,3},{3,0},{5,6},{6,5},{4,7},{7,4},{9,10},{10,9},{8,1... | collective-permute-start | bytes 147464 | tf_op jit(solution)/shard_map/ppermute | solution.py:641
  3.9 0.7 %collective-permute-start.1 = (f32[3,16,256]{2,1,0:T(8,128)S(1)}, f32[3,16,256]{2,1,0:T(8,128)S(1)}, u32[]{:S(2)}, u32[]{:S(2)}) collective-permute-start(f32[3,16,256]{2,1,0:T(8,128)S(1)} %get-tuple-element.51.early_ref), channel_id=1, source_target_pairs={{0,1},{2,3},{1,0},{3,2},{4,5},{6,7},{5,4},{7,6},{8,9},{10,11},{9,8... | collective-permute-start | bytes 147464 | tf_op jit(solution)/shard_map/ppermute | solution.py:641
  4.6 2.3 %shard_map.74 = (f32[4,14,8,256]{3,2,1,0:T(8,128)S(1)}, f32[6,16,256]{2,1,0:T(8,128)S(1)}, f32[16,8,256]{2,1,0:T(8,128)S(1)}, f32[16,8,256]{2,1,0:T(8,128)S(1)},...) custom-call(f32[16,128]{1,0:T(8,128)S(1)} %get-tuple-element.41.tab_, ...), custom_call_target="tpu_custom_call" | custom-call | tf_op jit(solution)/shard_map/pallas_call | solution.py:653
  6.8 0.0 collective-permute-done.beyond_late_ref
  6.9 0.0 collective-permute-done.1.beyond_early_ref
  6.9 0.2 shard_map.75
  7.1 1.7 %collective-permute-start.2 = (f32[14,8,256]{2,1,0:T(8,128)S(1)}, f32[14,8,256]{2,1,0:T(8,128)S(1)}, u32[]{:S(2)}, u32[]{:S(2)}) collective-permute-start(f32[14,8,256]{2,1,0:T(8,128)S(1)} %get-tuple-element.60), channel_id=1, source_target_pairs={{0,4},{4,0},{8,12},{12,8},{16,20},{20,16},{24,28},{28,24},{1,5},{5... | collective-permute-start | bytes 344072 | tf_op jit(solution)/shard_map/ppermute | solution.py:647
  8.7 2.3 %shard_map.76 = (f32[4,14,8,256]{3,2,1,0:T(8,128)S(1)}, f32[6,16,256]{2,1,0:T(8,128)S(1)}, f32[16,8,256]{2,1,0:T(8,128)S(1)}, f32[16,8,256]{2,1,0:T(8,128)S(1)},...) custom-call(f32[16,128]{1,0:T(8,128)S(1)} %get-tuple-element.41.tab_, ...), custom_call_target="tpu_custom_call" | custom-call | tf_op jit(solution)/shard_map/pallas_call | solution.py:653
  11.0 0.2 shard_map.77
  11.2 1.0 %collective-permute-done.2.other_ref = f32[14,8,256]{2,1,0:T(8,128)S(1)} collective-permute-done((f32[14,8,256]{2,1,0:T(8,128)S(1)}, f32[14,8,256]{2,1,0:T(8,128)S(1)}, u32[]{:S(2)}, u32[]{:S(2)}) %collective-permute-start.2) | collective-permute-done | bytes 114720 | tf_op jit(solution)/shard_map/ppermute | solution.py:647
  12.2 1.8 %collective-permute-start.3 = (f32[14,8,256]{2,1,0:T(8,128)S(1)}, f32[14,8,256]{2,1,0:T(8,128)S(1)}, u32[]{:S(2)}, u32[]{:S(2)}) collective-permute-start(f32[14,8,256]{2,1,0:T(8,128)S(1)} %get-tuple-element.61.own_ref), channel_id=1, source_target_pairs={{0,8},{4,12},{8,0},{12,4},{16,24},{20,28},{24,16},{28,20},{1,9},{5... | collective-permute-start | bytes 344072 | tf_op jit(solution)/shard_map/ppermute | solution.py:647
  14.0 3.0 %collective-permute-done.3.other_ref = f32[14,8,256]{2,1,0:T(8,128)S(1)} collective-permute-done((f32[14,8,256]{2,1,0:T(8,128)S(1)}, f32[14,8,256]{2,1,0:T(8,128)S(1)}, u32[]{:S(2)}, u32[]{:S(2)}) %collective-permute-start.3) | collective-permute-done | bytes 114720 | tf_op jit(solution)/shard_map/ppermute | solution.py:647
  17.1 2.8 %collective-permute-start.4 = (f32[5,8,256]{2,1,0:T(8,128)S(1)}, f32[5,8,256]{2,1,0:T(8,128)S(1)}, u32[]{:S(2)}, u32[]{:S(2)}) collective-permute-start(f32[5,8,256]{2,1,0:T(8,128)S(1)} %get-tuple-element.63), channel_id=1, source_target_pairs={{0,16},{4,20},{8,24},{12,28},{16,0},{20,4},{24,8},{28,12},{1,17},{... | collective-permute-start | bytes 122888 | tf_op jit(solution)/shard_map/ppermute | solution.py:647
  20.0 2.1 %collective-permute-done.4.other_ref = f32[5,8,256]{2,1,0:T(8,128)S(1)} collective-permute-done((f32[5,8,256]{2,1,0:T(8,128)S(1)}, f32[5,8,256]{2,1,0:T(8,128)S(1)}, u32[]{:S(2)}, u32[]{:S(2)}) %collective-permute-start.4) | collective-permute-done | bytes 40992 | tf_op jit(solution)/shard_map/ppermute | solution.py:647
  22.1 1.8 %collective-permute-start.5 = (f32[4,8,256]{2,1,0:T(8,128)S(1)}, f32[4,8,256]{2,1,0:T(8,128)S(1)}, u32[]{:S(2)}, u32[]{:S(2)}) collective-permute-start(f32[4,8,256]{2,1,0:T(8,128)S(1)} %get-tuple-element.66), channel_id=1, source_target_pairs={{0,4},{4,0},{8,12},{12,8},{16,20},{20,16},{24,28},{28,24},{1,5},{5... | collective-permute-start | bytes 98312 | tf_op jit(solution)/shard_map/ppermute | solution.py:647
  23.9 1.3 %shard_map.81.refs_0_ = f32[4,16,16,256]{3,2,1,0:T(8,128)} custom-call(f32[16,128]{1,0:T(8,128)S(1)} %get-tuple-element.41.tab_ref, s32[16,16,256]{2,1,0:T(8,128)S(1)} %get-tuple-element.42.stratum_ref, f32[4,16,16,256]{3,2,1,0:T(8,128)S(1)} %get-tuple-element.43.conc_ref, f32[16,8,256]{2,1,0:T(8,128)S(1)} %get-tuple-element.67.pass_a_ref, ...), custom_call_target="tpu_custom_call" | custom-call | tf_op jit(solution)/shard_map/pallas_call | solution.py:690
  25.2 0.9 %collective-permute-done.5.current_ref = f32[4,8,256]{2,1,0:T(8,128)S(1)} collective-permute-done((f32[4,8,256]{2,1,0:T(8,128)S(1)}, f32[4,8,256]{2,1,0:T(8,128)S(1)}, u32[]{:S(2)}, u32[]{:S(2)}) %collective-permute-start.5) | collective-permute-done | bytes 32800 | tf_op jit(solution)/shard_map/ppermute | solution.py:647
  26.1 1.3 %shard_map.82 = f32[4,16,16,256]{3,2,1,0:T(8,128)} custom-call(f32[16,128]{1,0:T(8,128)S(1)} %get-tuple-element.41.tab_ref, s32[16,16,256]{2,1,0:T(8,128)S(1)} %get-tuple-element.42.stratum_ref, f32[4,16,16,256]{3,2,1,0:T(8,128)S(1)} %get-tuple-element.43.conc_ref, f32[16,8,256]{2,1,0:T(8,128)S(1)} %get-tuple-element.44.pass_a_ref, ...), custom_call_target="tpu_custom_call", output_to_operand_aliasing={{}: (13, {})} | custom-call | tf_op jit(solution)/shard_map/pallas_call | solution.py:690
  (3 shorter events, 0.1 us)
Async XLA Ops:
  1.4 5.4 %collective-permute-start = (f32[3,16,256]{2,1,0:T(8,128)S(1)}, f32[3,16,256]{2,1,0:T(8,128)S(1)}, u32[]{:S(2)}, u32[]{:S(2)}) collective-permute-start(f32[3,16,256]{2,1,0:T(8,128)S(1)} %get-tuple-element.52.late_ref), channel_id=1, source_target_pairs={{1,2},{2,1},{0,3},{3,0},{5,6},{6,5},{4,7},{7,4},{9,10},{10,9},{8,1... | collective-permute-start | bytes 147464 | tf_op jit(solution)/shard_map/ppermute | solution.py:641
  3.9 3.0 %collective-permute-start.1 = (f32[3,16,256]{2,1,0:T(8,128)S(1)}, f32[3,16,256]{2,1,0:T(8,128)S(1)}, u32[]{:S(2)}, u32[]{:S(2)}) collective-permute-start(f32[3,16,256]{2,1,0:T(8,128)S(1)} %get-tuple-element.51.early_ref), channel_id=1, source_target_pairs={{0,1},{2,3},{1,0},{3,2},{4,5},{6,7},{5,4},{7,6},{8,9},{10,11},{9,8... | collective-permute-start | bytes 147464 | tf_op jit(solution)/shard_map/ppermute | solution.py:641
  7.1 5.1 %collective-permute-start.2 = (f32[14,8,256]{2,1,0:T(8,128)S(1)}, f32[14,8,256]{2,1,0:T(8,128)S(1)}, u32[]{:S(2)}, u32[]{:S(2)}) collective-permute-start(f32[14,8,256]{2,1,0:T(8,128)S(1)} %get-tuple-element.60), channel_id=1, source_target_pairs={{0,4},{4,0},{8,12},{12,8},{16,20},{20,16},{24,28},{28,24},{1,5},{5... | collective-permute-start | bytes 344072 | tf_op jit(solution)/shard_map/ppermute | solution.py:647
  12.2 4.9 %collective-permute-start.3 = (f32[14,8,256]{2,1,0:T(8,128)S(1)}, f32[14,8,256]{2,1,0:T(8,128)S(1)}, u32[]{:S(2)}, u32[]{:S(2)}) collective-permute-start(f32[14,8,256]{2,1,0:T(8,128)S(1)} %get-tuple-element.61.own_ref), channel_id=1, source_target_pairs={{0,8},{4,12},{8,0},{12,4},{16,24},{20,28},{24,16},{28,20},{1,9},{5... | collective-permute-start | bytes 344072 | tf_op jit(solution)/shard_map/ppermute | solution.py:647
  17.1 5.0 %collective-permute-start.4 = (f32[5,8,256]{2,1,0:T(8,128)S(1)}, f32[5,8,256]{2,1,0:T(8,128)S(1)}, u32[]{:S(2)}, u32[]{:S(2)}) collective-permute-start(f32[5,8,256]{2,1,0:T(8,128)S(1)} %get-tuple-element.63), channel_id=1, source_target_pairs={{0,16},{4,20},{8,24},{12,28},{16,0},{20,4},{24,8},{28,12},{1,17},{... | collective-permute-start | bytes 122888 | tf_op jit(solution)/shard_map/ppermute | solution.py:647
  22.1 4.0 %collective-permute-start.5 = (f32[4,8,256]{2,1,0:T(8,128)S(1)}, f32[4,8,256]{2,1,0:T(8,128)S(1)}, u32[]{:S(2)}, u32[]{:S(2)}) collective-permute-start(f32[4,8,256]{2,1,0:T(8,128)S(1)} %get-tuple-element.66), channel_id=1, source_target_pairs={{0,4},{4,0},{8,12},{12,8},{16,20},{20,16},{24,28},{28,24},{1,5},{5... | collective-permute-start | bytes 98312 | tf_op jit(solution)/shard_map/ppermute | solution.py:647

commit v10 on v9

--- a/solution.py
+++ b/solution.py
@@ -12,6 +12,7 @@
 QUANTITIES = 14
 CURRENTS = 4
 KEPT = 8
+CLOSING = 10
 PIECES = 4
 VMEM_LIMIT = 40 * 1024 * 1024
 
@@ -426,36 +427,47 @@
     return middle_a, middle_b
 
 
-def merge_kernel(stride, last, own_ref, other_ref, out_ref, kept_ref, *face_ref):
+def merge_kernel(stride, last, own_ref, other_ref, *refs):
     second = side_of("flow", stride)
     own = [own_ref[q] for q in range(QUANTITIES)]
     other = [other_ref[q] for q in range(QUANTITIES)]
     one = [jnp.where(second, b, a) for a, b in zip(own, other)]
     two = [jnp.where(second, a, b) for a, b in zip(own, other)]
     merged, kept = merge(one, two)
-    for q, value in merged.items():
-        out_ref[q] = value
-    for k, value in enumerate(kept):
-        kept_ref[k] = value
-    if last:
-        after = side_of("flow", 2 * stride)
-        for k, (l, r) in enumerate(zip(FACE_L, FACE_R)):
-            face_ref[0][k] = jnp.where(after, merged[l], merged[r])
-
-
-def close_kernel(strides, own_ref, other_ref, *refs):
-    kept_refs, mine_ref, send_ref = refs[:-2], refs[-2], refs[-1]
-    stride = strides[-1]
-    second = side_of("flow", stride)
-    own = [jnp.where(second, own_ref[l], own_ref[r]) for l, r in zip(FACE_L, FACE_R)]
-    z_a, z_b, couple, f_a, f_b = [own[k] + other_ref[k] for k in range(3)] + [
+    if not last:
+        out_ref, kept_ref = refs
+        for q, value in merged.items():
+            out_ref[q] = value
+        for k, value in enumerate(kept):
+            kept_ref[k] = value
+        return
+    kept_refs, face_ref, closing_ref = refs[:-2], refs[-2], refs[-1]
+    free_a, from_l, from_r, free_b, from_l_b, from_r_b, cross_l, cross_r = kept
+    after = side_of("flow", 2 * stride)
+    for k, (l, r) in enumerate(zip(FACE_L, FACE_R)):
+        face_ref[k] = closing_ref[k] = jnp.where(after, merged[l], merged[r])
+    closing_ref[5] = free_a
+    closing_ref[6] = jnp.where(after, from_l, from_r)
+    closing_ref[7] = free_b
+    closing_ref[8] = jnp.where(after, from_l_b, from_r_b)
+    closing_ref[9] = jnp.where(after, cross_l, cross_r)
+    for k, kept_ref in enumerate(kept_refs):
+        closing_ref[CLOSING + k * KEPT : CLOSING + (k + 1) * KEPT] = kept_ref[...]
+
+
+def close_kernel(strides, other_ref, closing_ref, out_ref):
+    second = side_of("flow", strides[-1])
+    own = [closing_ref[k] for k in range(CLOSING)]
+    z_a, z_b, couple = [own[k] + other_ref[k] for k in range(3)]
+    f_a, f_b = [
         jnp.where(second, other_ref[k] - own[k], own[k] - other_ref[k]) for k in (3, 4)
     ]
     current_a = recip(z_a) * f_a
     current_b = recip(z_b) * (f_b - couple * current_a)
     nothing = jnp.zeros_like(current_a)
 
-    def side_ends(after, middle_a, middle_b, ends):
+    def side_ends(stride, middle_a, middle_b, ends):
+        after = side_of("flow", stride)
         l_a, r_a, l_b, r_b = ends
         return (
             jnp.where(after, middle_a, l_a),
@@ -464,17 +476,16 @@
             jnp.where(after, r_b, -middle_b),
         )
 
-    ends = side_ends(second, current_a, current_b, (nothing,) * 4)
-    for stride, kept_ref in reversed(list(zip(strides[:-1], kept_refs))):
-        middle_a, middle_b = between([kept_ref[k] for k in range(KEPT)], ends)
-        after = side_of("flow", stride)
-        if stride == 1:
-            other_ends = side_ends(jnp.logical_not(after), middle_a, middle_b, ends)
-            for q, value in enumerate(other_ends):
-                send_ref[q] = value
-        ends = side_ends(after, middle_a, middle_b, ends)
+    ends = side_ends(strides[-1], current_a, current_b, (nothing,) * 4)
+    middle_a = own[5] + own[6] * current_a
+    middle_b = own[7] + own[8] * current_b + own[9] * current_a
+    ends = side_ends(strides[-2], middle_a, middle_b, ends)
+    for level in reversed(range(len(strides) - 2)):
+        stride, base = strides[level], CLOSING + level * KEPT
+        middle_a, middle_b = between([closing_ref[base + k] for k in range(KEPT)], ends)
+        ends = side_ends(stride, middle_a, middle_b, ends)
     for q, value in enumerate(ends):
-        mine_ref[q] = value
+        out_ref[q] = value
 
 
 def final_kernel(
@@ -669,21 +680,21 @@
 
     send, sent_rest = local(False)
     block, kept_rest = local(True)
-    kept = []
-    for stride in strides[:-1]:
-        other = exchange(send, stride)
-        last = stride == strides[-2]
-        block, keep, *face = call(
-            functools.partial(merge_kernel, stride, last),
-            [block_shape, (KEPT, half, planes_z)] + [(5, half, planes_z)] * last,
-        )(block, other)
-        kept.append(keep)
-        send = face[0] if last else block
-    ends_shape = (CURRENTS, half, planes_z)
-    mine, send = call(functools.partial(close_kernel, strides), [ends_shape, ends_shape])(
-        block, exchange(send, strides[-1]), *kept
-    )
-    currents = exchange(send, 1)
+    own_kept = []
+    for stride in strides[:-2]:
+        send, keep = call(
+            functools.partial(merge_kernel, stride, False), [block_shape, (KEPT, half, planes_z)]
+        )(block, exchange(send, stride))
+        block = send
+        own_kept.append(keep)
+    face, closing = call(
+        functools.partial(merge_kernel, strides[-2], True),
+        [(5, half, planes_z), (CLOSING + KEPT * len(own_kept), half, planes_z)],
+    )(block, exchange(send, strides[-2]), *own_kept)
+    close = call(functools.partial(close_kernel, strides), [(CURRENTS, half, planes_z)])
+    (mine,) = close(exchange(face, strides[-1]), closing)
+    (currents,) = close(exchange(face, strides[-1] ^ 1), exchange(closing, 1))
+
     def final(kept, rest, currents, *before):
         whole = jax.ShapeDtypeStruct((4,) + cells, jnp.float32)
         vmem = pl.BlockSpec(memory_space=pltpu.VMEM)

time: 27.6 us -> 28.8 us (1.043)
  waiting for transfers between devices: 7.1 us -> 8.38 us
    ppermute x4 -> x5, waiting for transfers between devices: 7.09 us -> 8.38 us  [exchange(): return lax.ppermute(value, 'flow', [(i, i ^ stride) for i in range(peers)])]
    ppermute x4 -> x5, starting transfers between devices: 8.05 us -> 7.92 us  [exchange(): return lax.ppermute(value, 'flow', [(i, i ^ stride) for i in range(peers)])]
  transfers between devices with their start and end apart: 6 -> 7, of which waited for: 4 -> 4; matrix products, arithmetic and copies ran while one was open for 0% -> 0% of each run, Pallas kernels for 22% -> 21%
where the time goes in v10:
time: 28.8 us; the launch traced here: 28.6 us
  starting transfers between devices  11 us (38%)
  Pallas kernels  9.15 us (32%)
  waiting for transfers between devices  8.38 us (29%)
    ppermute x5, waiting for transfers between devices, exchange(): return lax.ppermute(value, 'flow', [(i, i ^ stride) for i in range(peers)])  8.38 us
    ppermute x5, starting transfers between devices, exchange(): return lax.ppermute(value, 'flow', [(i, i ^ stride) for i in range(peers)])  7.92 us
    pallas_call x2, Pallas kernels, local(): call(functools.partial(local_kernel, kept), [(PIECES,) + block_shape, (6,...  4.57 us
    ppermute x2, starting transfers between devices, swap(): return lax.ppermute(value, 'trans', pairs)  3.12 us
    pallas_call x2, Pallas kernels, final(): pl.pallas_call(functools.partial(final_kernel, kept), out_shape=whole, in...  2.62 us
    pallas_call x1, Pallas kernels, per_device(): pl.pallas_call(pack_kernel, out_shape=[jax.ShapeDtypeStruct(halo, jnp.flo...  1.43 us
  transfers between devices with their start and end apart: 7, of which 4 were waited for; matrix products, arithmetic and copies ran while one was open for 0% of the time, Pallas kernels for 21%

profile of v10, /device:TPU:0, one launch (start us, length us, event | category | flops | bytes accessed | tf_op | source)
XLA Modules:
  0.0 28.6 jit_solution(14891643037625998775)
XLA Ops:
  0.0 1.4 %shard_map.73 = (f32[3,16,256]{2,1,0:T(8,128)S(1)}, f32[3,16,256]{2,1,0:T(8,128)S(1)}, f32[16,128]{1,0:T(8,128)S(1)}, f32[4,16,16,256]{3,2,1,0:T(8,128)S(1)}, s32[16,16,256]{2,1,0:T(8,128)S(1)}) custom-call(f32[4,16,16,256]{3,2,1,0:T(8,128)} %conc_hbm.1, s32[16,16,256]{2,1,0:T(8,128)} %stratum_hbm.1, f32[1,16]{1,0:T(1,128)} %bitcast.6, f32[2,16]{1,0:T(2,128)} %bitcast.5, ...), custom_call_target="tpu_custom_call" | custom-call | tf_op jit(solution)/shard_map/pallas_call | solution.py:612
  1.4 2.4 %collective-permute-start = (f32[3,16,256]{2,1,0:T(8,128)S(1)}, f32[3,16,256]{2,1,0:T(8,128)S(1)}, u32[]{:S(2)}, u32[]{:S(2)}) collective-permute-start(f32[3,16,256]{2,1,0:T(8,128)S(1)} %get-tuple-element.49.late_ref), channel_id=1, source_target_pairs={{1,2},{2,1},{0,3},{3,0},{5,6},{6,5},{4,7},{7,4},{9,10},{10,9},{8,1... | collective-permute-start | bytes 147464 | tf_op jit(solution)/shard_map/ppermute | solution.py:652
  3.9 0.7 %collective-permute-start.1 = (f32[3,16,256]{2,1,0:T(8,128)S(1)}, f32[3,16,256]{2,1,0:T(8,128)S(1)}, u32[]{:S(2)}, u32[]{:S(2)}) collective-permute-start(f32[3,16,256]{2,1,0:T(8,128)S(1)} %get-tuple-element.48.early_ref), channel_id=1, source_target_pairs={{0,1},{2,3},{1,0},{3,2},{4,5},{6,7},{5,4},{7,6},{8,9},{10,11},{9,8... | collective-permute-start | bytes 147464 | tf_op jit(solution)/shard_map/ppermute | solution.py:652
  4.6 2.3 %shard_map.74 = (f32[4,14,8,256]{3,2,1,0:T(8,128)S(1)}, f32[6,16,256]{2,1,0:T(8,128)S(1)}, f32[16,8,256]{2,1,0:T(8,128)S(1)}, f32[16,8,256]{2,1,0:T(8,128)S(1)},...) custom-call(f32[16,128]{1,0:T(8,128)S(1)} %get-tuple-element.38.tab_, ...), custom_call_target="tpu_custom_call" | custom-call | tf_op jit(solution)/shard_map/pallas_call | solution.py:664
  6.8 0.0 collective-permute-done.beyond_late_ref
  6.9 0.0 collective-permute-done.1.beyond_early_ref
  6.9 0.2 shard_map.75
  7.1 1.7 %collective-permute-start.2 = (f32[14,8,256]{2,1,0:T(8,128)S(1)}, f32[14,8,256]{2,1,0:T(8,128)S(1)}, u32[]{:S(2)}, u32[]{:S(2)}) collective-permute-start(f32[14,8,256]{2,1,0:T(8,128)S(1)} %get-tuple-element.57), channel_id=1, source_target_pairs={{0,4},{4,0},{8,12},{12,8},{16,20},{20,16},{24,28},{28,24},{1,5},{5... | collective-permute-start | bytes 344072 | tf_op jit(solution)/shard_map/ppermute | solution.py:658
  8.7 2.3 %shard_map.76 = (f32[4,14,8,256]{3,2,1,0:T(8,128)S(1)}, f32[6,16,256]{2,1,0:T(8,128)S(1)}, f32[16,8,256]{2,1,0:T(8,128)S(1)}, f32[16,8,256]{2,1,0:T(8,128)S(1)},...) custom-call(f32[16,128]{1,0:T(8,128)S(1)} %get-tuple-element.38.tab_, ...), custom_call_target="tpu_custom_call" | custom-call | tf_op jit(solution)/shard_map/pallas_call | solution.py:664
  11.0 0.2 shard_map.77
  11.2 1.0 %collective-permute-done.2.other_ref = f32[14,8,256]{2,1,0:T(8,128)S(1)} collective-permute-done((f32[14,8,256]{2,1,0:T(8,128)S(1)}, f32[14,8,256]{2,1,0:T(8,128)S(1)}, u32[]{:S(2)}, u32[]{:S(2)}) %collective-permute-start.2) | collective-permute-done | bytes 114720 | tf_op jit(solution)/shard_map/ppermute | solution.py:658
  12.2 1.8 %collective-permute-start.3 = (f32[14,8,256]{2,1,0:T(8,128)S(1)}, f32[14,8,256]{2,1,0:T(8,128)S(1)}, u32[]{:S(2)}, u32[]{:S(2)}) collective-permute-start(f32[14,8,256]{2,1,0:T(8,128)S(1)} %get-tuple-element.58.own_ref), channel_id=1, source_target_pairs={{0,8},{4,12},{8,0},{12,4},{16,24},{20,28},{24,16},{28,20},{1,9},{5... | collective-permute-start | bytes 344072 | tf_op jit(solution)/shard_map/ppermute | solution.py:658
  14.0 3.0 %collective-permute-done.3.other_ref = f32[14,8,256]{2,1,0:T(8,128)S(1)} collective-permute-done((f32[14,8,256]{2,1,0:T(8,128)S(1)}, f32[14,8,256]{2,1,0:T(8,128)S(1)}, u32[]{:S(2)}, u32[]{:S(2)}) %collective-permute-start.3) | collective-permute-done | bytes 114720 | tf_op jit(solution)/shard_map/ppermute | solution.py:658
  17.1 1.8 %collective-permute-start.5 = (f32[18,8,256]{2,1,0:T(8,128)S(1)}, f32[18,8,256]{2,1,0:T(8,128)S(1)}, u32[]{:S(2)}, u32[]{:S(2)}) collective-permute-start(f32[18,8,256]{2,1,0:T(8,128)S(1)} %get-tuple-element.61.closing_ref), channel_id=1, source_target_pairs={{0,4},{4,0},{8,12},{12,8},{16,20},{20,16},{24,28},{28,24},{1,5},{5... | collective-permute-start | bytes 442376 | tf_op jit(solution)/shard_map/ppermute | solution.py:658
  18.9 2.6 %collective-permute-start.6 = (f32[5,8,256]{2,1,0:T(8,128)S(1)}, f32[5,8,256]{2,1,0:T(8,128)S(1)}, u32[]{:S(2)}, u32[]{:S(2)}) collective-permute-start(f32[5,8,256]{2,1,0:T(8,128)S(1)} %get-tuple-element.60), channel_id=1, source_target_pairs={{0,16},{4,20},{8,24},{12,28},{16,0},{20,4},{24,8},{28,12},{1,17},{... | collective-permute-start | bytes 122888 | tf_op jit(solution)/shard_map/ppermute | solution.py:658
  21.5 0.1 collective-permute-start.4
  21.6 2.6 %collective-permute-done.6.other_ref = f32[5,8,256]{2,1,0:T(8,128)S(1)} collective-permute-done((f32[5,8,256]{2,1,0:T(8,128)S(1)}, f32[5,8,256]{2,1,0:T(8,128)S(1)}, u32[]{:S(2)}, u32[]{:S(2)}) %collective-permute-start.6) | collective-permute-done | bytes 40992 | tf_op jit(solution)/shard_map/ppermute | solution.py:658
  24.3 1.3 %shard_map.82.refs_0_ = f32[4,16,16,256]{3,2,1,0:T(8,128)} custom-call(f32[16,128]{1,0:T(8,128)S(1)} %get-tuple-element.38.tab_ref, s32[16,16,256]{2,1,0:T(8,128)S(1)} %get-tuple-element.39.stratum_ref, f32[4,16,16,256]{3,2,1,0:T(8,128)S(1)} %get-tuple-element.40.conc_ref, f32[16,8,256]{2,1,0:T(8,128)S(1)} %get-tuple-element.62.pass_a_ref, ...), custom_call_target="tpu_custom_call" | custom-call | tf_op jit(solution)/shard_map/pallas_call | solution.py:701
  25.6 1.7 %collective-permute-done.4.other_ref = f32[5,8,256]{2,1,0:T(8,128)S(1)} collective-permute-done((f32[5,8,256]{2,1,0:T(8,128)S(1)}, f32[5,8,256]{2,1,0:T(8,128)S(1)}, u32[]{:S(2)}, u32[]{:S(2)}) %collective-permute-start.4) | collective-permute-done | bytes 40992 | tf_op jit(solution)/shard_map/ppermute | solution.py:658
  27.3 0.0 collective-permute-done.5.closing_ref
  27.3 1.3 %shard_map.83 = f32[4,16,16,256]{3,2,1,0:T(8,128)} custom-call(f32[16,128]{1,0:T(8,128)S(1)} %get-tuple-element.38.tab_ref, s32[16,16,256]{2,1,0:T(8,128)S(1)} %get-tuple-element.39.stratum_ref, f32[4,16,16,256]{3,2,1,0:T(8,128)S(1)} %get-tuple-element.40.conc_ref, f32[16,8,256]{2,1,0:T(8,128)S(1)} %get-tuple-element.41.pass_a_ref, ...), custom_call_target="tpu_custom_call", output_to_operand_aliasing={{}: (13, {})} | custom-call | tf_op jit(solution)/shard_map/pallas_call | solution.py:701
  (4 shorter events, 0.2 us)
Async XLA Ops:
  1.4 5.4 %collective-permute-start = (f32[3,16,256]{2,1,0:T(8,128)S(1)}, f32[3,16,256]{2,1,0:T(8,128)S(1)}, u32[]{:S(2)}, u32[]{:S(2)}) collective-permute-start(f32[3,16,256]{2,1,0:T(8,128)S(1)} %get-tuple-element.49.late_ref), channel_id=1, source_target_pairs={{1,2},{2,1},{0,3},{3,0},{5,6},{6,5},{4,7},{7,4},{9,10},{10,9},{8,1... | collective-permute-start | bytes 147464 | tf_op jit(solution)/shard_map/ppermute | solution.py:652
  3.9 3.0 %collective-permute-start.1 = (f32[3,16,256]{2,1,0:T(8,128)S(1)}, f32[3,16,256]{2,1,0:T(8,128)S(1)}, u32[]{:S(2)}, u32[]{:S(2)}) collective-permute-start(f32[3,16,256]{2,1,0:T(8,128)S(1)} %get-tuple-element.48.early_ref), channel_id=1, source_target_pairs={{0,1},{2,3},{1,0},{3,2},{4,5},{6,7},{5,4},{7,6},{8,9},{10,11},{9,8... | collective-permute-start | bytes 147464 | tf_op jit(solution)/shard_map/ppermute | solution.py:652
  7.1 5.1 %collective-permute-start.2 = (f32[14,8,256]{2,1,0:T(8,128)S(1)}, f32[14,8,256]{2,1,0:T(8,128)S(1)}, u32[]{:S(2)}, u32[]{:S(2)}) collective-permute-start(f32[14,8,256]{2,1,0:T(8,128)S(1)} %get-tuple-element.57), channel_id=1, source_target_pairs={{0,4},{4,0},{8,12},{12,8},{16,20},{20,16},{24,28},{28,24},{1,5},{5... | collective-permute-start | bytes 344072 | tf_op jit(solution)/shard_map/ppermute | solution.py:658
  12.2 4.9 %collective-permute-start.3 = (f32[14,8,256]{2,1,0:T(8,128)S(1)}, f32[14,8,256]{2,1,0:T(8,128)S(1)}, u32[]{:S(2)}, u32[]{:S(2)}) collective-permute-start(f32[14,8,256]{2,1,0:T(8,128)S(1)} %get-tuple-element.58.own_ref), channel_id=1, source_target_pairs={{0,8},{4,12},{8,0},{12,4},{16,24},{20,28},{24,16},{28,20},{1,9},{5... | collective-permute-start | bytes 344072 | tf_op jit(solution)/shard_map/ppermute | solution.py:658
  17.1 10.2 %collective-permute-start.5 = (f32[18,8,256]{2,1,0:T(8,128)S(1)}, f32[18,8,256]{2,1,0:T(8,128)S(1)}, u32[]{:S(2)}, u32[]{:S(2)}) collective-permute-start(f32[18,8,256]{2,1,0:T(8,128)S(1)} %get-tuple-element.61.closing_ref), channel_id=1, source_target_pairs={{0,4},{4,0},{8,12},{12,8},{16,20},{20,16},{24,28},{28,24},{1,5},{5... | collective-permute-start | bytes 442376 | tf_op jit(solution)/shard_map/ppermute | solution.py:658
  18.9 5.3 %collective-permute-start.6 = (f32[5,8,256]{2,1,0:T(8,128)S(1)}, f32[5,8,256]{2,1,0:T(8,128)S(1)}, u32[]{:S(2)}, u32[]{:S(2)}) collective-permute-start(f32[5,8,256]{2,1,0:T(8,128)S(1)} %get-tuple-element.60), channel_id=1, source_target_pairs={{0,16},{4,20},{8,24},{12,28},{16,0},{20,4},{24,8},{28,12},{1,17},{... | collective-permute-start | bytes 122888 | tf_op jit(solution)/shard_map/ppermute | solution.py:658
  21.5 5.8 %collective-permute-start.4 = (f32[5,8,256]{2,1,0:T(8,128)S(1)}, f32[5,8,256]{2,1,0:T(8,128)S(1)}, u32[]{:S(2)}, u32[]{:S(2)}) collective-permute-start(f32[5,8,256]{2,1,0:T(8,128)S(1)} %get-tuple-element.60), channel_id=1, source_target_pairs={{0,20},{4,16},{8,28},{12,24},{16,4},{20,0},{24,12},{28,8},{1,21},{... | collective-permute-start | bytes 122888 | tf_op jit(solution)/shard_map/ppermute | solution.py:658

commit v11 on v9

--- a/solution.py
+++ b/solution.py
@@ -178,13 +178,13 @@
     over_ref,
     source_a_ref,
     source_b_ref,
-    head_a,
-    head_b,
-    kappa_ref,
     left_a,
     right_a,
     left_b,
     right_b,
+    head_a,
+    head_b,
+    kappa_ref,
     adj_l,
     adj_r,
 ):
@@ -443,7 +443,7 @@
             face_ref[0][k] = jnp.where(after, merged[l], merged[r])
 
 
-def close_kernel(strides, own_ref, other_ref, *refs):
+def close_kernel(strides, ready_ref, own_ref, other_ref, *refs):
     kept_refs, mine_ref, send_ref = refs[:-2], refs[-2], refs[-1]
     stride = strides[-1]
     second = side_of("flow", stride)
@@ -475,6 +475,143 @@
         ends = side_ends(after, middle_a, middle_b, ends)
     for q, value in enumerate(ends):
         mine_ref[q] = value
+
+
+def piece_ends(kept_ref, current_ref):
+    ends = [tuple(current_ref[q] for q in range(CURRENTS))]
+    slot = PIECES - 1
+    while len(ends) < PIECES:
+        slot -= len(ends)
+        parts = []
+        for k, (l_a, r_a, l_b, r_b) in enumerate(ends):
+            values = [kept_ref[slot + k, v] for v in range(KEPT)]
+            middle_a, middle_b = between(values, (l_a, r_a, l_b, r_b))
+            parts += [(l_a, -middle_a, l_b, -middle_b), (middle_a, r_a, middle_b, r_b)]
+        ends = parts
+    return ends
+
+
+def prepare_kernel(
+    kept,
+    tab_ref,
+    stratum_ref,
+    conc_ref,
+    pass_a_ref,
+    drop_a_ref,
+    pass_b_ref,
+    drop_b_ref,
+    over_ref,
+    source_a_ref,
+    source_b_ref,
+    flow_ref,
+    left_a,
+    right_a,
+    free_a_ref,
+    free_b_ref,
+    cross_l_ref,
+    cross_r_ref,
+    own_2_ref,
+    own_3_ref,
+    gamma_ref,
+    share_ref,
+    decay_ref,
+):
+    n, planes_y, planes_z = stratum_ref.shape
+    half = planes_y // 2
+    which = half_of(kept)
+    rows = pl.ds(pl.multiple_of(which * half, half), half)
+    number = Numbers(tab_ref)
+    line = lax.broadcasted_iota(jnp.int32, (half, planes_z), 0)
+    outer = line == (half - 1) * which
+    zero = jnp.zeros((half, planes_z), jnp.float32)
+    m = n // PIECES
+
+    def with_border(source, component, i):
+        flow = jnp.broadcast_to(flow_ref[component, i : i + 1, :], source.shape)
+        return source + jnp.where(outer, flow, 0.0)
+
+    def solve(s, forcing, pass_ref, drop_ref, over, out_ref):
+        value, gathered = zero, []
+        for j in range(m):
+            value = forcing(s * m + j) + (pass_ref[s * m + j] * value if j else 0.0)
+            gathered.append(value)
+        x = gathered[-1] * over
+        for j in reversed(range(m)):
+            i = s * m + j
+            if j < m - 1:
+                x = pass_ref[i + 1] * x + drop_ref[i + 1] * gathered[j]
+            out_ref[i] = x
+
+    for i in range(n):
+        index = stratum_ref[i, rows, :]
+        own_2_ref[i] = number("beta", index) * conc_ref[2, i, rows, :]
+        own_3_ref[i] = number("free_b", index) * conc_ref[3, i, rows, :]
+        gamma_ref[i] = number("gamma", index)
+        share_ref[i] = number("share_b", index)
+        decay_ref[i] = number("decay_b", index)
+    for s in range(PIECES):
+        kappa = {}
+        for i in range(s * m, s * m + m):
+            kappa[i] = number("kappa", stratum_ref[i, rows, :])
+        solve(
+            s,
+            lambda i: with_border(source_a_ref[i], 0, i),
+            pass_a_ref,
+            drop_a_ref,
+            over_ref[0, s],
+            free_a_ref,
+        )
+        forcings = (
+            (lambda i: with_border(source_b_ref[i], 1, i) + kappa[i] * free_a_ref[i], free_b_ref),
+            (lambda i: kappa[i] * left_a[i], cross_l_ref),
+            (lambda i: kappa[i] * right_a[i], cross_r_ref),
+        )
+        for forcing, out_ref in forcings:
+            solve(s, forcing, pass_b_ref, drop_b_ref, over_ref[1, s], out_ref)
+
+
+def add_kernel(
+    kept,
+    kept_ref,
+    current_ref,
+    free_a_ref,
+    free_b_ref,
+    cross_l_ref,
+    cross_r_ref,
+    own_2_ref,
+    own_3_ref,
+    gamma_ref,
+    share_ref,
+    decay_ref,
+    left_a,
+    right_a,
+    left_b,
+    right_b,
+    before_hbm,
+    out_hbm,
+    made,
+    sems,
+):
+    n, half, planes_z = free_a_ref.shape
+    rows = pl.ds(pl.multiple_of(half_of(kept) * half, half), half)
+    ends = piece_ends(kept_ref, current_ref)
+    m = n // PIECES
+    copies = []
+    for i in range(n):
+        l_a, r_a, l_b, r_b = ends[i // m]
+        x0 = free_a_ref[i] + left_a[i] * l_a + right_a[i] * r_a
+        x1 = (free_b_ref[i] + cross_l_ref[i] * l_a + cross_r_ref[i] * r_a) + (
+            left_b[i] * l_b + right_b[i] * r_b
+        )
+        x2 = own_2_ref[i] + gamma_ref[i] * x0
+        made[0, i], made[1, i], made[2, i] = x0, x1, x2
+        made[3, i] = own_3_ref[i] + share_ref[i] * x1 + decay_ref[i] * x2
+        copies.append(
+            pltpu.make_async_copy(made.at[:, i], out_hbm.at[:, i, rows, :], sems.at[i])
+        )
+        copies[-1].start()
+    for copy in copies:
+        copy.wait()
 
 
 def final_kernel(
@@ -507,17 +644,7 @@
         flow = jnp.broadcast_to(flow_ref[component, pl.ds(i, 1), :], source.shape)
         return source + jnp.where(outer, flow, 0.0)
 
-    ends = [tuple(current_ref[q] for q in range(CURRENTS))]
-    slot = PIECES - 1
-    while len(ends) < PIECES:
-        slot -= len(ends)
-        parts = []
-        for k, (l_a, r_a, l_b, r_b) in enumerate(ends):
-            values = [kept_ref[slot + k, v] for v in range(KEPT)]
-            middle_a, middle_b = between(values, (l_a, r_a, l_b, r_b))
-            parts += [(l_a, -middle_a, l_b, -middle_b), (middle_a, r_a, middle_b, r_b)]
-        ends = parts
-
+    ends = piece_ends(kept_ref, current_ref)
     pieces = range(PIECES)
     m = n // PIECES
     values = [ends[s][0] for s in pieces]
@@ -657,18 +784,18 @@
                 (6, n, planes_z),
                 *[half_cells] * 4,
                 (2, PIECES, half, planes_z),
-                *[half_cells] * 2,
+                *[half_cells] * 6,
             ],
-            [half_cells] * 9,
+            [half_cells] * 5,
         )(table, stratum, concentration)
         pay, parts, flow = call(
             functools.partial(border_kernel, kept),
             [block_shape, (PIECES - 1, KEPT, half, planes_z), (2, n, planes_z)],
         )(table, early, late, beyond_late, beyond_early, edge, pay)
-        return pay, (*rest, parts, flow)
-
-    send, sent_rest = local(False)
-    block, kept_rest = local(True)
+        return pay, rest[:7], rest[7:], parts, flow
+
+    send, sent_rest, sent_responses, sent_parts, sent_flow = local(False)
+    block, kept_rest, _, kept_parts, kept_flow = local(True)
     kept = []
     for stride in strides[:-1]:
         other = exchange(send, stride)
@@ -679,31 +806,38 @@
         )(block, other)
         kept.append(keep)
         send = face[0] if last else block
-    ends_shape = (CURRENTS, half, planes_z)
-    mine, send = call(functools.partial(close_kernel, strides), [ends_shape, ends_shape])(
-        block, exchange(send, strides[-1]), *kept
+    prepared = call(functools.partial(prepare_kernel, False), [half_cells] * 9)(
+        table, stratum, concentration, *sent_rest, sent_flow, *sent_responses[:2]
     )
+    ends_shape = jax.ShapeDtypeStruct((CURRENTS, half, planes_z), jnp.float32)
+    vmem = pl.BlockSpec(memory_space=pltpu.VMEM)
+    limit = pltpu.CompilerParams(vmem_limit_bytes=VMEM_LIMIT)
+    mine, send = pl.pallas_call(
+        functools.partial(close_kernel, strides),
+        out_shape=[ends_shape, ends_shape],
+        in_specs=[pl.BlockSpec(memory_space=pl.ANY)] + [vmem] * (2 + len(kept)),
+        compiler_params=limit,
+    )(prepared[0], block, exchange(send, strides[-1]), *kept)
     currents = exchange(send, 1)
-    def final(kept, rest, currents, *before):
-        whole = jax.ShapeDtypeStruct((4,) + cells, jnp.float32)
-        vmem = pl.BlockSpec(memory_space=pltpu.VMEM)
-        return pl.pallas_call(
-            functools.partial(final_kernel, kept),
-            out_shape=whole,
-            in_specs=[vmem] * 13 + [hbm] * len(before),
-            out_specs=hbm,
-            scratch_shapes=[
-                pltpu.VMEM(half_cells, jnp.float32),
-                pltpu.VMEM(half_cells, jnp.float32),
-                pltpu.VMEM((4,) + half_cells, jnp.float32),
-                pltpu.SemaphoreType.DMA((n,)),
-            ],
-            input_output_aliases={13: 0} if before else {},
-            compiler_params=pltpu.CompilerParams(vmem_limit_bytes=VMEM_LIMIT),
-        )(table, stratum, concentration, *rest, currents, *before)
-
-    out = final(True, kept_rest, mine)
-    return final(False, sent_rest, currents, out)
+    whole = jax.ShapeDtypeStruct((4,) + cells, jnp.float32)
+    results = [pltpu.VMEM((4,) + half_cells, jnp.float32), pltpu.SemaphoreType.DMA((n,))]
+    out = pl.pallas_call(
+        functools.partial(final_kernel, True),
+        out_shape=whole,
+        in_specs=[vmem] * 13,
+        out_specs=hbm,
+        scratch_shapes=[pltpu.VMEM(half_cells, jnp.float32)] * 2 + results,
+        compiler_params=limit,
+    )(table, stratum, concentration, *kept_rest, kept_parts, kept_flow, mine)
+    return pl.pallas_call(
+        functools.partial(add_kernel, False),
+        out_shape=whole,
+        in_specs=[vmem] * 15 + [hbm],
+        out_specs=hbm,
+        scratch_shapes=results,
+        input_output_aliases={15: 0},
+        compiler_params=limit,
+    )(sent_parts, currents, *prepared, *sent_responses, out)
 
 
 def solution(mesh):

time: 27.6 us -> 27.3 us (0.989)
  Pallas kernels: 9.09 us -> 9.93 us
  waiting for transfers between devices: 7.1 us -> 6.49 us
  starting transfers between devices: 11.2 us -> 10.7 us
    pallas_call x2, Pallas kernels: 4.57 us -> 5.22 us  [local(): call(functools.partial(local_kernel, kept), [(PIECES,) + block_shape, (6,...]
    ppermute x4, waiting for transfers between devices: 7.09 us -> 6.49 us  [exchange(): return lax.ppermute(value, 'flow', [(i, i ^ stride) for i in range(peers)])]
    ppermute x4, starting transfers between devices: 8.05 us -> 7.56 us  [exchange(): return lax.ppermute(value, 'flow', [(i, i ^ stride) for i in range(peers)])]
    pallas_call x3 -> x4, Pallas kernels: 2.63 us -> 2.84 us  [the longest x1 1.29 us: per_device(): pl.pallas_call(functools.partial(final_kernel, True), out_shape=whole, in...]
  transfers between devices with their start and end apart: 6 -> 6, of which waited for: 4 -> 4; matrix products, arithmetic and copies ran while one was open for 0% -> 0% of each run, Pallas kernels for 22% -> 26%
where the time goes in v11:
time: 27.3 us; the launch traced here: 27.2 us
  starting transfers between devices  10.7 us (39%)
  Pallas kernels  9.93 us (36%)
  waiting for transfers between devices  6.49 us (24%)
    ppermute x4, starting transfers between devices, exchange(): return lax.ppermute(value, 'flow', [(i, i ^ stride) for i in range(peers)])  7.56 us
    ppermute x4, waiting for transfers between devices, exchange(): return lax.ppermute(value, 'flow', [(i, i ^ stride) for i in range(peers)])  6.49 us
    pallas_call x2, Pallas kernels, local(): call(functools.partial(local_kernel, kept), [(PIECES,) + block_shape, (6,...  5.22 us
    ppermute x2, starting transfers between devices, swap(): return lax.ppermute(value, 'trans', pairs)  3.13 us
    pallas_call x1, Pallas kernels, per_device(): pl.pallas_call(pack_kernel, out_shape=[jax.ShapeDtypeStruct(halo, jnp.flo...  1.43 us
    pallas_call x1, Pallas kernels, per_device(): pl.pallas_call(functools.partial(final_kernel, True), out_shape=whole, in...  1.29 us
    pallas_call x1, Pallas kernels, per_device(): pl.pallas_call(functools.partial(add_kernel, False), out_shape=whole, in_...  0.99 us
  transfers between devices with their start and end apart: 6, of which 4 were waited for; matrix products, arithmetic and copies ran while one was open for 0% of the time, Pallas kernels for 26%

profile of v11, /device:TPU:0, one launch (start us, length us, event | category | flops | bytes accessed | tf_op | source)
XLA Modules:
  0.0 27.2 jit_solution(8133815980601823485)
XLA Ops:
  0.0 1.4 %shard_map.73 = (f32[3,16,256]{2,1,0:T(8,128)S(1)}, f32[3,16,256]{2,1,0:T(8,128)S(1)}, f32[16,128]{1,0:T(8,128)S(1)}, f32[4,16,16,256]{3,2,1,0:T(8,128)S(1)}, s32[16,16,256]{2,1,0:T(8,128)S(1)}) custom-call(f32[4,16,16,256]{3,2,1,0:T(8,128)} %conc_hbm.1, s32[16,16,256]{2,1,0:T(8,128)} %stratum_hbm.1, f32[1,16]{1,0:T(1,128)} %bitcast.6, f32[2,16]{1,0:T(2,128)} %bitcast.5, ...), custom_call_target="tpu_custom_call" | custom-call | tf_op jit(solution)/shard_map/pallas_call | solution.py:728
  1.4 0.5 %collective-permute-start.1 = (f32[3,16,256]{2,1,0:T(8,128)S(1)}, f32[3,16,256]{2,1,0:T(8,128)S(1)}, u32[]{:S(2)}, u32[]{:S(2)}) collective-permute-start(f32[3,16,256]{2,1,0:T(8,128)S(1)} %get-tuple-element.55.early_ref), channel_id=1, source_target_pairs={{0,1},{2,3},{1,0},{3,2},{4,5},{6,7},{5,4},{7,6},{8,9},{10,11},{9,8... | collective-permute-start | bytes 147464 | tf_op jit(solution)/shard_map/ppermute | solution.py:768
  2.0 2.6 %collective-permute-start = (f32[3,16,256]{2,1,0:T(8,128)S(1)}, f32[3,16,256]{2,1,0:T(8,128)S(1)}, u32[]{:S(2)}, u32[]{:S(2)}) collective-permute-start(f32[3,16,256]{2,1,0:T(8,128)S(1)} %get-tuple-element.56.late_ref), channel_id=1, source_target_pairs={{1,2},{2,1},{0,3},{3,0},{5,6},{6,5},{4,7},{7,4},{9,10},{10,9},{8,1... | collective-permute-start | bytes 147464 | tf_op jit(solution)/shard_map/ppermute | solution.py:768
  4.6 2.3 %shard_map.74 = (f32[4,14,8,256]{3,2,1,0:T(8,128)S(1)}, f32[6,16,256]{2,1,0:T(8,128)S(1)}, f32[16,8,256]{2,1,0:T(8,128)S(1)}, f32[16,8,256]{2,1,0:T(8,128)S(1)},...) custom-call(f32[16,128]{1,0:T(8,128)S(1)} %get-tuple-element.54.tab_, ...), custom_call_target="tpu_custom_call" | custom-call | tf_op jit(solution)/shard_map/pallas_call | solution.py:780
  6.9 0.0 collective-permute-done.1.beyond_early_ref
  6.9 0.0 collective-permute-done.beyond_late_ref
  6.9 0.2 shard_map.75
  7.1 1.6 %collective-permute-start.2 = (f32[14,8,256]{2,1,0:T(8,128)S(1)}, f32[14,8,256]{2,1,0:T(8,128)S(1)}, u32[]{:S(2)}, u32[]{:S(2)}) collective-permute-start(f32[14,8,256]{2,1,0:T(8,128)S(1)} %get-tuple-element.76), channel_id=1, source_target_pairs={{0,4},{4,0},{8,12},{12,8},{16,20},{20,16},{24,28},{28,24},{1,5},{5... | collective-permute-start | bytes 344072 | tf_op jit(solution)/shard_map/ppermute | solution.py:774
  8.7 2.9 %shard_map.77 = (f32[4,14,8,256]{3,2,1,0:T(8,128)S(1)}, f32[6,16,256]{2,1,0:T(8,128)S(1)}, f32[16,8,256]{2,1,0:T(8,128)S(1)}, f32[16,8,256]{2,1,0:T(8,128)S(1)},...) custom-call(f32[16,128]{1,0:T(8,128)S(1)} %get-tuple-element.54.tab_, ...), custom_call_target="tpu_custom_call" | custom-call | tf_op jit(solution)/shard_map/pallas_call | solution.py:780
  11.6 0.2 shard_map.78
  11.8 0.5 %collective-permute-done.2.other_ref = f32[14,8,256]{2,1,0:T(8,128)S(1)} collective-permute-done((f32[14,8,256]{2,1,0:T(8,128)S(1)}, f32[14,8,256]{2,1,0:T(8,128)S(1)}, u32[]{:S(2)}, u32[]{:S(2)}) %collective-permute-start.2) | collective-permute-done | bytes 114720 | tf_op jit(solution)/shard_map/ppermute | solution.py:774
  12.3 1.7 %collective-permute-start.3 = (f32[14,8,256]{2,1,0:T(8,128)S(1)}, f32[14,8,256]{2,1,0:T(8,128)S(1)}, u32[]{:S(2)}, u32[]{:S(2)}) collective-permute-start(f32[14,8,256]{2,1,0:T(8,128)S(1)} %get-tuple-element.77.own_ref), channel_id=1, source_target_pairs={{0,8},{4,12},{8,0},{12,4},{16,24},{20,28},{24,16},{28,20},{1,9},{5... | collective-permute-start | bytes 344072 | tf_op jit(solution)/shard_map/ppermute | solution.py:774
  14.0 3.2 %collective-permute-done.3.other_ref = f32[14,8,256]{2,1,0:T(8,128)S(1)} collective-permute-done((f32[14,8,256]{2,1,0:T(8,128)S(1)}, f32[14,8,256]{2,1,0:T(8,128)S(1)}, u32[]{:S(2)}, u32[]{:S(2)}) %collective-permute-start.3) | collective-permute-done | bytes 114720 | tf_op jit(solution)/shard_map/ppermute | solution.py:774
  17.2 2.7 %collective-permute-start.4 = (f32[5,8,256]{2,1,0:T(8,128)S(1)}, f32[5,8,256]{2,1,0:T(8,128)S(1)}, u32[]{:S(2)}, u32[]{:S(2)}) collective-permute-start(f32[5,8,256]{2,1,0:T(8,128)S(1)} %get-tuple-element.79), channel_id=1, source_target_pairs={{0,16},{4,20},{8,24},{12,28},{16,0},{20,4},{24,8},{28,12},{1,17},{... | collective-permute-start | bytes 122888 | tf_op jit(solution)/shard_map/ppermute | solution.py:774
  19.9 0.5 %shard_map.76 = (f32[16,8,256]{2,1,0:T(8,128)S(1)}, f32[16,8,256]{2,1,0:T(8,128)S(1)}, f32[16,8,256]{2,1,0:T(8,128)S(1)}, f32[16,8,256]{2,1,0:T(8,128)S(1)}, f32...) custom-call(f32[16,128]{1,0:T(8,128)S(1)} %get-tuple-element.54.tab_, ...), custom_call_target="tpu_custom_call" | custom-call | tf_op jit(solution)/shard_map/pallas_call | solution.py:809
  20.4 1.7 %collective-permute-done.4.other_ref = f32[5,8,256]{2,1,0:T(8,128)S(1)} collective-permute-done((f32[5,8,256]{2,1,0:T(8,128)S(1)}, f32[5,8,256]{2,1,0:T(8,128)S(1)}, u32[]{:S(2)}, u32[]{:S(2)}) %collective-permute-start.4) | collective-permute-done | bytes 40992 | tf_op jit(solution)/shard_map/ppermute | solution.py:774
  22.2 1.6 %collective-permute-start.5 = (f32[4,8,256]{2,1,0:T(8,128)S(1)}, f32[4,8,256]{2,1,0:T(8,128)S(1)}, u32[]{:S(2)}, u32[]{:S(2)}) collective-permute-start(f32[4,8,256]{2,1,0:T(8,128)S(1)} %get-tuple-element.82), channel_id=1, source_target_pairs={{0,4},{4,0},{8,12},{12,8},{16,20},{20,16},{24,28},{28,24},{1,5},{5... | collective-permute-start | bytes 98312 | tf_op jit(solution)/shard_map/ppermute | solution.py:774
  23.8 1.3 %shard_map.82.before_hbm = f32[4,16,16,256]{3,2,1,0:T(8,128)} custom-call(f32[16,128]{1,0:T(8,128)S(1)} %get-tuple-element.54.tab_ref, s32[16,16,256]{2,1,0:T(8,128)S(1)} %get-tuple-element.57.stratum_ref, f32[4,16,16,256]{3,2,1,0:T(8,128)S(1)} %get-tuple-element.58.conc_ref, f32[16,8,256]{2,1,0:T(8,128)S(1)} %get-tuple-element.93.pass_a_ref, ...), custom_call_target="tpu_custom_call" | custom-call | tf_op jit(solution)/shard_map/pallas_call | solution.py:824
  25.1 1.1 %collective-permute-done.5.current_ref = f32[4,8,256]{2,1,0:T(8,128)S(1)} collective-permute-done((f32[4,8,256]{2,1,0:T(8,128)S(1)}, f32[4,8,256]{2,1,0:T(8,128)S(1)}, u32[]{:S(2)}, u32[]{:S(2)}) %collective-permute-start.5) | collective-permute-done | bytes 32800 | tf_op jit(solution)/shard_map/ppermute | solution.py:774
  26.2 1.0 %shard_map.83 = f32[4,16,16,256]{3,2,1,0:T(8,128)} custom-call(f32[3,8,8,256]{3,2,1,0:T(8,128)S(1)} %get-tuple-element.61.kept_ref, f32[4,8,256]{2,1,0:T(8,128)S(1)} %collective-permute-done.5.current_ref, f32[16,8,256]{2,1,0:T(8,128)S(1)} %get-tuple-element.72.ready_ref.free_a_ref, ...), custom_call_target="tpu_custom_call", output_to_operand_aliasing={{}: (15, {})} | custom-call | tf_op jit(solution)/shard_map/pallas_call | solution.py:832
  (3 shorter events, 0.1 us)
Async XLA Ops:
  1.4 5.4 %collective-permute-start.1 = (f32[3,16,256]{2,1,0:T(8,128)S(1)}, f32[3,16,256]{2,1,0:T(8,128)S(1)}, u32[]{:S(2)}, u32[]{:S(2)}) collective-permute-start(f32[3,16,256]{2,1,0:T(8,128)S(1)} %get-tuple-element.55.early_ref), channel_id=1, source_target_pairs={{0,1},{2,3},{1,0},{3,2},{4,5},{6,7},{5,4},{7,6},{8,9},{10,11},{9,8... | collective-permute-start | bytes 147464 | tf_op jit(solution)/shard_map/ppermute | solution.py:768
  2.0 4.9 %collective-permute-start = (f32[3,16,256]{2,1,0:T(8,128)S(1)}, f32[3,16,256]{2,1,0:T(8,128)S(1)}, u32[]{:S(2)}, u32[]{:S(2)}) collective-permute-start(f32[3,16,256]{2,1,0:T(8,128)S(1)} %get-tuple-element.56.late_ref), channel_id=1, source_target_pairs={{1,2},{2,1},{0,3},{3,0},{5,6},{6,5},{4,7},{7,4},{9,10},{10,9},{8,1... | collective-permute-start | bytes 147464 | tf_op jit(solution)/shard_map/ppermute | solution.py:768
  7.1 5.2 %collective-permute-start.2 = (f32[14,8,256]{2,1,0:T(8,128)S(1)}, f32[14,8,256]{2,1,0:T(8,128)S(1)}, u32[]{:S(2)}, u32[]{:S(2)}) collective-permute-start(f32[14,8,256]{2,1,0:T(8,128)S(1)} %get-tuple-element.76), channel_id=1, source_target_pairs={{0,4},{4,0},{8,12},{12,8},{16,20},{20,16},{24,28},{28,24},{1,5},{5... | collective-permute-start | bytes 344072 | tf_op jit(solution)/shard_map/ppermute | solution.py:774
  12.3 4.9 %collective-permute-start.3 = (f32[14,8,256]{2,1,0:T(8,128)S(1)}, f32[14,8,256]{2,1,0:T(8,128)S(1)}, u32[]{:S(2)}, u32[]{:S(2)}) collective-permute-start(f32[14,8,256]{2,1,0:T(8,128)S(1)} %get-tuple-element.77.own_ref), channel_id=1, source_target_pairs={{0,8},{4,12},{8,0},{12,4},{16,24},{20,28},{24,16},{28,20},{1,9},{5... | collective-permute-start | bytes 344072 | tf_op jit(solution)/shard_map/ppermute | solution.py:774
  17.2 5.0 %collective-permute-start.4 = (f32[5,8,256]{2,1,0:T(8,128)S(1)}, f32[5,8,256]{2,1,0:T(8,128)S(1)}, u32[]{:S(2)}, u32[]{:S(2)}) collective-permute-start(f32[5,8,256]{2,1,0:T(8,128)S(1)} %get-tuple-element.79), channel_id=1, source_target_pairs={{0,16},{4,20},{8,24},{12,28},{16,0},{20,4},{24,8},{28,12},{1,17},{... | collective-permute-start | bytes 122888 | tf_op jit(solution)/shard_map/ppermute | solution.py:774
  22.2 4.0 %collective-permute-start.5 = (f32[4,8,256]{2,1,0:T(8,128)S(1)}, f32[4,8,256]{2,1,0:T(8,128)S(1)}, u32[]{:S(2)}, u32[]{:S(2)}) collective-permute-start(f32[4,8,256]{2,1,0:T(8,128)S(1)} %get-tuple-element.82), channel_id=1, source_target_pairs={{0,4},{4,0},{8,12},{12,8},{16,20},{20,16},{24,28},{28,24},{1,5},{5... | collective-permute-start | bytes 98312 | tf_op jit(solution)/shard_map/ppermute | solution.py:774

commit v12 on v11

--- a/solution.py
+++ b/solution.py
@@ -764,7 +764,7 @@
         low = range(start, groups - 1, 2)
         pairs = [(i, i + 1) for i in low] + [(i + 1, i) for i in low]
         if start:
-            pairs += [(0, groups - 1), (groups - 1, 0)]
+            pairs += [(0, 0), (groups - 1, groups - 1)]
         return lax.ppermute(value, "trans", pairs)
 
     beyond_late = swap(late, 1)

time: 27.3 us -> 27.6 us (1.011)
  the two profiles are of different devices: /device:TPU:0 before, /device:TPU:18 now
where the time goes in v12:
time: 27.6 us; the launch traced here: 27.4 us
  waiting for transfers between devices  10.4 us (38%)
  Pallas kernels  9.95 us (36%)
  starting transfers between devices  7 us (25%)
    ppermute x4, waiting for transfers between devices, exchange(): return lax.ppermute(value, 'flow', [(i, i ^ stride) for i in range(peers)])  9.83 us
    pallas_call x2, Pallas kernels, local(): call(functools.partial(local_kernel, kept), [(PIECES,) + block_shape, (6,...  5.23 us
    ppermute x4, starting transfers between devices, exchange(): return lax.ppermute(value, 'flow', [(i, i ^ stride) for i in range(peers)])  4.4 us
    ppermute x2, starting transfers between devices, swap(): return lax.ppermute(value, 'trans', pairs)  2.6 us
    pallas_call x1, Pallas kernels, per_device(): pl.pallas_call(pack_kernel, out_shape=[jax.ShapeDtypeStruct(halo, jnp.flo...  1.43 us
    pallas_call x1, Pallas kernels, per_device(): pl.pallas_call(functools.partial(final_kernel, True), out_shape=whole, in...  1.29 us
    pallas_call x1, Pallas kernels, per_device(): pl.pallas_call(functools.partial(add_kernel, False), out_shape=whole, in_...  0.99 us
    ppermute x2, waiting for transfers between devices, swap(): return lax.ppermute(value, 'trans', pairs)  0.56 us
  transfers between devices with their start and end apart: 6, of which 5 were waited for; matrix products, arithmetic and copies ran while one was open for 0% of the time, Pallas kernels for 26%

profile of v12, /device:TPU:18, one launch (start us, length us, event | category | flops | bytes accessed | tf_op | source)
XLA Modules:
  0.0 27.4 jit_solution(8113949557325378312)
XLA Ops:
  0.0 1.4 %shard_map.73 = (f32[3,16,256]{2,1,0:T(8,128)S(1)}, f32[3,16,256]{2,1,0:T(8,128)S(1)}, f32[16,128]{1,0:T(8,128)S(1)}, f32[4,16,16,256]{3,2,1,0:T(8,128)S(1)}, s32[16,16,256]{2,1,0:T(8,128)S(1)}) custom-call(f32[4,16,16,256]{3,2,1,0:T(8,128)} %conc_hbm.1, s32[16,16,256]{2,1,0:T(8,128)} %stratum_hbm.1, f32[1,16]{1,0:T(1,128)} %bitcast.6, f32[2,16]{1,0:T(2,128)} %bitcast.5, ...), custom_call_target="tpu_custom_call" | custom-call | tf_op jit(solution)/shard_map/pallas_call | solution.py:728
  1.4 0.1 collective-permute-start.1
  1.5 2.5 %collective-permute-start = (f32[3,16,256]{2,1,0:T(8,128)S(1)}, f32[3,16,256]{2,1,0:T(8,128)S(1)}, u32[]{:S(2)}, u32[]{:S(2)}) collective-permute-start(f32[3,16,256]{2,1,0:T(8,128)S(1)} %get-tuple-element.56.late_ref), channel_id=1, source_target_pairs={{1,2},{2,1},{0,0},{3,3},{5,6},{6,5},{4,4},{7,7},{9,10},{10,9},{8,8... | collective-permute-start | bytes 147464 | tf_op jit(solution)/shard_map/ppermute | solution.py:768
  4.1 2.3 %shard_map.74 = (f32[4,14,8,256]{3,2,1,0:T(8,128)S(1)}, f32[6,16,256]{2,1,0:T(8,128)S(1)}, f32[16,8,256]{2,1,0:T(8,128)S(1)}, f32[16,8,256]{2,1,0:T(8,128)S(1)},...) custom-call(f32[16,128]{1,0:T(8,128)S(1)} %get-tuple-element.54.tab_, ...), custom_call_target="tpu_custom_call" | custom-call | tf_op jit(solution)/shard_map/pallas_call | solution.py:780
  6.4 0.0 collective-permute-done.1.beyond_early_ref
  6.4 0.6 %collective-permute-done.beyond_late_ref = f32[3,16,256]{2,1,0:T(8,128)S(1)} collective-permute-done((f32[3,16,256]{2,1,0:T(8,128)S(1)}, f32[3,16,256]{2,1,0:T(8,128)S(1)}, u32[]{:S(2)}, u32[]{:S(2)}) %collective-permute-start) | collective-permute-done | bytes 49184 | tf_op jit(solution)/shard_map/ppermute | solution.py:768
  6.9 0.2 shard_map.75
  7.1 1.6 %collective-permute-start.2 = (f32[14,8,256]{2,1,0:T(8,128)S(1)}, f32[14,8,256]{2,1,0:T(8,128)S(1)}, u32[]{:S(2)}, u32[]{:S(2)}) collective-permute-start(f32[14,8,256]{2,1,0:T(8,128)S(1)} %get-tuple-element.76), channel_id=1, source_target_pairs={{0,4},{4,0},{8,12},{12,8},{16,20},{20,16},{24,28},{28,24},{1,5},{5... | collective-permute-start | bytes 344072 | tf_op jit(solution)/shard_map/ppermute | solution.py:774
  8.7 2.9 %shard_map.77 = (f32[4,14,8,256]{3,2,1,0:T(8,128)S(1)}, f32[6,16,256]{2,1,0:T(8,128)S(1)}, f32[16,8,256]{2,1,0:T(8,128)S(1)}, f32[16,8,256]{2,1,0:T(8,128)S(1)},...) custom-call(f32[16,128]{1,0:T(8,128)S(1)} %get-tuple-element.54.tab_, ...), custom_call_target="tpu_custom_call" | custom-call | tf_op jit(solution)/shard_map/pallas_call | solution.py:780
  11.6 0.2 shard_map.78
  11.8 0.2 collective-permute-done.2.other_ref
  12.0 1.6 %collective-permute-start.3 = (f32[14,8,256]{2,1,0:T(8,128)S(1)}, f32[14,8,256]{2,1,0:T(8,128)S(1)}, u32[]{:S(2)}, u32[]{:S(2)}) collective-permute-start(f32[14,8,256]{2,1,0:T(8,128)S(1)} %get-tuple-element.77.own_ref), channel_id=1, source_target_pairs={{0,8},{4,12},{8,0},{12,4},{16,24},{20,28},{24,16},{28,20},{1,9},{5... | collective-permute-start | bytes 344072 | tf_op jit(solution)/shard_map/ppermute | solution.py:774
  13.6 3.7 %collective-permute-done.3.other_ref = f32[14,8,256]{2,1,0:T(8,128)S(1)} collective-permute-done((f32[14,8,256]{2,1,0:T(8,128)S(1)}, f32[14,8,256]{2,1,0:T(8,128)S(1)}, u32[]{:S(2)}, u32[]{:S(2)}) %collective-permute-start.3) | collective-permute-done | bytes 114720 | tf_op jit(solution)/shard_map/ppermute | solution.py:774
  17.3 0.1 collective-permute-start.4
  17.4 0.5 %shard_map.76 = (f32[16,8,256]{2,1,0:T(8,128)S(1)}, f32[16,8,256]{2,1,0:T(8,128)S(1)}, f32[16,8,256]{2,1,0:T(8,128)S(1)}, f32[16,8,256]{2,1,0:T(8,128)S(1)}, f32...) custom-call(f32[16,128]{1,0:T(8,128)S(1)} %get-tuple-element.54.tab_, ...), custom_call_target="tpu_custom_call" | custom-call | tf_op jit(solution)/shard_map/pallas_call | solution.py:809
  18.0 4.4 %collective-permute-done.4.other_ref = f32[5,8,256]{2,1,0:T(8,128)S(1)} collective-permute-done((f32[5,8,256]{2,1,0:T(8,128)S(1)}, f32[5,8,256]{2,1,0:T(8,128)S(1)}, u32[]{:S(2)}, u32[]{:S(2)}) %collective-permute-start.4) | collective-permute-done | bytes 40992 | tf_op jit(solution)/shard_map/ppermute | solution.py:774
  22.5 1.1 %collective-permute-start.5 = (f32[4,8,256]{2,1,0:T(8,128)S(1)}, f32[4,8,256]{2,1,0:T(8,128)S(1)}, u32[]{:S(2)}, u32[]{:S(2)}) collective-permute-start(f32[4,8,256]{2,1,0:T(8,128)S(1)} %get-tuple-element.82), channel_id=1, source_target_pairs={{0,4},{4,0},{8,12},{12,8},{16,20},{20,16},{24,28},{28,24},{1,5},{5... | collective-permute-start | bytes 98312 | tf_op jit(solution)/shard_map/ppermute | solution.py:774
  23.6 1.3 %shard_map.82.before_hbm = f32[4,16,16,256]{3,2,1,0:T(8,128)} custom-call(f32[16,128]{1,0:T(8,128)S(1)} %get-tuple-element.54.tab_ref, s32[16,16,256]{2,1,0:T(8,128)S(1)} %get-tuple-element.57.stratum_ref, f32[4,16,16,256]{3,2,1,0:T(8,128)S(1)} %get-tuple-element.58.conc_ref, f32[16,8,256]{2,1,0:T(8,128)S(1)} %get-tuple-element.93.pass_a_ref, ...), custom_call_target="tpu_custom_call" | custom-call | tf_op jit(solution)/shard_map/pallas_call | solution.py:824
  24.9 1.6 %collective-permute-done.5.current_ref = f32[4,8,256]{2,1,0:T(8,128)S(1)} collective-permute-done((f32[4,8,256]{2,1,0:T(8,128)S(1)}, f32[4,8,256]{2,1,0:T(8,128)S(1)}, u32[]{:S(2)}, u32[]{:S(2)}) %collective-permute-start.5) | collective-permute-done | bytes 32800 | tf_op jit(solution)/shard_map/ppermute | solution.py:774
  26.4 1.0 %shard_map.83 = f32[4,16,16,256]{3,2,1,0:T(8,128)} custom-call(f32[3,8,8,256]{3,2,1,0:T(8,128)S(1)} %get-tuple-element.61.kept_ref, f32[4,8,256]{2,1,0:T(8,128)S(1)} %collective-permute-done.5.current_ref, f32[16,8,256]{2,1,0:T(8,128)S(1)} %get-tuple-element.72.ready_ref.free_a_ref, ...), custom_call_target="tpu_custom_call", output_to_operand_aliasing={{}: (15, {})} | custom-call | tf_op jit(solution)/shard_map/pallas_call | solution.py:832
  (3 shorter events, 0.1 us)
Async XLA Ops:
  1.4 4.9 %collective-permute-start.1 = (f32[3,16,256]{2,1,0:T(8,128)S(1)}, f32[3,16,256]{2,1,0:T(8,128)S(1)}, u32[]{:S(2)}, u32[]{:S(2)}) collective-permute-start(f32[3,16,256]{2,1,0:T(8,128)S(1)} %get-tuple-element.55.early_ref), channel_id=1, source_target_pairs={{0,1},{2,3},{1,0},{3,2},{4,5},{6,7},{5,4},{7,6},{8,9},{10,11},{9,8... | collective-permute-start | bytes 147464 | tf_op jit(solution)/shard_map/ppermute | solution.py:768
  1.5 5.4 %collective-permute-start = (f32[3,16,256]{2,1,0:T(8,128)S(1)}, f32[3,16,256]{2,1,0:T(8,128)S(1)}, u32[]{:S(2)}, u32[]{:S(2)}) collective-permute-start(f32[3,16,256]{2,1,0:T(8,128)S(1)} %get-tuple-element.56.late_ref), channel_id=1, source_target_pairs={{1,2},{2,1},{0,0},{3,3},{5,6},{6,5},{4,4},{7,7},{9,10},{10,9},{8,8... | collective-permute-start | bytes 147464 | tf_op jit(solution)/shard_map/ppermute | solution.py:768
  7.1 4.9 %collective-permute-start.2 = (f32[14,8,256]{2,1,0:T(8,128)S(1)}, f32[14,8,256]{2,1,0:T(8,128)S(1)}, u32[]{:S(2)}, u32[]{:S(2)}) collective-permute-start(f32[14,8,256]{2,1,0:T(8,128)S(1)} %get-tuple-element.76), channel_id=1, source_target_pairs={{0,4},{4,0},{8,12},{12,8},{16,20},{20,16},{24,28},{28,24},{1,5},{5... | collective-permute-start | bytes 344072 | tf_op jit(solution)/shard_map/ppermute | solution.py:774
  12.0 5.3 %collective-permute-start.3 = (f32[14,8,256]{2,1,0:T(8,128)S(1)}, f32[14,8,256]{2,1,0:T(8,128)S(1)}, u32[]{:S(2)}, u32[]{:S(2)}) collective-permute-start(f32[14,8,256]{2,1,0:T(8,128)S(1)} %get-tuple-element.77.own_ref), channel_id=1, source_target_pairs={{0,8},{4,12},{8,0},{12,4},{16,24},{20,28},{24,16},{28,20},{1,9},{5... | collective-permute-start | bytes 344072 | tf_op jit(solution)/shard_map/ppermute | solution.py:774
  17.3 5.1 %collective-permute-start.4 = (f32[5,8,256]{2,1,0:T(8,128)S(1)}, f32[5,8,256]{2,1,0:T(8,128)S(1)}, u32[]{:S(2)}, u32[]{:S(2)}) collective-permute-start(f32[5,8,256]{2,1,0:T(8,128)S(1)} %get-tuple-element.79), channel_id=1, source_target_pairs={{0,16},{4,20},{8,24},{12,28},{16,0},{20,4},{24,8},{28,12},{1,17},{... | collective-permute-start | bytes 122888 | tf_op jit(solution)/shard_map/ppermute | solution.py:774
  22.5 4.0 %collective-permute-start.5 = (f32[4,8,256]{2,1,0:T(8,128)S(1)}, f32[4,8,256]{2,1,0:T(8,128)S(1)}, u32[]{:S(2)}, u32[]{:S(2)}) collective-permute-start(f32[4,8,256]{2,1,0:T(8,128)S(1)} %get-tuple-element.82), channel_id=1, source_target_pairs={{0,4},{4,0},{8,12},{12,8},{16,20},{20,16},{24,28},{28,24},{1,5},{5... | collective-permute-start | bytes 98312 | tf_op jit(solution)/shard_map/ppermute | solution.py:774

commit v13 on v12

--- a/solution.py
+++ b/solution.py
@@ -761,11 +761,15 @@
     )
     groups = lax.axis_size("trans")
     def swap(value, start):
-        low = range(start, groups - 1, 2)
-        pairs = [(i, i + 1) for i in low] + [(i + 1, i) for i in low]
-        if start:
-            pairs += [(0, 0), (groups - 1, groups - 1)]
-        return lax.ppermute(value, "trans", pairs)
+        pairs = []
+        for f in range(peers):
+            for t in range(groups):
+                other = t + 1 if (t - start) % 2 == 0 else t - 1
+                if 0 <= other < groups:
+                    pairs.append((f * groups + t, f * groups + other))
+                else:
+                    pairs.append((f * groups + t, (f ^ 1) * groups + t))
+        return lax.ppermute(value, ("flow", "trans"), pairs)
 
     beyond_late = swap(late, 1)
     beyond_early = swap(early, 0)

time: 27.6 us -> 27.4 us (level)
  the two profiles are of different devices: /device:TPU:18 before, /device:TPU:0 now
where the time goes in v13:
time: 27.4 us; the launch traced here: 27.2 us
  starting transfers between devices  11.5 us (42%)
  Pallas kernels  9.93 us (36%)
  waiting for transfers between devices  5.75 us (21%)
    ppermute x4, starting transfers between devices, exchange(): return lax.ppermute(value, 'flow', [(i, i ^ stride) for i in range(peers)])  8.37 us
    ppermute x4, waiting for transfers between devices, exchange(): return lax.ppermute(value, 'flow', [(i, i ^ stride) for i in range(peers)])  5.75 us
    pallas_call x2, Pallas kernels, local(): call(functools.partial(local_kernel, kept), [(PIECES,) + block_shape, (6,...  5.22 us
    ppermute x2, starting transfers between devices, swap(): return lax.ppermute(value, ('flow', 'trans'), pairs)  3.11 us
    pallas_call x1, Pallas kernels, per_device(): pl.pallas_call(pack_kernel, out_shape=[jax.ShapeDtypeStruct(halo, jnp.flo...  1.43 us
    pallas_call x1, Pallas kernels, per_device(): pl.pallas_call(functools.partial(final_kernel, True), out_shape=whole, in...  1.29 us
    pallas_call x1, Pallas kernels, per_device(): pl.pallas_call(functools.partial(add_kernel, False), out_shape=whole, in_...  0.99 us
  transfers between devices with their start and end apart: 6, of which 4 were waited for; matrix products, arithmetic and copies ran while one was open for 0% of the time, Pallas kernels for 26%

profile of v13, /device:TPU:0, one launch (start us, length us, event | category | flops | bytes accessed | tf_op | source)
XLA Modules:
  0.0 27.2 jit_solution(1810338444970139487)
XLA Ops:
  0.0 1.4 %shard_map.73 = (f32[3,16,256]{2,1,0:T(8,128)S(1)}, f32[3,16,256]{2,1,0:T(8,128)S(1)}, f32[16,128]{1,0:T(8,128)S(1)}, f32[4,16,16,256]{3,2,1,0:T(8,128)S(1)}, s32[16,16,256]{2,1,0:T(8,128)S(1)}) custom-call(f32[4,16,16,256]{3,2,1,0:T(8,128)} %conc_hbm.1, s32[16,16,256]{2,1,0:T(8,128)} %stratum_hbm.1, f32[1,16]{1,0:T(1,128)} %bitcast.6, f32[2,16]{1,0:T(2,128)} %bitcast.5, ...), custom_call_target="tpu_custom_call" | custom-call | tf_op jit(solution)/shard_map/pallas_call | solution.py:728
  1.4 0.5 %collective-permute-start.1 = (f32[3,16,256]{2,1,0:T(8,128)S(1)}, f32[3,16,256]{2,1,0:T(8,128)S(1)}, u32[]{:S(2)}, u32[]{:S(2)}) collective-permute-start(f32[3,16,256]{2,1,0:T(8,128)S(1)} %get-tuple-element.55.early_ref), channel_id=1, source_target_pairs={{0,1},{1,0},{2,3},{3,2},{4,5},{5,4},{6,7},{7,6},{8,9},{9,8},{10,11... | collective-permute-start | bytes 147464 | tf_op jit(solution)/shard_map/ppermute | solution.py:772
  2.0 2.6 %collective-permute-start = (f32[3,16,256]{2,1,0:T(8,128)S(1)}, f32[3,16,256]{2,1,0:T(8,128)S(1)}, u32[]{:S(2)}, u32[]{:S(2)}) collective-permute-start(f32[3,16,256]{2,1,0:T(8,128)S(1)} %get-tuple-element.56.late_ref), channel_id=1, source_target_pairs={{0,4},{1,2},{2,1},{3,7},{4,0},{5,6},{6,5},{7,3},{8,12},{9,10},{10,... | collective-permute-start | bytes 147464 | tf_op jit(solution)/shard_map/ppermute | solution.py:772
  4.6 2.3 %shard_map.74 = (f32[4,14,8,256]{3,2,1,0:T(8,128)S(1)}, f32[6,16,256]{2,1,0:T(8,128)S(1)}, f32[16,8,256]{2,1,0:T(8,128)S(1)}, f32[16,8,256]{2,1,0:T(8,128)S(1)},...) custom-call(f32[16,128]{1,0:T(8,128)S(1)} %get-tuple-element.54.tab_, ...), custom_call_target="tpu_custom_call" | custom-call | tf_op jit(solution)/shard_map/pallas_call | solution.py:784
  6.8 0.0 collective-permute-done.1.beyond_early_ref
  6.8 0.0 collective-permute-done.beyond_late_ref
  6.9 0.2 shard_map.75
  7.0 1.8 %collective-permute-start.2 = (f32[14,8,256]{2,1,0:T(8,128)S(1)}, f32[14,8,256]{2,1,0:T(8,128)S(1)}, u32[]{:S(2)}, u32[]{:S(2)}) collective-permute-start(f32[14,8,256]{2,1,0:T(8,128)S(1)} %get-tuple-element.76), channel_id=1, source_target_pairs={{0,4},{4,0},{8,12},{12,8},{16,20},{20,16},{24,28},{28,24},{1,5},{5... | collective-permute-start | bytes 344072 | tf_op jit(solution)/shard_map/ppermute | solution.py:778
  8.9 2.9 %shard_map.77 = (f32[4,14,8,256]{3,2,1,0:T(8,128)S(1)}, f32[6,16,256]{2,1,0:T(8,128)S(1)}, f32[16,8,256]{2,1,0:T(8,128)S(1)}, f32[16,8,256]{2,1,0:T(8,128)S(1)},...) custom-call(f32[16,128]{1,0:T(8,128)S(1)} %get-tuple-element.54.tab_, ...), custom_call_target="tpu_custom_call" | custom-call | tf_op jit(solution)/shard_map/pallas_call | solution.py:784
  11.8 0.2 shard_map.78
  12.0 0.3 %collective-permute-done.2.other_ref = f32[14,8,256]{2,1,0:T(8,128)S(1)} collective-permute-done((f32[14,8,256]{2,1,0:T(8,128)S(1)}, f32[14,8,256]{2,1,0:T(8,128)S(1)}, u32[]{:S(2)}, u32[]{:S(2)}) %collective-permute-start.2) | collective-permute-done | bytes 114720 | tf_op jit(solution)/shard_map/ppermute | solution.py:778
  12.3 1.9 %collective-permute-start.3 = (f32[14,8,256]{2,1,0:T(8,128)S(1)}, f32[14,8,256]{2,1,0:T(8,128)S(1)}, u32[]{:S(2)}, u32[]{:S(2)}) collective-permute-start(f32[14,8,256]{2,1,0:T(8,128)S(1)} %get-tuple-element.77.own_ref), channel_id=1, source_target_pairs={{0,8},{4,12},{8,0},{12,4},{16,24},{20,28},{24,16},{28,20},{1,9},{5... | collective-permute-start | bytes 344072 | tf_op jit(solution)/shard_map/ppermute | solution.py:778
  14.2 3.0 %collective-permute-done.3.other_ref = f32[14,8,256]{2,1,0:T(8,128)S(1)} collective-permute-done((f32[14,8,256]{2,1,0:T(8,128)S(1)}, f32[14,8,256]{2,1,0:T(8,128)S(1)}, u32[]{:S(2)}, u32[]{:S(2)}) %collective-permute-start.3) | collective-permute-done | bytes 114720 | tf_op jit(solution)/shard_map/ppermute | solution.py:778
  17.3 2.9 %collective-permute-start.4 = (f32[5,8,256]{2,1,0:T(8,128)S(1)}, f32[5,8,256]{2,1,0:T(8,128)S(1)}, u32[]{:S(2)}, u32[]{:S(2)}) collective-permute-start(f32[5,8,256]{2,1,0:T(8,128)S(1)} %get-tuple-element.79), channel_id=1, source_target_pairs={{0,16},{4,20},{8,24},{12,28},{16,0},{20,4},{24,8},{28,12},{1,17},{... | collective-permute-start | bytes 122888 | tf_op jit(solution)/shard_map/ppermute | solution.py:778
  20.1 0.5 %shard_map.76 = (f32[16,8,256]{2,1,0:T(8,128)S(1)}, f32[16,8,256]{2,1,0:T(8,128)S(1)}, f32[16,8,256]{2,1,0:T(8,128)S(1)}, f32[16,8,256]{2,1,0:T(8,128)S(1)}, f32...) custom-call(f32[16,128]{1,0:T(8,128)S(1)} %get-tuple-element.54.tab_, ...), custom_call_target="tpu_custom_call" | custom-call | tf_op jit(solution)/shard_map/pallas_call | solution.py:813
  20.7 1.6 %collective-permute-done.4.other_ref = f32[5,8,256]{2,1,0:T(8,128)S(1)} collective-permute-done((f32[5,8,256]{2,1,0:T(8,128)S(1)}, f32[5,8,256]{2,1,0:T(8,128)S(1)}, u32[]{:S(2)}, u32[]{:S(2)}) %collective-permute-start.4) | collective-permute-done | bytes 40992 | tf_op jit(solution)/shard_map/ppermute | solution.py:778
  22.3 1.8 %collective-permute-start.5 = (f32[4,8,256]{2,1,0:T(8,128)S(1)}, f32[4,8,256]{2,1,0:T(8,128)S(1)}, u32[]{:S(2)}, u32[]{:S(2)}) collective-permute-start(f32[4,8,256]{2,1,0:T(8,128)S(1)} %get-tuple-element.82), channel_id=1, source_target_pairs={{0,4},{4,0},{8,12},{12,8},{16,20},{20,16},{24,28},{28,24},{1,5},{5... | collective-permute-start | bytes 98312 | tf_op jit(solution)/shard_map/ppermute | solution.py:778
  24.1 1.3 %shard_map.82.before_hbm = f32[4,16,16,256]{3,2,1,0:T(8,128)} custom-call(f32[16,128]{1,0:T(8,128)S(1)} %get-tuple-element.54.tab_ref, s32[16,16,256]{2,1,0:T(8,128)S(1)} %get-tuple-element.57.stratum_ref, f32[4,16,16,256]{3,2,1,0:T(8,128)S(1)} %get-tuple-element.58.conc_ref, f32[16,8,256]{2,1,0:T(8,128)S(1)} %get-tuple-element.93.pass_a_ref, ...), custom_call_target="tpu_custom_call" | custom-call | tf_op jit(solution)/shard_map/pallas_call | solution.py:828
  25.4 0.9 %collective-permute-done.5.current_ref = f32[4,8,256]{2,1,0:T(8,128)S(1)} collective-permute-done((f32[4,8,256]{2,1,0:T(8,128)S(1)}, f32[4,8,256]{2,1,0:T(8,128)S(1)}, u32[]{:S(2)}, u32[]{:S(2)}) %collective-permute-start.5) | collective-permute-done | bytes 32800 | tf_op jit(solution)/shard_map/ppermute | solution.py:778
  26.2 1.0 %shard_map.83 = f32[4,16,16,256]{3,2,1,0:T(8,128)} custom-call(f32[3,8,8,256]{3,2,1,0:T(8,128)S(1)} %get-tuple-element.61.kept_ref, f32[4,8,256]{2,1,0:T(8,128)S(1)} %collective-permute-done.5.current_ref, f32[16,8,256]{2,1,0:T(8,128)S(1)} %get-tuple-element.72.ready_ref.free_a_ref, ...), custom_call_target="tpu_custom_call", output_to_operand_aliasing={{}: (15, {})} | custom-call | tf_op jit(solution)/shard_map/pallas_call | solution.py:836
  (3 shorter events, 0.1 us)
Async XLA Ops:
  1.4 5.4 %collective-permute-start.1 = (f32[3,16,256]{2,1,0:T(8,128)S(1)}, f32[3,16,256]{2,1,0:T(8,128)S(1)}, u32[]{:S(2)}, u32[]{:S(2)}) collective-permute-start(f32[3,16,256]{2,1,0:T(8,128)S(1)} %get-tuple-element.55.early_ref), channel_id=1, source_target_pairs={{0,1},{1,0},{2,3},{3,2},{4,5},{5,4},{6,7},{7,6},{8,9},{9,8},{10,11... | collective-permute-start | bytes 147464 | tf_op jit(solution)/shard_map/ppermute | solution.py:772
  2.0 4.9 %collective-permute-start = (f32[3,16,256]{2,1,0:T(8,128)S(1)}, f32[3,16,256]{2,1,0:T(8,128)S(1)}, u32[]{:S(2)}, u32[]{:S(2)}) collective-permute-start(f32[3,16,256]{2,1,0:T(8,128)S(1)} %get-tuple-element.56.late_ref), channel_id=1, source_target_pairs={{0,4},{1,2},{2,1},{3,7},{4,0},{5,6},{6,5},{7,3},{8,12},{9,10},{10,... | collective-permute-start | bytes 147464 | tf_op jit(solution)/shard_map/ppermute | solution.py:772
  7.0 5.3 %collective-permute-start.2 = (f32[14,8,256]{2,1,0:T(8,128)S(1)}, f32[14,8,256]{2,1,0:T(8,128)S(1)}, u32[]{:S(2)}, u32[]{:S(2)}) collective-permute-start(f32[14,8,256]{2,1,0:T(8,128)S(1)} %get-tuple-element.76), channel_id=1, source_target_pairs={{0,4},{4,0},{8,12},{12,8},{16,20},{20,16},{24,28},{28,24},{1,5},{5... | collective-permute-start | bytes 344072 | tf_op jit(solution)/shard_map/ppermute | solution.py:778
  12.3 4.9 %collective-permute-start.3 = (f32[14,8,256]{2,1,0:T(8,128)S(1)}, f32[14,8,256]{2,1,0:T(8,128)S(1)}, u32[]{:S(2)}, u32[]{:S(2)}) collective-permute-start(f32[14,8,256]{2,1,0:T(8,128)S(1)} %get-tuple-element.77.own_ref), channel_id=1, source_target_pairs={{0,8},{4,12},{8,0},{12,4},{16,24},{20,28},{24,16},{28,20},{1,9},{5... | collective-permute-start | bytes 344072 | tf_op jit(solution)/shard_map/ppermute | solution.py:778
  17.3 5.0 %collective-permute-start.4 = (f32[5,8,256]{2,1,0:T(8,128)S(1)}, f32[5,8,256]{2,1,0:T(8,128)S(1)}, u32[]{:S(2)}, u32[]{:S(2)}) collective-permute-start(f32[5,8,256]{2,1,0:T(8,128)S(1)} %get-tuple-element.79), channel_id=1, source_target_pairs={{0,16},{4,20},{8,24},{12,28},{16,0},{20,4},{24,8},{28,12},{1,17},{... | collective-permute-start | bytes 122888 | tf_op jit(solution)/shard_map/ppermute | solution.py:778
  22.3 4.0 %collective-permute-start.5 = (f32[4,8,256]{2,1,0:T(8,128)S(1)}, f32[4,8,256]{2,1,0:T(8,128)S(1)}, u32[]{:S(2)}, u32[]{:S(2)}) collective-permute-start(f32[4,8,256]{2,1,0:T(8,128)S(1)} %get-tuple-element.82), channel_id=1, source_target_pairs={{0,4},{4,0},{8,12},{12,8},{16,20},{20,16},{24,28},{28,24},{1,5},{5... | collective-permute-start | bytes 98312 | tf_op jit(solution)/shard_map/ppermute | solution.py:778

commit v14 on v11

--- a/solution.py
+++ b/solution.py
@@ -218,7 +218,8 @@
             after.append((cond_a, cond_b, new_a, new_b, through_a, through_b))
         return after
 
-    ahead = lax.fori_loop(0, m, from_left, [(zero, zero, zero, zero, one, one)] * PIECES)
+    start = [(zero, zero, zero, zero, one, one)] * PIECES
+    ahead = lax.fori_loop(0, m, from_left, start, unroll=2)
     over_a, over_b = [recip(c[0]) for c in ahead], [recip(c[1]) for c in ahead]
     for s in pieces:
         over_ref[0, s], over_ref[1, s] = over_a[s], over_b[s]
@@ -246,6 +247,7 @@
         m,
         from_right,
         [(one, a, one, b, zero, a, zero, b, zero, zero, zero, zero) for a, b in zip(over_a, over_b)],
+        unroll=2,
     )
 
     def share(j, carry):
@@ -259,7 +261,7 @@
             after.append((g_l, g_r))
         return after
 
-    lax.fori_loop(0, m, share, [(zero, zero)] * PIECES)
+    lax.fori_loop(0, m, share, [(zero, zero)] * PIECES, unroll=2)
 
     lane = lax.broadcasted_iota(jnp.int32, shape, 1)
     line = lax.broadcasted_iota(jnp.int32, shape, 0)
@@ -306,7 +308,7 @@
             after.append((pass_a_ref[i], drop_a_ref[i], w_l, w_r, *free))
         return after
 
-    totals = lax.fori_loop(0, m, sources, [(one, a) + (zero,) * 6 for a in over_a])
+    totals = lax.fori_loop(0, m, sources, [(one, a) + (zero,) * 6 for a in over_a], unroll=2)
     for s in pieces:
         l_a, r_a, l_b, r_b, *couple = responses[s][4:]
         first = stratum_ref[s * m, rows, :]

time: 27.3 us -> 27.1 us (level)
  starting transfers between devices: 10.7 us -> 11.2 us
  Pallas kernels: 9.93 us -> 9.53 us
  waiting for transfers between devices: 6.49 us -> 6.16 us
    ppermute x4, starting transfers between devices: 7.56 us -> 8.11 us  [exchange(): return lax.ppermute(value, 'flow', [(i, i ^ stride) for i in range(peers)])]
    pallas_call x2, Pallas kernels: 5.22 us -> 4.82 us  [local(): call(functools.partial(local_kernel, kept), [(PIECES,) + block_shape, (6,...]
    ppermute x4, waiting for transfers between devices: 6.49 us -> 6.15 us  [exchange(): return lax.ppermute(value, 'flow', [(i, i ^ stride) for i in range(peers)])]
  transfers between devices with their start and end apart: 6 -> 6, of which waited for: 4 -> 4; matrix products, arithmetic and copies ran while one was open for 0% -> 0% of each run, Pallas kernels for 26% -> 25%
where the time goes in v14:
time: 27.1 us; the launch traced here: 27 us
  starting transfers between devices  11.2 us (41%)
  Pallas kernels  9.53 us (35%)
  waiting for transfers between devices  6.16 us (23%)
    ppermute x4, starting transfers between devices, exchange(): return lax.ppermute(value, 'flow', [(i, i ^ stride) for i in range(peers)])  8.11 us
    ppermute x4, waiting for transfers between devices, exchange(): return lax.ppermute(value, 'flow', [(i, i ^ stride) for i in range(peers)])  6.15 us
    pallas_call x2, Pallas kernels, local(): call(functools.partial(local_kernel, kept), [(PIECES,) + block_shape, (6,...  4.82 us
    ppermute x2, starting transfers between devices, swap(): return lax.ppermute(value, 'trans', pairs)  3.13 us
    pallas_call x1, Pallas kernels, per_device(): pl.pallas_call(pack_kernel, out_shape=[jax.ShapeDtypeStruct(halo, jnp.flo...  1.43 us
    pallas_call x1, Pallas kernels, per_device(): pl.pallas_call(functools.partial(final_kernel, True), out_shape=whole, in...  1.29 us
    pallas_call x1, Pallas kernels, per_device(): pl.pallas_call(functools.partial(add_kernel, False), out_shape=whole, in_...  0.99 us
  transfers between devices with their start and end apart: 6, of which 4 were waited for; matrix products, arithmetic and copies ran while one was open for 0% of the time, Pallas kernels for 25%

profile of v14, /device:TPU:0, one launch (start us, length us, event | category | flops | bytes accessed | tf_op | source)
XLA Modules:
  0.0 27.0 jit_solution(99932744700311219)
XLA Ops:
  0.0 1.4 %shard_map.73 = (f32[3,16,256]{2,1,0:T(8,128)S(1)}, f32[3,16,256]{2,1,0:T(8,128)S(1)}, f32[16,128]{1,0:T(8,128)S(1)}, f32[4,16,16,256]{3,2,1,0:T(8,128)S(1)}, s32[16,16,256]{2,1,0:T(8,128)S(1)}) custom-call(f32[4,16,16,256]{3,2,1,0:T(8,128)} %conc_hbm.1, s32[16,16,256]{2,1,0:T(8,128)} %stratum_hbm.1, f32[1,16]{1,0:T(1,128)} %bitcast.6, f32[2,16]{1,0:T(2,128)} %bitcast.5, ...), custom_call_target="tpu_custom_call" | custom-call | tf_op jit(solution)/shard_map/pallas_call | solution.py:730
  1.4 0.5 %collective-permute-start.1 = (f32[3,16,256]{2,1,0:T(8,128)S(1)}, f32[3,16,256]{2,1,0:T(8,128)S(1)}, u32[]{:S(2)}, u32[]{:S(2)}) collective-permute-start(f32[3,16,256]{2,1,0:T(8,128)S(1)} %get-tuple-element.55.early_ref), channel_id=1, source_target_pairs={{0,1},{2,3},{1,0},{3,2},{4,5},{6,7},{5,4},{7,6},{8,9},{10,11},{9,8... | collective-permute-start | bytes 147464 | tf_op jit(solution)/shard_map/ppermute | solution.py:770
  2.0 2.6 %collective-permute-start = (f32[3,16,256]{2,1,0:T(8,128)S(1)}, f32[3,16,256]{2,1,0:T(8,128)S(1)}, u32[]{:S(2)}, u32[]{:S(2)}) collective-permute-start(f32[3,16,256]{2,1,0:T(8,128)S(1)} %get-tuple-element.56.late_ref), channel_id=1, source_target_pairs={{1,2},{2,1},{0,3},{3,0},{5,6},{6,5},{4,7},{7,4},{9,10},{10,9},{8,1... | collective-permute-start | bytes 147464 | tf_op jit(solution)/shard_map/ppermute | solution.py:770
  4.6 2.1 %shard_map.74 = (f32[4,14,8,256]{3,2,1,0:T(8,128)S(1)}, f32[6,16,256]{2,1,0:T(8,128)S(1)}, f32[16,8,256]{2,1,0:T(8,128)S(1)}, f32[16,8,256]{2,1,0:T(8,128)S(1)},...) custom-call(f32[16,128]{1,0:T(8,128)S(1)} %get-tuple-element.54.tab_, ...), custom_call_target="tpu_custom_call" | custom-call | tf_op jit(solution)/shard_map/pallas_call | solution.py:782
  6.7 0.0 collective-permute-done.1.beyond_early_ref
  6.7 0.0 collective-permute-done.beyond_late_ref
  6.7 0.2 shard_map.75
  6.9 1.6 %collective-permute-start.2 = (f32[14,8,256]{2,1,0:T(8,128)S(1)}, f32[14,8,256]{2,1,0:T(8,128)S(1)}, u32[]{:S(2)}, u32[]{:S(2)}) collective-permute-start(f32[14,8,256]{2,1,0:T(8,128)S(1)} %get-tuple-element.76), channel_id=1, source_target_pairs={{0,4},{4,0},{8,12},{12,8},{16,20},{20,16},{24,28},{28,24},{1,5},{5... | collective-permute-start | bytes 344072 | tf_op jit(solution)/shard_map/ppermute | solution.py:776
  8.5 2.7 %shard_map.77 = (f32[4,14,8,256]{3,2,1,0:T(8,128)S(1)}, f32[6,16,256]{2,1,0:T(8,128)S(1)}, f32[16,8,256]{2,1,0:T(8,128)S(1)}, f32[16,8,256]{2,1,0:T(8,128)S(1)},...) custom-call(f32[16,128]{1,0:T(8,128)S(1)} %get-tuple-element.54.tab_, ...), custom_call_target="tpu_custom_call" | custom-call | tf_op jit(solution)/shard_map/pallas_call | solution.py:782
  11.2 0.2 shard_map.78
  11.4 0.7 %collective-permute-done.2.other_ref = f32[14,8,256]{2,1,0:T(8,128)S(1)} collective-permute-done((f32[14,8,256]{2,1,0:T(8,128)S(1)}, f32[14,8,256]{2,1,0:T(8,128)S(1)}, u32[]{:S(2)}, u32[]{:S(2)}) %collective-permute-start.2) | collective-permute-done | bytes 114720 | tf_op jit(solution)/shard_map/ppermute | solution.py:776
  12.1 1.9 %collective-permute-start.3 = (f32[14,8,256]{2,1,0:T(8,128)S(1)}, f32[14,8,256]{2,1,0:T(8,128)S(1)}, u32[]{:S(2)}, u32[]{:S(2)}) collective-permute-start(f32[14,8,256]{2,1,0:T(8,128)S(1)} %get-tuple-element.77.own_ref), channel_id=1, source_target_pairs={{0,8},{4,12},{8,0},{12,4},{16,24},{20,28},{24,16},{28,20},{1,9},{5... | collective-permute-start | bytes 344072 | tf_op jit(solution)/shard_map/ppermute | solution.py:776
  14.0 3.0 %collective-permute-done.3.other_ref = f32[14,8,256]{2,1,0:T(8,128)S(1)} collective-permute-done((f32[14,8,256]{2,1,0:T(8,128)S(1)}, f32[14,8,256]{2,1,0:T(8,128)S(1)}, u32[]{:S(2)}, u32[]{:S(2)}) %collective-permute-start.3) | collective-permute-done | bytes 114720 | tf_op jit(solution)/shard_map/ppermute | solution.py:776
  17.0 2.9 %collective-permute-start.4 = (f32[5,8,256]{2,1,0:T(8,128)S(1)}, f32[5,8,256]{2,1,0:T(8,128)S(1)}, u32[]{:S(2)}, u32[]{:S(2)}) collective-permute-start(f32[5,8,256]{2,1,0:T(8,128)S(1)} %get-tuple-element.79), channel_id=1, source_target_pairs={{0,16},{4,20},{8,24},{12,28},{16,0},{20,4},{24,8},{28,12},{1,17},{... | collective-permute-start | bytes 122888 | tf_op jit(solution)/shard_map/ppermute | solution.py:776
  19.9 0.5 %shard_map.76 = (f32[16,8,256]{2,1,0:T(8,128)S(1)}, f32[16,8,256]{2,1,0:T(8,128)S(1)}, f32[16,8,256]{2,1,0:T(8,128)S(1)}, f32[16,8,256]{2,1,0:T(8,128)S(1)}, f32...) custom-call(f32[16,128]{1,0:T(8,128)S(1)} %get-tuple-element.54.tab_, ...), custom_call_target="tpu_custom_call" | custom-call | tf_op jit(solution)/shard_map/pallas_call | solution.py:811
  20.4 1.6 %collective-permute-done.4.other_ref = f32[5,8,256]{2,1,0:T(8,128)S(1)} collective-permute-done((f32[5,8,256]{2,1,0:T(8,128)S(1)}, f32[5,8,256]{2,1,0:T(8,128)S(1)}, u32[]{:S(2)}, u32[]{:S(2)}) %collective-permute-start.4) | collective-permute-done | bytes 40992 | tf_op jit(solution)/shard_map/ppermute | solution.py:776
  22.0 1.8 %collective-permute-start.5 = (f32[4,8,256]{2,1,0:T(8,128)S(1)}, f32[4,8,256]{2,1,0:T(8,128)S(1)}, u32[]{:S(2)}, u32[]{:S(2)}) collective-permute-start(f32[4,8,256]{2,1,0:T(8,128)S(1)} %get-tuple-element.82), channel_id=1, source_target_pairs={{0,4},{4,0},{8,12},{12,8},{16,20},{20,16},{24,28},{28,24},{1,5},{5... | collective-permute-start | bytes 98312 | tf_op jit(solution)/shard_map/ppermute | solution.py:776
  23.8 1.3 %shard_map.82.before_hbm = f32[4,16,16,256]{3,2,1,0:T(8,128)} custom-call(f32[16,128]{1,0:T(8,128)S(1)} %get-tuple-element.54.tab_ref, s32[16,16,256]{2,1,0:T(8,128)S(1)} %get-tuple-element.57.stratum_ref, f32[4,16,16,256]{3,2,1,0:T(8,128)S(1)} %get-tuple-element.58.conc_ref, f32[16,8,256]{2,1,0:T(8,128)S(1)} %get-tuple-element.93.pass_a_ref, ...), custom_call_target="tpu_custom_call" | custom-call | tf_op jit(solution)/shard_map/pallas_call | solution.py:826
  25.1 0.9 %collective-permute-done.5.current_ref = f32[4,8,256]{2,1,0:T(8,128)S(1)} collective-permute-done((f32[4,8,256]{2,1,0:T(8,128)S(1)}, f32[4,8,256]{2,1,0:T(8,128)S(1)}, u32[]{:S(2)}, u32[]{:S(2)}) %collective-permute-start.5) | collective-permute-done | bytes 32800 | tf_op jit(solution)/shard_map/ppermute | solution.py:776
  26.0 1.0 %shard_map.83 = f32[4,16,16,256]{3,2,1,0:T(8,128)} custom-call(f32[3,8,8,256]{3,2,1,0:T(8,128)S(1)} %get-tuple-element.61.kept_ref, f32[4,8,256]{2,1,0:T(8,128)S(1)} %collective-permute-done.5.current_ref, f32[16,8,256]{2,1,0:T(8,128)S(1)} %get-tuple-element.72.ready_ref.free_a_ref, ...), custom_call_target="tpu_custom_call", output_to_operand_aliasing={{}: (15, {})} | custom-call | tf_op jit(solution)/shard_map/pallas_call | solution.py:834
  (3 shorter events, 0.1 us)
Async XLA Ops:
  1.4 5.2 %collective-permute-start.1 = (f32[3,16,256]{2,1,0:T(8,128)S(1)}, f32[3,16,256]{2,1,0:T(8,128)S(1)}, u32[]{:S(2)}, u32[]{:S(2)}) collective-permute-start(f32[3,16,256]{2,1,0:T(8,128)S(1)} %get-tuple-element.55.early_ref), channel_id=1, source_target_pairs={{0,1},{2,3},{1,0},{3,2},{4,5},{6,7},{5,4},{7,6},{8,9},{10,11},{9,8... | collective-permute-start | bytes 147464 | tf_op jit(solution)/shard_map/ppermute | solution.py:770
  2.0 4.7 %collective-permute-start = (f32[3,16,256]{2,1,0:T(8,128)S(1)}, f32[3,16,256]{2,1,0:T(8,128)S(1)}, u32[]{:S(2)}, u32[]{:S(2)}) collective-permute-start(f32[3,16,256]{2,1,0:T(8,128)S(1)} %get-tuple-element.56.late_ref), channel_id=1, source_target_pairs={{1,2},{2,1},{0,3},{3,0},{5,6},{6,5},{4,7},{7,4},{9,10},{10,9},{8,1... | collective-permute-start | bytes 147464 | tf_op jit(solution)/shard_map/ppermute | solution.py:770
  6.9 5.2 %collective-permute-start.2 = (f32[14,8,256]{2,1,0:T(8,128)S(1)}, f32[14,8,256]{2,1,0:T(8,128)S(1)}, u32[]{:S(2)}, u32[]{:S(2)}) collective-permute-start(f32[14,8,256]{2,1,0:T(8,128)S(1)} %get-tuple-element.76), channel_id=1, source_target_pairs={{0,4},{4,0},{8,12},{12,8},{16,20},{20,16},{24,28},{28,24},{1,5},{5... | collective-permute-start | bytes 344072 | tf_op jit(solution)/shard_map/ppermute | solution.py:776
  12.1 4.9 %collective-permute-start.3 = (f32[14,8,256]{2,1,0:T(8,128)S(1)}, f32[14,8,256]{2,1,0:T(8,128)S(1)}, u32[]{:S(2)}, u32[]{:S(2)}) collective-permute-start(f32[14,8,256]{2,1,0:T(8,128)S(1)} %get-tuple-element.77.own_ref), channel_id=1, source_target_pairs={{0,8},{4,12},{8,0},{12,4},{16,24},{20,28},{24,16},{28,20},{1,9},{5... | collective-permute-start | bytes 344072 | tf_op jit(solution)/shard_map/ppermute | solution.py:776
  17.0 5.0 %collective-permute-start.4 = (f32[5,8,256]{2,1,0:T(8,128)S(1)}, f32[5,8,256]{2,1,0:T(8,128)S(1)}, u32[]{:S(2)}, u32[]{:S(2)}) collective-permute-start(f32[5,8,256]{2,1,0:T(8,128)S(1)} %get-tuple-element.79), channel_id=1, source_target_pairs={{0,16},{4,20},{8,24},{12,28},{16,0},{20,4},{24,8},{28,12},{1,17},{... | collective-permute-start | bytes 122888 | tf_op jit(solution)/shard_map/ppermute | solution.py:776
  22.0 4.0 %collective-permute-start.5 = (f32[4,8,256]{2,1,0:T(8,128)S(1)}, f32[4,8,256]{2,1,0:T(8,128)S(1)}, u32[]{:S(2)}, u32[]{:S(2)}) collective-permute-start(f32[4,8,256]{2,1,0:T(8,128)S(1)} %get-tuple-element.82), channel_id=1, source_target_pairs={{0,4},{4,0},{8,12},{12,8},{16,20},{20,16},{24,28},{28,24},{1,5},{5... | collective-permute-start | bytes 98312 | tf_op jit(solution)/shard_map/ppermute | solution.py:776

commit v15 on v14

--- a/solution.py
+++ b/solution.py
@@ -219,7 +219,7 @@
         return after
 
     start = [(zero, zero, zero, zero, one, one)] * PIECES
-    ahead = lax.fori_loop(0, m, from_left, start, unroll=2)
+    ahead = lax.fori_loop(0, m, from_left, start, unroll=4)
     over_a, over_b = [recip(c[0]) for c in ahead], [recip(c[1]) for c in ahead]
     for s in pieces:
         over_ref[0, s], over_ref[1, s] = over_a[s], over_b[s]
@@ -247,7 +247,7 @@
         m,
         from_right,
         [(one, a, one, b, zero, a, zero, b, zero, zero, zero, zero) for a, b in zip(over_a, over_b)],
-        unroll=2,
+        unroll=4,
     )
 
     def share(j, carry):
@@ -261,7 +261,7 @@
             after.append((g_l, g_r))
         return after
 
-    lax.fori_loop(0, m, share, [(zero, zero)] * PIECES, unroll=2)
+    lax.fori_loop(0, m, share, [(zero, zero)] * PIECES, unroll=4)
 
     lane = lax.broadcasted_iota(jnp.int32, shape, 1)
     line = lax.broadcasted_iota(jnp.int32, shape, 0)
@@ -308,7 +308,7 @@
             after.append((pass_a_ref[i], drop_a_ref[i], w_l, w_r, *free))
         return after
 
-    totals = lax.fori_loop(0, m, sources, [(one, a) + (zero,) * 6 for a in over_a], unroll=2)
+    totals = lax.fori_loop(0, m, sources, [(one, a) + (zero,) * 6 for a in over_a], unroll=4)
     for s in pieces:
         l_a, r_a, l_b, r_b, *couple = responses[s][4:]
         first = stratum_ref[s * m, rows, :]

time: 27.1 us -> 28.1 us (1.037)
  Pallas kernels: 9.53 us -> 11.1 us
  starting transfers between devices: 11.2 us -> 10.4 us
    pallas_call x2, Pallas kernels: 4.82 us -> 6.39 us  [local(): call(functools.partial(local_kernel, kept), [(PIECES,) + block_shape, (6,...]
    ppermute x4, starting transfers between devices: 8.11 us -> 7.3 us  [exchange(): return lax.ppermute(value, 'flow', [(i, i ^ stride) for i in range(peers)])]
  transfers between devices with their start and end apart: 6 -> 6, of which waited for: 4 -> 3; matrix products, arithmetic and copies ran while one was open for 0% -> 0% of each run, Pallas kernels for 25% -> 30%
where the time goes in v15:
time: 28.1 us; the launch traced here: 27.9 us
  Pallas kernels  11.1 us (40%)
  starting transfers between devices  10.4 us (37%)
  waiting for transfers between devices  6.31 us (22%)
    ppermute x4, starting transfers between devices, exchange(): return lax.ppermute(value, 'flow', [(i, i ^ stride) for i in range(peers)])  7.3 us
    pallas_call x2, Pallas kernels, local(): call(functools.partial(local_kernel, kept), [(PIECES,) + block_shape, (6,...  6.39 us
    ppermute x4, waiting for transfers between devices, exchange(): return lax.ppermute(value, 'flow', [(i, i ^ stride) for i in range(peers)])  6.3 us
    ppermute x2, starting transfers between devices, swap(): return lax.ppermute(value, 'trans', pairs)  3.13 us
    pallas_call x1, Pallas kernels, per_device(): pl.pallas_call(pack_kernel, out_shape=[jax.ShapeDtypeStruct(halo, jnp.flo...  1.43 us
    pallas_call x1, Pallas kernels, per_device(): pl.pallas_call(functools.partial(final_kernel, True), out_shape=whole, in...  1.29 us
    pallas_call x1, Pallas kernels, per_device(): pl.pallas_call(functools.partial(add_kernel, False), out_shape=whole, in_...  0.99 us
  transfers between devices with their start and end apart: 6, of which 3 were waited for; matrix products, arithmetic and copies ran while one was open for 0% of the time, Pallas kernels for 30%

profile of v15, /device:TPU:0, one launch (start us, length us, event | category | flops | bytes accessed | tf_op | source)
XLA Modules:
  0.0 27.9 jit_solution(564102896155353630)
XLA Ops:
  0.0 1.4 %shard_map.73 = (f32[3,16,256]{2,1,0:T(8,128)S(1)}, f32[3,16,256]{2,1,0:T(8,128)S(1)}, f32[16,128]{1,0:T(8,128)S(1)}, f32[4,16,16,256]{3,2,1,0:T(8,128)S(1)}, s32[16,16,256]{2,1,0:T(8,128)S(1)}) custom-call(f32[4,16,16,256]{3,2,1,0:T(8,128)} %conc_hbm.1, s32[16,16,256]{2,1,0:T(8,128)} %stratum_hbm.1, f32[1,16]{1,0:T(1,128)} %bitcast.6, f32[2,16]{1,0:T(2,128)} %bitcast.5, ...), custom_call_target="tpu_custom_call" | custom-call | tf_op jit(solution)/shard_map/pallas_call | solution.py:730
  1.4 0.5 %collective-permute-start.1 = (f32[3,16,256]{2,1,0:T(8,128)S(1)}, f32[3,16,256]{2,1,0:T(8,128)S(1)}, u32[]{:S(2)}, u32[]{:S(2)}) collective-permute-start(f32[3,16,256]{2,1,0:T(8,128)S(1)} %get-tuple-element.55.early_ref), channel_id=1, source_target_pairs={{0,1},{2,3},{1,0},{3,2},{4,5},{6,7},{5,4},{7,6},{8,9},{10,11},{9,8... | collective-permute-start | bytes 147464 | tf_op jit(solution)/shard_map/ppermute | solution.py:770
  2.0 2.6 %collective-permute-start = (f32[3,16,256]{2,1,0:T(8,128)S(1)}, f32[3,16,256]{2,1,0:T(8,128)S(1)}, u32[]{:S(2)}, u32[]{:S(2)}) collective-permute-start(f32[3,16,256]{2,1,0:T(8,128)S(1)} %get-tuple-element.56.late_ref), channel_id=1, source_target_pairs={{1,2},{2,1},{0,3},{3,0},{5,6},{6,5},{4,7},{7,4},{9,10},{10,9},{8,1... | collective-permute-start | bytes 147464 | tf_op jit(solution)/shard_map/ppermute | solution.py:770
  4.6 2.9 %shard_map.74 = (f32[4,14,8,256]{3,2,1,0:T(8,128)S(1)}, f32[6,16,256]{2,1,0:T(8,128)S(1)}, f32[16,8,256]{2,1,0:T(8,128)S(1)}, f32[16,8,256]{2,1,0:T(8,128)S(1)},...) custom-call(f32[16,128]{1,0:T(8,128)S(1)} %get-tuple-element.54.tab_, ...), custom_call_target="tpu_custom_call" | custom-call | tf_op jit(solution)/shard_map/pallas_call | solution.py:782
  7.4 0.0 collective-permute-done.1.beyond_early_ref
  7.4 0.0 collective-permute-done.beyond_late_ref
  7.5 0.2 shard_map.75
  7.6 1.6 %collective-permute-start.2 = (f32[14,8,256]{2,1,0:T(8,128)S(1)}, f32[14,8,256]{2,1,0:T(8,128)S(1)}, u32[]{:S(2)}, u32[]{:S(2)}) collective-permute-start(f32[14,8,256]{2,1,0:T(8,128)S(1)} %get-tuple-element.76), channel_id=1, source_target_pairs={{0,4},{4,0},{8,12},{12,8},{16,20},{20,16},{24,28},{28,24},{1,5},{5... | collective-permute-start | bytes 344072 | tf_op jit(solution)/shard_map/ppermute | solution.py:776
  9.2 3.5 %shard_map.77 = (f32[4,14,8,256]{3,2,1,0:T(8,128)S(1)}, f32[6,16,256]{2,1,0:T(8,128)S(1)}, f32[16,8,256]{2,1,0:T(8,128)S(1)}, f32[16,8,256]{2,1,0:T(8,128)S(1)},...) custom-call(f32[16,128]{1,0:T(8,128)S(1)} %get-tuple-element.54.tab_, ...), custom_call_target="tpu_custom_call" | custom-call | tf_op jit(solution)/shard_map/pallas_call | solution.py:782
  12.8 0.2 shard_map.78
  12.9 0.0 collective-permute-done.2.other_ref
  13.0 1.6 %collective-permute-start.3 = (f32[14,8,256]{2,1,0:T(8,128)S(1)}, f32[14,8,256]{2,1,0:T(8,128)S(1)}, u32[]{:S(2)}, u32[]{:S(2)}) collective-permute-start(f32[14,8,256]{2,1,0:T(8,128)S(1)} %get-tuple-element.77.own_ref), channel_id=1, source_target_pairs={{0,8},{4,12},{8,0},{12,4},{16,24},{20,28},{24,16},{28,20},{1,9},{5... | collective-permute-start | bytes 344072 | tf_op jit(solution)/shard_map/ppermute | solution.py:776
  14.6 3.3 %collective-permute-done.3.other_ref = f32[14,8,256]{2,1,0:T(8,128)S(1)} collective-permute-done((f32[14,8,256]{2,1,0:T(8,128)S(1)}, f32[14,8,256]{2,1,0:T(8,128)S(1)}, u32[]{:S(2)}, u32[]{:S(2)}) %collective-permute-start.3) | collective-permute-done | bytes 114720 | tf_op jit(solution)/shard_map/ppermute | solution.py:776
  17.9 2.7 %collective-permute-start.4 = (f32[5,8,256]{2,1,0:T(8,128)S(1)}, f32[5,8,256]{2,1,0:T(8,128)S(1)}, u32[]{:S(2)}, u32[]{:S(2)}) collective-permute-start(f32[5,8,256]{2,1,0:T(8,128)S(1)} %get-tuple-element.79), channel_id=1, source_target_pairs={{0,16},{4,20},{8,24},{12,28},{16,0},{20,4},{24,8},{28,12},{1,17},{... | collective-permute-start | bytes 122888 | tf_op jit(solution)/shard_map/ppermute | solution.py:776
  20.6 0.5 %shard_map.76 = (f32[16,8,256]{2,1,0:T(8,128)S(1)}, f32[16,8,256]{2,1,0:T(8,128)S(1)}, f32[16,8,256]{2,1,0:T(8,128)S(1)}, f32[16,8,256]{2,1,0:T(8,128)S(1)}, f32...) custom-call(f32[16,128]{1,0:T(8,128)S(1)} %get-tuple-element.54.tab_, ...), custom_call_target="tpu_custom_call" | custom-call | tf_op jit(solution)/shard_map/pallas_call | solution.py:811
  21.1 1.8 %collective-permute-done.4.other_ref = f32[5,8,256]{2,1,0:T(8,128)S(1)} collective-permute-done((f32[5,8,256]{2,1,0:T(8,128)S(1)}, f32[5,8,256]{2,1,0:T(8,128)S(1)}, u32[]{:S(2)}, u32[]{:S(2)}) %collective-permute-start.4) | collective-permute-done | bytes 40992 | tf_op jit(solution)/shard_map/ppermute | solution.py:776
  23.0 1.4 %collective-permute-start.5 = (f32[4,8,256]{2,1,0:T(8,128)S(1)}, f32[4,8,256]{2,1,0:T(8,128)S(1)}, u32[]{:S(2)}, u32[]{:S(2)}) collective-permute-start(f32[4,8,256]{2,1,0:T(8,128)S(1)} %get-tuple-element.82), channel_id=1, source_target_pairs={{0,4},{4,0},{8,12},{12,8},{16,20},{20,16},{24,28},{28,24},{1,5},{5... | collective-permute-start | bytes 98312 | tf_op jit(solution)/shard_map/ppermute | solution.py:776
  24.4 1.3 %shard_map.82.before_hbm = f32[4,16,16,256]{3,2,1,0:T(8,128)} custom-call(f32[16,128]{1,0:T(8,128)S(1)} %get-tuple-element.54.tab_ref, s32[16,16,256]{2,1,0:T(8,128)S(1)} %get-tuple-element.57.stratum_ref, f32[4,16,16,256]{3,2,1,0:T(8,128)S(1)} %get-tuple-element.58.conc_ref, f32[16,8,256]{2,1,0:T(8,128)S(1)} %get-tuple-element.93.pass_a_ref, ...), custom_call_target="tpu_custom_call" | custom-call | tf_op jit(solution)/shard_map/pallas_call | solution.py:826
  25.7 1.3 %collective-permute-done.5.current_ref = f32[4,8,256]{2,1,0:T(8,128)S(1)} collective-permute-done((f32[4,8,256]{2,1,0:T(8,128)S(1)}, f32[4,8,256]{2,1,0:T(8,128)S(1)}, u32[]{:S(2)}, u32[]{:S(2)}) %collective-permute-start.5) | collective-permute-done | bytes 32800 | tf_op jit(solution)/shard_map/ppermute | solution.py:776
  26.9 1.0 %shard_map.83 = f32[4,16,16,256]{3,2,1,0:T(8,128)} custom-call(f32[3,8,8,256]{3,2,1,0:T(8,128)S(1)} %get-tuple-element.61.kept_ref, f32[4,8,256]{2,1,0:T(8,128)S(1)} %collective-permute-done.5.current_ref, f32[16,8,256]{2,1,0:T(8,128)S(1)} %get-tuple-element.72.ready_ref.free_a_ref, ...), custom_call_target="tpu_custom_call", output_to_operand_aliasing={{}: (15, {})} | custom-call | tf_op jit(solution)/shard_map/pallas_call | solution.py:834
  (3 shorter events, 0.1 us)
Async XLA Ops:
  1.4 6.0 %collective-permute-start.1 = (f32[3,16,256]{2,1,0:T(8,128)S(1)}, f32[3,16,256]{2,1,0:T(8,128)S(1)}, u32[]{:S(2)}, u32[]{:S(2)}) collective-permute-start(f32[3,16,256]{2,1,0:T(8,128)S(1)} %get-tuple-element.55.early_ref), channel_id=1, source_target_pairs={{0,1},{2,3},{1,0},{3,2},{4,5},{6,7},{5,4},{7,6},{8,9},{10,11},{9,8... | collective-permute-start | bytes 147464 | tf_op jit(solution)/shard_map/ppermute | solution.py:770
  2.0 5.5 %collective-permute-start = (f32[3,16,256]{2,1,0:T(8,128)S(1)}, f32[3,16,256]{2,1,0:T(8,128)S(1)}, u32[]{:S(2)}, u32[]{:S(2)}) collective-permute-start(f32[3,16,256]{2,1,0:T(8,128)S(1)} %get-tuple-element.56.late_ref), channel_id=1, source_target_pairs={{1,2},{2,1},{0,3},{3,0},{5,6},{6,5},{4,7},{7,4},{9,10},{10,9},{8,1... | collective-permute-start | bytes 147464 | tf_op jit(solution)/shard_map/ppermute | solution.py:770
  7.6 5.3 %collective-permute-start.2 = (f32[14,8,256]{2,1,0:T(8,128)S(1)}, f32[14,8,256]{2,1,0:T(8,128)S(1)}, u32[]{:S(2)}, u32[]{:S(2)}) collective-permute-start(f32[14,8,256]{2,1,0:T(8,128)S(1)} %get-tuple-element.76), channel_id=1, source_target_pairs={{0,4},{4,0},{8,12},{12,8},{16,20},{20,16},{24,28},{28,24},{1,5},{5... | collective-permute-start | bytes 344072 | tf_op jit(solution)/shard_map/ppermute | solution.py:776
  13.0 4.9 %collective-permute-start.3 = (f32[14,8,256]{2,1,0:T(8,128)S(1)}, f32[14,8,256]{2,1,0:T(8,128)S(1)}, u32[]{:S(2)}, u32[]{:S(2)}) collective-permute-start(f32[14,8,256]{2,1,0:T(8,128)S(1)} %get-tuple-element.77.own_ref), channel_id=1, source_target_pairs={{0,8},{4,12},{8,0},{12,4},{16,24},{20,28},{24,16},{28,20},{1,9},{5... | collective-permute-start | bytes 344072 | tf_op jit(solution)/shard_map/ppermute | solution.py:776
  17.9 5.0 %collective-permute-start.4 = (f32[5,8,256]{2,1,0:T(8,128)S(1)}, f32[5,8,256]{2,1,0:T(8,128)S(1)}, u32[]{:S(2)}, u32[]{:S(2)}) collective-permute-start(f32[5,8,256]{2,1,0:T(8,128)S(1)} %get-tuple-element.79), channel_id=1, source_target_pairs={{0,16},{4,20},{8,24},{12,28},{16,0},{20,4},{24,8},{28,12},{1,17},{... | collective-permute-start | bytes 122888 | tf_op jit(solution)/shard_map/ppermute | solution.py:776
  23.0 4.0 %collective-permute-start.5 = (f32[4,8,256]{2,1,0:T(8,128)S(1)}, f32[4,8,256]{2,1,0:T(8,128)S(1)}, u32[]{:S(2)}, u32[]{:S(2)}) collective-permute-start(f32[4,8,256]{2,1,0:T(8,128)S(1)} %get-tuple-element.82), channel_id=1, source_target_pairs={{0,4},{4,0},{8,12},{12,8},{16,20},{20,16},{24,28},{28,24},{1,5},{5... | collective-permute-start | bytes 98312 | tf_op jit(solution)/shard_map/ppermute | solution.py:776

commit v16 on v14

--- a/solution.py
+++ b/solution.py
@@ -12,7 +12,7 @@
 QUANTITIES = 14
 CURRENTS = 4
 KEPT = 8
-PIECES = 4
+PIECES = 2
 VMEM_LIMIT = 40 * 1024 * 1024
 
 

time: 27.1 us -> 27.1 us (level)
  starting transfers between devices: 11.2 us -> 11.6 us
    ppermute x4, starting transfers between devices: 8.11 us -> 8.44 us  [exchange(): return lax.ppermute(value, 'flow', [(i, i ^ stride) for i in range(peers)])]
where the time goes in v16:
time: 27.1 us; the launch traced here: 27 us
  starting transfers between devices  11.6 us (43%)
  Pallas kernels  9.39 us (35%)
  waiting for transfers between devices  5.97 us (22%)
    ppermute x4, starting transfers between devices, exchange(): return lax.ppermute(value, 'flow', [(i, i ^ stride) for i in range(peers)])  8.44 us
    ppermute x4, waiting for transfers between devices, exchange(): return lax.ppermute(value, 'flow', [(i, i ^ stride) for i in range(peers)])  5.97 us
    pallas_call x2, Pallas kernels, local(): call(functools.partial(local_kernel, kept), [(PIECES,) + block_shape, (6,...  4.78 us
    ppermute x2, starting transfers between devices, swap(): return lax.ppermute(value, 'trans', pairs)  3.12 us
    pallas_call x1, Pallas kernels, per_device(): pl.pallas_call(pack_kernel, out_shape=[jax.ShapeDtypeStruct(halo, jnp.flo...  1.43 us
    pallas_call x1, Pallas kernels, per_device(): pl.pallas_call(functools.partial(final_kernel, True), out_shape=whole, in...  1.29 us
    pallas_call x1, Pallas kernels, per_device(): pl.pallas_call(functools.partial(add_kernel, False), out_shape=whole, in_...  0.94 us
    pallas_call x1, Pallas kernels, per_device(): call(functools.partial(prepare_kernel, False), [half_cells] * 9)  0.55 us
  transfers between devices with their start and end apart: 6, of which 4 were waited for; matrix products, arithmetic and copies ran while one was open for 0% of the time, Pallas kernels for 25%

profile of v16, /device:TPU:0, one launch (start us, length us, event | category | flops | bytes accessed | tf_op | source)
XLA Modules:
  0.0 27.0 jit_solution(90867608813820511)
XLA Ops:
  0.0 1.4 %shard_map.73 = (f32[3,16,256]{2,1,0:T(8,128)S(1)}, f32[3,16,256]{2,1,0:T(8,128)S(1)}, f32[16,128]{1,0:T(8,128)S(1)}, f32[4,16,16,256]{3,2,1,0:T(8,128)S(1)}, s32[16,16,256]{2,1,0:T(8,128)S(1)}) custom-call(f32[4,16,16,256]{3,2,1,0:T(8,128)} %conc_hbm.1, s32[16,16,256]{2,1,0:T(8,128)} %stratum_hbm.1, f32[1,16]{1,0:T(1,128)} %bitcast.6, f32[2,16]{1,0:T(2,128)} %bitcast.5, ...), custom_call_target="tpu_custom_call" | custom-call | tf_op jit(solution)/shard_map/pallas_call | solution.py:730
  1.4 2.4 %collective-permute-start = (f32[3,16,256]{2,1,0:T(8,128)S(1)}, f32[3,16,256]{2,1,0:T(8,128)S(1)}, u32[]{:S(2)}, u32[]{:S(2)}) collective-permute-start(f32[3,16,256]{2,1,0:T(8,128)S(1)} %get-tuple-element.56.late_ref), channel_id=1, source_target_pairs={{1,2},{2,1},{0,3},{3,0},{5,6},{6,5},{4,7},{7,4},{9,10},{10,9},{8,1... | collective-permute-start | bytes 147464 | tf_op jit(solution)/shard_map/ppermute | solution.py:770
  3.9 0.7 %collective-permute-start.1 = (f32[3,16,256]{2,1,0:T(8,128)S(1)}, f32[3,16,256]{2,1,0:T(8,128)S(1)}, u32[]{:S(2)}, u32[]{:S(2)}) collective-permute-start(f32[3,16,256]{2,1,0:T(8,128)S(1)} %get-tuple-element.55.early_ref), channel_id=1, source_target_pairs={{0,1},{2,3},{1,0},{3,2},{4,5},{6,7},{5,4},{7,6},{8,9},{10,11},{9,8... | collective-permute-start | bytes 147464 | tf_op jit(solution)/shard_map/ppermute | solution.py:770
  4.6 2.0 %shard_map.74 = (f32[2,14,8,256]{3,2,1,0:T(8,128)S(1)}, f32[6,16,256]{2,1,0:T(8,128)S(1)}, f32[16,8,256]{2,1,0:T(8,128)S(1)}, f32[16,8,256]{2,1,0:T(8,128)S(1)},...) custom-call(f32[16,128]{1,0:T(8,128)S(1)} %get-tuple-element.54.tab_, ...), custom_call_target="tpu_custom_call" | custom-call | tf_op jit(solution)/shard_map/pallas_call | solution.py:782
  6.6 0.0 collective-permute-done.beyond_late_ref
  6.6 0.0 collective-permute-done.1.beyond_early_ref
  6.6 0.1 shard_map.75
  6.8 1.9 %collective-permute-start.2 = (f32[14,8,256]{2,1,0:T(8,128)S(1)}, f32[14,8,256]{2,1,0:T(8,128)S(1)}, u32[]{:S(2)}, u32[]{:S(2)}) collective-permute-start(f32[14,8,256]{2,1,0:T(8,128)S(1)} %get-tuple-element.76), channel_id=1, source_target_pairs={{0,4},{4,0},{8,12},{12,8},{16,20},{20,16},{24,28},{28,24},{1,5},{5... | collective-permute-start | bytes 344072 | tf_op jit(solution)/shard_map/ppermute | solution.py:776
  8.7 2.7 %shard_map.77 = (f32[2,14,8,256]{3,2,1,0:T(8,128)S(1)}, f32[6,16,256]{2,1,0:T(8,128)S(1)}, f32[16,8,256]{2,1,0:T(8,128)S(1)}, f32[16,8,256]{2,1,0:T(8,128)S(1)},...) custom-call(f32[16,128]{1,0:T(8,128)S(1)} %get-tuple-element.54.tab_, ...), custom_call_target="tpu_custom_call" | custom-call | tf_op jit(solution)/shard_map/pallas_call | solution.py:782
  11.4 0.1 shard_map.78
  11.5 0.6 %collective-permute-done.2.other_ref = f32[14,8,256]{2,1,0:T(8,128)S(1)} collective-permute-done((f32[14,8,256]{2,1,0:T(8,128)S(1)}, f32[14,8,256]{2,1,0:T(8,128)S(1)}, u32[]{:S(2)}, u32[]{:S(2)}) %collective-permute-start.2) | collective-permute-done | bytes 114720 | tf_op jit(solution)/shard_map/ppermute | solution.py:776
  12.1 1.9 %collective-permute-start.3 = (f32[14,8,256]{2,1,0:T(8,128)S(1)}, f32[14,8,256]{2,1,0:T(8,128)S(1)}, u32[]{:S(2)}, u32[]{:S(2)}) collective-permute-start(f32[14,8,256]{2,1,0:T(8,128)S(1)} %get-tuple-element.77.own_ref), channel_id=1, source_target_pairs={{0,8},{4,12},{8,0},{12,4},{16,24},{20,28},{24,16},{28,20},{1,9},{5... | collective-permute-start | bytes 344072 | tf_op jit(solution)/shard_map/ppermute | solution.py:776
  14.0 3.0 %collective-permute-done.3.other_ref = f32[14,8,256]{2,1,0:T(8,128)S(1)} collective-permute-done((f32[14,8,256]{2,1,0:T(8,128)S(1)}, f32[14,8,256]{2,1,0:T(8,128)S(1)}, u32[]{:S(2)}, u32[]{:S(2)}) %collective-permute-start.3) | collective-permute-done | bytes 114720 | tf_op jit(solution)/shard_map/ppermute | solution.py:776
  17.0 2.9 %collective-permute-start.4 = (f32[5,8,256]{2,1,0:T(8,128)S(1)}, f32[5,8,256]{2,1,0:T(8,128)S(1)}, u32[]{:S(2)}, u32[]{:S(2)}) collective-permute-start(f32[5,8,256]{2,1,0:T(8,128)S(1)} %get-tuple-element.79), channel_id=1, source_target_pairs={{0,16},{4,20},{8,24},{12,28},{16,0},{20,4},{24,8},{28,12},{1,17},{... | collective-permute-start | bytes 122888 | tf_op jit(solution)/shard_map/ppermute | solution.py:776
  19.9 0.6 %shard_map.76 = (f32[16,8,256]{2,1,0:T(8,128)S(1)}, f32[16,8,256]{2,1,0:T(8,128)S(1)}, f32[16,8,256]{2,1,0:T(8,128)S(1)}, f32[16,8,256]{2,1,0:T(8,128)S(1)}, f32...) custom-call(f32[16,128]{1,0:T(8,128)S(1)} %get-tuple-element.54.tab_, ...), custom_call_target="tpu_custom_call" | custom-call | tf_op jit(solution)/shard_map/pallas_call | solution.py:811
  20.5 1.5 %collective-permute-done.4.other_ref = f32[5,8,256]{2,1,0:T(8,128)S(1)} collective-permute-done((f32[5,8,256]{2,1,0:T(8,128)S(1)}, f32[5,8,256]{2,1,0:T(8,128)S(1)}, u32[]{:S(2)}, u32[]{:S(2)}) %collective-permute-start.4) | collective-permute-done | bytes 40992 | tf_op jit(solution)/shard_map/ppermute | solution.py:776
  22.1 1.8 %collective-permute-start.5 = (f32[4,8,256]{2,1,0:T(8,128)S(1)}, f32[4,8,256]{2,1,0:T(8,128)S(1)}, u32[]{:S(2)}, u32[]{:S(2)}) collective-permute-start(f32[4,8,256]{2,1,0:T(8,128)S(1)} %get-tuple-element.82), channel_id=1, source_target_pairs={{0,4},{4,0},{8,12},{12,8},{16,20},{20,16},{24,28},{28,24},{1,5},{5... | collective-permute-start | bytes 98312 | tf_op jit(solution)/shard_map/ppermute | solution.py:776
  23.9 1.3 %shard_map.82.before_hbm = f32[4,16,16,256]{3,2,1,0:T(8,128)} custom-call(f32[16,128]{1,0:T(8,128)S(1)} %get-tuple-element.54.tab_ref, s32[16,16,256]{2,1,0:T(8,128)S(1)} %get-tuple-element.57.stratum_ref, f32[4,16,16,256]{3,2,1,0:T(8,128)S(1)} %get-tuple-element.58.conc_ref, f32[16,8,256]{2,1,0:T(8,128)S(1)} %get-tuple-element.93.pass_a_ref, ...), custom_call_target="tpu_custom_call" | custom-call | tf_op jit(solution)/shard_map/pallas_call | solution.py:826
  25.2 0.9 %collective-permute-done.5.current_ref = f32[4,8,256]{2,1,0:T(8,128)S(1)} collective-permute-done((f32[4,8,256]{2,1,0:T(8,128)S(1)}, f32[4,8,256]{2,1,0:T(8,128)S(1)}, u32[]{:S(2)}, u32[]{:S(2)}) %collective-permute-start.5) | collective-permute-done | bytes 32800 | tf_op jit(solution)/shard_map/ppermute | solution.py:776
  26.0 0.9 %shard_map.83 = f32[4,16,16,256]{3,2,1,0:T(8,128)} custom-call(f32[1,8,8,256]{3,2,1,0:T(8,128)S(1)} %get-tuple-element.61.kept_ref, f32[4,8,256]{2,1,0:T(8,128)S(1)} %collective-permute-done.5.current_ref, f32[16,8,256]{2,1,0:T(8,128)S(1)} %get-tuple-element.72.ready_ref.free_a_ref, ...), custom_call_target="tpu_custom_call", output_to_operand_aliasing={{}: (15, {})} | custom-call | tf_op jit(solution)/shard_map/pallas_call | solution.py:834
  (3 shorter events, 0.1 us)
Async XLA Ops:
  1.4 5.2 %collective-permute-start = (f32[3,16,256]{2,1,0:T(8,128)S(1)}, f32[3,16,256]{2,1,0:T(8,128)S(1)}, u32[]{:S(2)}, u32[]{:S(2)}) collective-permute-start(f32[3,16,256]{2,1,0:T(8,128)S(1)} %get-tuple-element.56.late_ref), channel_id=1, source_target_pairs={{1,2},{2,1},{0,3},{3,0},{5,6},{6,5},{4,7},{7,4},{9,10},{10,9},{8,1... | collective-permute-start | bytes 147464 | tf_op jit(solution)/shard_map/ppermute | solution.py:770
  3.9 2.7 %collective-permute-start.1 = (f32[3,16,256]{2,1,0:T(8,128)S(1)}, f32[3,16,256]{2,1,0:T(8,128)S(1)}, u32[]{:S(2)}, u32[]{:S(2)}) collective-permute-start(f32[3,16,256]{2,1,0:T(8,128)S(1)} %get-tuple-element.55.early_ref), channel_id=1, source_target_pairs={{0,1},{2,3},{1,0},{3,2},{4,5},{6,7},{5,4},{7,6},{8,9},{10,11},{9,8... | collective-permute-start | bytes 147464 | tf_op jit(solution)/shard_map/ppermute | solution.py:770
  6.8 5.3 %collective-permute-start.2 = (f32[14,8,256]{2,1,0:T(8,128)S(1)}, f32[14,8,256]{2,1,0:T(8,128)S(1)}, u32[]{:S(2)}, u32[]{:S(2)}) collective-permute-start(f32[14,8,256]{2,1,0:T(8,128)S(1)} %get-tuple-element.76), channel_id=1, source_target_pairs={{0,4},{4,0},{8,12},{12,8},{16,20},{20,16},{24,28},{28,24},{1,5},{5... | collective-permute-start | bytes 344072 | tf_op jit(solution)/shard_map/ppermute | solution.py:776
  12.1 4.9 %collective-permute-start.3 = (f32[14,8,256]{2,1,0:T(8,128)S(1)}, f32[14,8,256]{2,1,0:T(8,128)S(1)}, u32[]{:S(2)}, u32[]{:S(2)}) collective-permute-start(f32[14,8,256]{2,1,0:T(8,128)S(1)} %get-tuple-element.77.own_ref), channel_id=1, source_target_pairs={{0,8},{4,12},{8,0},{12,4},{16,24},{20,28},{24,16},{28,20},{1,9},{5... | collective-permute-start | bytes 344072 | tf_op jit(solution)/shard_map/ppermute | solution.py:776
  17.0 5.0 %collective-permute-start.4 = (f32[5,8,256]{2,1,0:T(8,128)S(1)}, f32[5,8,256]{2,1,0:T(8,128)S(1)}, u32[]{:S(2)}, u32[]{:S(2)}) collective-permute-start(f32[5,8,256]{2,1,0:T(8,128)S(1)} %get-tuple-element.79), channel_id=1, source_target_pairs={{0,16},{4,20},{8,24},{12,28},{16,0},{20,4},{24,8},{28,12},{1,17},{... | collective-permute-start | bytes 122888 | tf_op jit(solution)/shard_map/ppermute | solution.py:776
  22.1 4.0 %collective-permute-start.5 = (f32[4,8,256]{2,1,0:T(8,128)S(1)}, f32[4,8,256]{2,1,0:T(8,128)S(1)}, u32[]{:S(2)}, u32[]{:S(2)}) collective-permute-start(f32[4,8,256]{2,1,0:T(8,128)S(1)} %get-tuple-element.82), channel_id=1, source_target_pairs={{0,4},{4,0},{8,12},{12,8},{16,20},{20,16},{24,28},{28,24},{1,5},{5... | collective-permute-start | bytes 98312 | tf_op jit(solution)/shard_map/ppermute | solution.py:776
